TPU v7x, 32 devices: a whole 2x2x4 slice. The times are simulated.
32 devices in a mesh: dp: 8 (over y, x, core), tensor: 4 (over z).
Axes of the slice: x: 2, y: 2, z: 4, core: 2. Of those that a mesh axis runs over, the one named last changes fastest.
Arguments:
- hidden: bfloat16 [16, 256, 4096], P('dp', None, 'tensor'), may hold values from -6 to 6
- targets: int32 [16, 256], P('dp'), may hold values from 0 to 511
- lengths: int32 [16], P('dp'), may hold values from 1 to 256, 2048 in all
- conv_filter: bfloat16 [3, 4096], P(None, 'tensor'), may hold values from -3 to 3
- proj_weight: bfloat16 [4096, 4096], P('tensor'), may hold values from -0.09375 to 0.09375
- unembed: bfloat16 [512, 4096], P(None, 'tensor'), may hold values from -0.140625 to 0.140625
- proj_in: bfloat16 [4096, 64], P('tensor'), may hold values from -0.09375 to 0.09375
- proj_out: bfloat16 [4096, 64], P('tensor'), may hold values from -0.09375 to 0.09375
- query_grads: bfloat16 [128, 4096], P('dp', 'tensor'), may hold values from -6 to 6
Outputs:
- scores: float32 [16, 128], P('dp')
Inputs may be any that keep to these rules, and one draw needn't show every extreme that they name: `lengths`: some row has exactly 256 live tokens.
All inputs are finite; a program needn't handle non-finite values. No bound on the sum of `lengths` on one device may be relied on, other than what follows from the above.
Results may differ from a plain program's by a relative error of at most 0.0075.
Values may be sent and summed in bfloat16 or wider, within the bound.
No kernel may reach another device: no remote copies, remote signals or barrier semaphores. Data moves between devices by JAX's collectives and lax.ppermute only.
A program may use at most 64 MiB of HBM per device.

v0:
```python
import jax
import jax.numpy as jnp
from jax import lax
from jax.sharding import PartitionSpec as P

eps = 1e-06


def short_conv(hidden, conv_filter):
    values = hidden.astype(jnp.float32)
    taps = conv_filter.astype(jnp.float32)
    zero = jnp.zeros_like(values[..., :1, :])
    first = jnp.concatenate([zero, values[..., :-1, :]], axis=-2)
    second = jnp.concatenate([zero, zero, values[..., :-2, :]], axis=-2)
    return (taps[0] * values + taps[1] * first + taps[2] * second).astype(jnp.bfloat16)


def per_device(
    hidden, targets, lengths, conv_filter, proj_weight, unembed, proj_in, proj_out, query_grads
):
    rows, length, local_width = hidden.shape
    tokens = rows * length
    rank = proj_in.shape[1]
    vocab = unembed.shape[0]
    mixed = short_conv(hidden, conv_filter).reshape(tokens, local_width)
    layer_out = lax.psum_scatter(
        lax.dot_general(
            proj_weight, mixed, (((0,), (1,)), ((), ())), preferred_element_type=jnp.float32
        ),
        "tensor",
        scatter_dimension=0,
        tiled=True,
    )
    layer_low = layer_out.astype(jnp.bfloat16)
    partial_logits = jnp.dot(unembed, layer_low, preferred_element_type=jnp.float32)
    logits = lax.psum(partial_logits, "tensor")
    expo = jnp.exp(logits)
    prob = expo / jnp.sum(expo, axis=0, keepdims=True)
    live = (jnp.arange(length)[None, :] < lengths[:, None]).astype(jnp.float32).reshape(tokens)
    onehot = (jnp.arange(vocab)[:, None] == targets.reshape(tokens)[None, :]).astype(jnp.float32)
    grad_logits = ((prob - onehot) * live[None, :]).astype(jnp.bfloat16)
    grad_out = lax.dot_general(
        unembed, grad_logits, (((0,), (0,)), ((), ())), preferred_element_type=jnp.float32
    ).astype(jnp.bfloat16)
    part_in = lax.dot_general(
        proj_in, mixed, (((0,), (1,)), ((), ())), preferred_element_type=jnp.float32
    )
    part_out = lax.dot_general(
        proj_out, grad_out, (((0,), (0,)), ((), ())), preferred_element_type=jnp.float32
    )
    share = rank // lax.axis_size("tensor")
    whole_in, whole_out = lax.psum((part_in, part_out), "tensor")
    share_in = lax.dynamic_slice_in_dim(whole_in, lax.axis_index("tensor") * share, share, 0)
    row_grad = jnp.einsum(
        "irt,jrt->rij",
        share_in.reshape(share, rows, length),
        whole_out.reshape(rank, rows, length),
        precision=lax.Precision.HIGHEST,
    )
    row_grad = row_grad.reshape(rows, share * rank)
    row_norm = jnp.sum(row_grad * row_grad, axis=1)
    row_low = row_grad.astype(jnp.bfloat16)
    partial_scores = lax.dot_general(
        row_low,
        lax.all_gather(query_grads, "dp", axis=0, tiled=True),
        (((1,), (1,)), ((), ())),
        preferred_element_type=jnp.float32,
    )
    inner, norms = lax.psum((partial_scores, row_norm), "tensor")
    return inner / jnp.sqrt(norms + eps)[:, None]


def solution(mesh):
    in_specs = (
        P("dp", None, "tensor"),
        P("dp", None),
        P("dp"),
        P(None, "tensor"),
        P("tensor", None),
        P(None, "tensor"),
        P("tensor", None),
        P("tensor", None),
        P("dp", "tensor"),
    )
    out_specs = P("dp", None)
    return jax.shard_map(
        per_device, mesh=mesh, in_specs=in_specs, out_specs=out_specs, check_vma=False
    )
```

profile of v0, /device:TPU:0, one launch (start us, length us, event | category | flops | bytes accessed | tf_op | source)
XLA Modules:
  0.0 281.3 jit_solution(17839849035660007910)
XLA Ops:
  6.5 0.0 copy-start
  6.5 0.0 copy-start.1
  6.5 0.0 reduce-scatter.2.cloned.1.call-start
  6.5 1.6 slice.24
  8.2 0.0 copy-done.1
  8.2 0.0 copy-start.4
  8.2 0.0 copy-start.7
  8.2 0.2 slice.22
  8.4 0.4 copy-done.4
  8.9 0.8 add_convert_fusion
  9.7 1.9 copy-done.7
  11.6 6.8 %convolution_bitcast_fusion = f32[4096,512]{0,1:T(8,128)} fusion(bf16[512,1024]{1,0:T(8,128)(2,1)S(1)} %bitcast.36, bf16[1024,4096]{1,0:T(8,128)(2,1)S(1)} %copy-done.7), kind=kOutput, calls=%fused_computation | convolution fusion | flops 4294967296 | bytes 17825792 | tf_op jit(solution)/shard_map/dot_general | solution.py:27
  18.3 0.0 reduce-scatter.2.cloned.1.call-update
  18.3 0.0 copy-start.5
  18.4 0.0 copy-start.6
  18.4 0.0 copy-start.2
  18.4 0.0 all-reduce.7.cloned.1.call-start
  18.4 147.2 %reduce-scatter.2.cloned.1.call-done = f32[1024,512]{0,1:T(8,128)} async-done(((f32[4096,512]{0,1:T(8,128)}), f32[1024,512]{0,1:T(8,128)}) %reduce-scatter.2.cloned.1.call-update) | async-done | bytes 2097168 | tf_op jit(solution)/shard_map/reduce_scatter | solution.py:26
  165.7 0.0 copy-done
  165.7 3.3 %convolution_bitcast_fusion.1 = f32[512,512]{0,1:T(8,128)} fusion(bf16[512,1024]{1,0:T(8,128)(2,1)S(1)} %copy-done, f32[1024,512]{0,1:T(8,128)} %reduce-scatter.2.cloned.1.call-done), kind=kOutput, calls=%fused_computation.4 | convolution fusion | flops 537395200 | bytes 4194304 | tf_op jit(solution)/shard_map/dot_general | solution.py:35
  169.0 0.0 copy-start.8
  169.0 0.0 all-reduce.7.cloned.1.call-update
  169.0 0.0 all-reduce.9.cloned.1.call-start
  169.0 0.0 copy-done.5
  169.1 0.0 copy-done.6
  169.1 0.1 fusion.11
  169.2 0.0 copy-done.2
  169.2 1.1 convolution_bitcast_fusion.2
  170.3 51.5 %all-reduce.7.cloned.1.call-done = f32[512,512]{0,1:T(8,128)} async-done(((f32[512,512]{0,1:T(8,128)}), f32[512,512]{0,1:T(8,128)}) %all-reduce.7.cloned.1.call-update) | async-done | bytes 1048592 | tf_op jit(solution)/shard_map/psum | solution.py:36
  221.7 1.4 exponential_reduce_fusion
  223.2 0.0 copy-done.8
  223.2 0.0 copy-start.3
  223.2 2.4 fusion
  225.5 0.7 copy.24
  226.2 0.0 all-reduce.9.cloned.1.call-update
  226.2 0.0 copy-done.3
  226.2 9.3 %all_gather.3 = bf16[128,1024]{1,0:T(8,128)(2,1)S(1)} all-gather(bf16[16,1024]{1,0:T(8,128)(2,1)S(1)} %copy-done.3), channel_id=1, replica_groups=mesh['dp'=8,'tensor'=4] {'dp'}, dimensions={0}, use_global_device_ids=true | all-gather | bytes 294912 | tf_op jit(solution)/shard_map/all_gather | solution.py:65
  235.5 25.8 %all-reduce.9.cloned.1.call-done = (f32[64,2,256]{2,0,1:T(8,128)}, f32[64,512]{1,0:T(8,128)}) async-done(((f32[64,2,256]{2,0,1:T(8,128)}, f32[64,512]{1,0:T(8,128)}), (f32[64,2,256]{2,0,1:T(8,128)}, f32[64,512]{1,0:T(8,128)})) %all-reduce.9.cloned.1.call-update) | async-done | bytes 262160 | tf_op jit(solution)/shard_map/psum | solution.py:52
  261.3 0.8 constant_dynamic-slice_fusion
  262.0 1.2 multiply_reduce_fusion
  263.3 0.1 convert_element_type.48
  263.4 0.2 fusion.13
  263.5 10.5 %all-reduce.2 = (f32[2,128]{1,0:T(2,128)S(1)}, f32[2]{0:T(128)S(1)}) all-reduce(f32[2,128]{1,0:T(2,128)S(1)} %fusion.13, f32[2]{0:T(128)S(1)} %get-tuple-element.9), channel_id=1, replica_groups=mesh['dp'=8,'tensor'=4] {'tensor'}, use_global_device_ids=true, to_apply=%region_5.0 | all-reduce | flops 258 | bytes 2064 | tf_op jit(solution)/shard_map/psum | solution.py:69
  274.1 0.6 broadcast_divide_fusion
  (4 shorter events, 0.0 us)
Async XLA Ops:
  6.5 159.1 %copy-start = (bf16[512,1024]{1,0:T(8,128)(2,1)S(1)}, bf16[512,1024]{1,0:T(8,128)(2,1)}, u32[]{:S(2)}) copy-start(bf16[512,1024]{1,0:T(8,128)(2,1)} %param.14) | copy-start | bytes 3145732
  6.5 1.6 copy-start.1
  6.5 159.1 %reduce-scatter.2.cloned.1.call-start = ((), (), s32[]{:S(2)}) async-start(), calls=%async_computation.1 | async-start | bytes 10485760 | tf_op jit(solution)/shard_map/reduce_scatter | solution.py:26
  8.2 0.7 copy-start.4
  8.2 3.4 %copy-start.7 = (bf16[1024,4096]{1,0:T(8,128)(2,1)S(1)}, bf16[1024,4096]{1,0:T(8,128)(2,1)}, u32[]{:S(2)}) copy-start(bf16[1024,4096]{1,0:T(8,128)(2,1)} %param.13) | copy-start | bytes 25165828
  18.3 150.7 %copy-start.5 = (s32[2,256]{1,0:T(2,128)S(1)}, s32[2,256]{1,0:T(2,128)}, u32[]{:S(2)}) copy-start(s32[2,256]{1,0:T(2,128)} %param.10) | copy-start | bytes 6148
  18.4 150.7 %copy-start.6 = (s32[2]{0:T(128)S(1)}, s32[2]{0:T(128)}, u32[]{:S(2)}) copy-start(s32[2]{0:T(128)} %param.11) | copy-start | bytes 28
  18.4 150.8 %copy-start.2 = (bf16[1024,64]{0,1:T(8,128)(2,1)S(1)}, bf16[1024,64]{0,1:T(8,128)(2,1)}, u32[]{:S(2)}) copy-start(bf16[1024,64]{0,1:T(8,128)(2,1)} %param.15) | copy-start | bytes 393220
  18.4 203.3 %all-reduce.7.cloned.1.call-start = ((), (), s32[]{:S(2)}) async-start(), calls=%async_computation.2 | async-start | bytes 2097152 | tf_op jit(solution)/shard_map/psum | solution.py:36
  169.0 54.2 %copy-start.8 = (bf16[1024,64]{0,1:T(8,128)(2,1)S(1)}, bf16[1024,64]{0,1:T(8,128)(2,1)}, u32[]{:S(2)}) copy-start(bf16[1024,64]{0,1:T(8,128)(2,1)} %param.16) | copy-start | bytes 393220
  169.0 92.3 %all-reduce.9.cloned.1.call-start = ((), (), s32[]{:S(2)}) async-start(), calls=%async_computation.3 | async-start | bytes 524288 | tf_op jit(solution)/shard_map/psum | solution.py:52
  223.2 3.1 %copy-start.3 = (bf16[16,1024]{1,0:T(8,128)(2,1)S(1)}, bf16[16,1024]{1,0:T(8,128)(2,1)}, u32[]{:S(2)}) copy-start(bf16[16,1024]{1,0:T(8,128)(2,1)} %param.17) | copy-start | bytes 98308
Sparse Core Ops, SparseCore 0:
  18.5 147.1 reduce-scatter.1
  169.1 52.5 all-reduce.6
  226.3 34.8 all-reduce.8
where the time goes:
time: 282 us; the launch traced here: 281 us
  waiting for transfers between devices  225 us (80%)
  blocking collectives  19.8 us (7%)
  matrix products  14.9 us (5%)
  between operations  13.2 us (5%)
  local copies, waits for them, and re-layouts  5.74 us (2%)
  other arithmetic  2.97 us (1%)
    reduce_scatter x1, waiting for transfers between devices, per_device(): lax.psum_scatter(lax.dot_general(proj_weight, mixed, (((0,), (1,)), ((),...  147 us
    psum x1, waiting for transfers between devices, per_device(): logits = lax.psum(partial_logits, 'tensor')  51.5 us
    psum x1, waiting for transfers between devices, per_device(): whole_in, whole_out = lax.psum((part_in, part_out), 'tensor')  25.8 us
    psum x1, blocking collectives, per_device(): inner, norms = lax.psum((partial_scores, row_norm), 'tensor')  10.5 us
    all_gather x1, blocking collectives, per_device(): lax.all_gather(query_grads, 'dp', axis=0, tiled=True)  9.28 us
    dot_general x1, matrix products, per_device(): lax.dot_general(proj_weight, mixed, (((0,), (1,)), ((), ())), preferred_e...  6.75 us
  transfers between devices with their start and end apart: 3, of which 3 were waited for; matrix products, arithmetic and copies ran while one was open for 0% of the time, Pallas kernels for 0%

commit v1 on v0

v1 whole, which is shorter than its diff:
```python
import jax
import jax.numpy as jnp
from jax import lax
from jax.experimental import pallas as pl
from jax.experimental.pallas import tpu as pltpu
from jax.sharding import PartitionSpec as P

eps = 1e-06
f32, bf16 = jnp.float32, jnp.bfloat16
NT = (((1,), (1,)), ((), ()))
TN = (((0,), (0,)), ((), ()))
VM = pl.BlockSpec(memory_space=pltpu.VMEM)
ANY = pl.BlockSpec(memory_space=pl.ANY)
NEAR = [(0, 1), (1, 0), (2, 3), (3, 2)]
FAR = [(0, 2), (3, 1), (1, 0), (2, 3)]


def split2(value, axis):
    high = value.astype(bf16)
    low = (value - high.astype(f32)).astype(bf16)
    return jnp.concatenate([high, low], axis=axis)


def arr(shape, dtype):
    return jax.ShapeDtypeStruct(shape, dtype)


def call(body, outs, args, flops=0, in_specs=None, scratch=()):
    moved = sum(a.size * a.dtype.itemsize for a in args)
    return pl.pallas_call(
        body,
        out_shape=outs,
        in_specs=in_specs or [VM] * len(args),
        out_specs=jax.tree.map(lambda _: VM, outs),
        scratch_shapes=list(scratch),
        cost_estimate=pl.CostEstimate(flops=flops, bytes_accessed=moved, transcendentals=0),
        compiler_params=pltpu.CompilerParams(vmem_limit_bytes=32 << 20),
    )(*args)


def near(x):
    return pltpu.with_memory_space_constraint(x, pltpu.VMEM)


def far(x):
    return pltpu.with_memory_space_constraint(x, pltpu.HBM)


def own_rows(parts, unembed):
    vocab, width = unembed.shape
    step = vocab // parts

    def body(e_ref, out_ref, sem):
        own = pl.multiple_of((lax.axis_index("dp") % parts) * step, step)
        copy = pltpu.make_async_copy(e_ref.at[pl.ds(own, step), :], out_ref, sem)
        copy.start()
        copy.wait()

    return call(
        body,
        arr((step, width), bf16),
        (far(unembed),),
        in_specs=[ANY],
        scratch=[pltpu.SemaphoreType.DMA],
    )


def fold_term(rows, w_ref, share):
    width = rows.shape[1]
    cols = pl.ds(pl.multiple_of(share * width, width), width)
    return lax.dot_general(rows, w_ref[:, cols], NT, preferred_element_type=f32)


def local_work(hidden, conv_filter, proj_in_t, proj_out_t, query_grads, start, proj_weight):
    rows, length, width = hidden.shape
    rank = proj_in_t.shape[0]
    step = start.shape[0]
    tokens = rows * length
    wide = 2 * rank
    q_rows = query_grads.shape[0]
    lines = width // wide
    u_begin = lines * q_rows
    side_begin = u_begin + step

    def body(
        h_any, p_any, o_any, w_any, c_ref, q_ref, b_ref,
        mixed_ref, out_ref, fold_ref, w_ref, h_ref, p_ref, o_ref, hold, sems,
    ):
        pairs = ((h_any, h_ref), (p_any, p_ref), (o_any, o_ref), (w_any, w_ref))
        copies = [pltpu.make_async_copy(a, b, sems.at[k]) for k, (a, b) in enumerate(pairs)]
        for copy in copies:
            copy.start()
        taps = c_ref[...].astype(f32)
        place = lax.broadcasted_iota(jnp.int32, (length, width), 0)
        copies[0].wait()
        for row in range(rows):
            here = h_ref[row].astype(f32)
            first = jnp.where(place >= 1, pltpu.roll(here, 1, 0), 0.0)
            second = jnp.where(place >= 2, pltpu.roll(here, 2, 0), 0.0)
            mixed_ref[pl.ds(row * length, length), :] = (
                taps[0:1] * here + taps[1:2] * first + taps[2:3] * second
            ).astype(bf16)
        copies[1].wait()
        side = lax.dot_general(p_ref[...], mixed_ref[...], NT, preferred_element_type=f32)
        for k in range(tokens // wide):
            hold[k] = side[:, k * wide : (k + 1) * wide]
        for k in range(tokens // wide):
            pair = [hold[k, pl.ds(odd, rank // 2, stride=2), :] for odd in (0, 1)]
            begin = side_begin + k * wide
            out_ref[begin : begin + wide, :] = split2(jnp.concatenate(pair, axis=0), 0)
        for k in range(lines):
            out_ref[k * q_rows : (k + 1) * q_rows, :] = q_ref[:, k * wide : (k + 1) * wide]
        copies[2].wait()
        u = lax.dot_general(b_ref[...], o_ref[...], NT, preferred_element_type=f32)
        out_ref[u_begin:side_begin, :] = split2(u, 1)
        copies[3].wait()
        fold_ref[...] = fold_term(b_ref[...], w_ref, lax.axis_index("tensor"))

    return call(
        body,
        (
            arr((tokens, width), bf16),
            arr((side_begin + tokens, wide), bf16),
            arr((step, width), f32),
            pltpu.VMEM(proj_weight.shape, bf16),
        ),
        (far(hidden), far(proj_in_t), far(proj_out_t), far(proj_weight), conv_filter, query_grads, start),
        2 * tokens * width * rank + 2 * step * width * width,
        in_specs=[ANY] * 4 + [VM] * 3,
        scratch=[
            pltpu.VMEM(hidden.shape, bf16),
            pltpu.VMEM(proj_in_t.shape, bf16),
            pltpu.VMEM(proj_out_t.shape, bf16),
            pltpu.VMEM((tokens // wide, rank, wide), f32),
            pltpu.SemaphoreType.DMA((4,)),
        ],
    )


def fold_more(so_far, block, weight, slot, dtype):
    step, width = block.shape

    def body(f_ref, b_ref, w_ref, out_ref):
        share = lax.axis_index("tensor") ^ slot
        out_ref[...] = (f_ref[...] + fold_term(b_ref[...], w_ref, share)).astype(dtype)

    return call(
        body, arr((step, width), dtype), (so_far, block, near(weight)), 2 * step * width * width
    )


def halve(value):
    half = value.shape[0] // 2
    return value[:half] + value[half:]


def relay_shares(own, near_by, block, step, half):
    wide = own.shape[1]
    begin = block + step
    parts = half // wide

    def body(o_ref, n_ref, out_ref, keep_ref):
        row = lax.axis_index("tensor") // 2
        out_ref[:block, :] = o_ref[:block, :]
        out_ref[block : 2 * block, :] = n_ref[:block, :]
        u = o_ref[block:begin, :].astype(f32) + n_ref[block:begin, :].astype(f32)
        out_ref[2 * block : 2 * block + step, :] = split2(u[:, : wide // 2] + u[:, wide // 2 :], 1)
        for k in range(parts):
            at = [pl.ds(pl.multiple_of(begin + (r * parts + k) * wide, wide // 2), wide) for r in (row, 1 - row)]
            mine, other = [halve(o_ref[c, :].astype(f32) + n_ref[c, :].astype(f32)) for c in at]
            keep_ref[:, k * wide : (k + 1) * wide] = mine
            place = 2 * block + step + k * wide
            out_ref[place : place + wide, :] = split2(other, 0)

    return call(
        body,
        (arr((2 * block + step + half, wide), bf16), arr((wide // 2, half), f32)),
        (own, near_by),
    )


def first_logits(ours, theirs, mixed):
    step, width = ours.shape
    half = mixed.shape[0] // 2

    def body(a_ref, b_ref, m_ref, out_ref):
        weight = jnp.concatenate([a_ref[...], b_ref[...]], axis=0)
        row = 1 - lax.axis_index("tensor") // 2
        tokens = m_ref[pl.ds(pl.multiple_of(row * half, half), half), :]
        logits = lax.dot_general(weight, tokens, NT, preferred_element_type=f32)
        out_ref[...] = logits.astype(bf16)

    return call(
        body, arr((2 * step, half), bf16), (ours, theirs, mixed), 4 * step * half * width
    )


def gather_shares(own, cross, keep, block, step):
    wide = own.shape[1]
    parts = keep.shape[1] // wide
    begin = 2 * block

    def body(o_ref, c_ref, k_ref, out_ref, side_ref):
        me = lax.axis_index("tensor")
        for ref, share in ((o_ref, me), (c_ref, 3 - me)):
            for k, place in enumerate((share, share ^ 1)):
                place = pl.multiple_of(place * block, block)
                out_ref[pl.ds(place, block), :] = ref[k * block : (k + 1) * block, :]
        u = o_ref[begin : begin + step, :].astype(f32) + c_ref[begin : begin + step, :].astype(f32)
        out_ref[4 * block :, :] = split2(u[:, : wide // 2] + u[:, wide // 2 :], 1)
        for k in range(parts):
            cols = slice(k * wide, (k + 1) * wide)
            at = begin + step + k * wide
            side_ref[:, cols] = k_ref[:, cols] + halve(c_ref[at : at + wide, :].astype(f32))

    return call(
        body,
        (arr((4 * block + step, wide), bf16), arr(keep.shape, f32)),
        (own, cross, keep),
        0,
    )


def pass_on(x):
    def body(x_ref, out_ref):
        out_ref[...] = x_ref[...]

    return call(body, arr(x.shape, x.dtype), (x,), 1 << 30)


def stack(pieces):
    high = pieces[0].shape[0]

    def body(*refs):
        for k, ref in enumerate(refs[:-1]):
            refs[-1][k * high : (k + 1) * high, :] = ref[...]

    return call(body, arr((high * len(pieces), pieces[0].shape[1]), bf16), tuple(pieces))


def logit_rows(folded, mixed, *after):
    slots = list(folded)
    step, width = folded[0].shape
    vocab = step * len(folded)
    half = mixed.shape[0] // 2

    def body(*refs):
        parts, refs = refs[: len(folded)], refs[len(folded) :]
        m_ref, (keep_ref, near_ref, other_ref, rest_ref) = refs[0], refs[-4:]
        row = lax.axis_index("tensor") // 2
        weight = jnp.concatenate([parts[slots.index(k)][...] for k in range(len(slots))], axis=0)
        tokens = m_ref[pl.ds(pl.multiple_of((1 - row) * half, half), half), :]
        other = lax.dot_general(weight, tokens, NT, preferred_element_type=f32).astype(bf16)
        other_ref[...] = other
        rest_ref[...] = other[2 * step :]
        tokens = m_ref[pl.ds(pl.multiple_of(row * half, half), half), :]
        mine = lax.dot_general(weight, tokens, NT, preferred_element_type=f32)
        keep_ref[...] = mine
        near_ref[...] = mine.astype(bf16)

    whole = (vocab, half)
    return call(
        body,
        (arr(whole, f32), arr(whole, bf16), arr(whole, bf16), arr((vocab - 2 * step, half), bf16)),
        (*folded.values(), mixed, *after),
        4 * vocab * half * width,
    )


def token_grads(parts, pieces, first, side_in, targets, lengths):
    vocab, length = pieces[0].shape
    rank = side_in.shape[0]
    step = vocab // parts

    def body(k_ref, n_ref, c_ref, f_ref, l_ref, side_ref, t_ref, live_ref, out_ref):
        row = lax.axis_index("tensor") // 2
        own = lax.axis_index("dp") % parts
        total = k_ref[...] + n_ref[...].astype(f32) + c_ref[...].astype(f32)
        total += jnp.concatenate([l_ref[...], f_ref[...]], axis=0).astype(f32)
        expo = jnp.exp(total)
        targets_here = jnp.where(row == 0, t_ref[0:1, :], t_ref[1:2, :])
        lengths_here = jnp.where(row == 0, live_ref[0:1, :], live_ref[1:2, :])
        live = lax.broadcasted_iota(jnp.int32, (1, length), 1) < lengths_here
        scale = jnp.where(live, 1.0 / jnp.sum(expo, axis=0, keepdims=True), 0.0)
        ids = lax.broadcasted_iota(jnp.int32, (vocab, length), 0) ^ (own * step)
        targets_here = jnp.where(live, targets_here, -1)
        grad = (expo * scale - jnp.where(ids == targets_here, 1.0, 0.0)).astype(bf16)
        joint = lax.dot_general(split2(side_ref[...], 0), grad, NT, preferred_element_type=f32)
        out_ref[...] = split2(halve(joint), 0)

    spread = jnp.broadcast_to(lengths[:, None], targets.shape)
    return call(
        body,
        arr((2 * rank, vocab), bf16),
        (*pieces, first, side_in, targets, spread),
        1 << 34,
    )


def row_scores(parts, joint, ours, theirs, queries):
    wide, vocab = joint.shape
    rank = wide // 2
    step = vocab // parts
    lines = rank // 2
    count = parts if queries is None else queries.shape[0]
    high = ours.shape[0] // (parts // 2)
    rows = (high - step) // lines
    extra_args = () if queries is None else (queries,)

    def body(j_ref, a_ref, b_ref, *refs):
        q_ref, refs = (None, refs) if queries is None else (refs[0], refs[1:])
        out_ref, hold = refs
        own = lax.axis_index("dp") % parts
        s_refs = [ref.at[pl.ds(k * high, high), :] for k in range(parts // 2) for ref in (a_ref, b_ref)]
        u = jnp.concatenate([ref[rows * lines :, :] for ref in s_refs], axis=0)
        grads = halve(jnp.dot(j_ref[...], u, preferred_element_type=f32))
        grads = grads[:, :rank] + grads[:, rank:]
        grads = jnp.concatenate([grads[:lines], grads[lines:]], axis=1)
        norm = jnp.sum(grads * grads, keepdims=True)
        low = grads.astype(bf16).astype(f32)
        for k in range(count):
            block = s_refs[k][: rows * lines, :] if q_ref is None else q_ref[k]
            terms = block.astype(f32).reshape(lines, rows, wide) * low[:, None, :]
            place = k if q_ref is not None else k ^ own
            at = pl.ds(pl.multiple_of(place * rows, rows), rows)
            hold[at, :] = split2(jnp.sum(terms, axis=0), 1)
        ones = jnp.ones((16, 2 * wide), bf16)
        inner = lax.dot_general(ones, hold[...], NT, preferred_element_type=f32)
        out_ref[...] = inner[:8] / jnp.sqrt(norm + eps)

    return call(
        body,
        arr((8, count * rows), f32),
        (joint, ours, theirs, *extra_args),
        2 * vocab * rank * rank,
        scratch=[pltpu.VMEM((count * rows, 2 * wide), bf16)],
    )


def join_rows(own, crossed):
    def body(o_ref, c_ref, out_ref):
        first = lax.axis_index("tensor") < 2
        out_ref[0:1] = jnp.where(first, o_ref[0:1], c_ref[0:1])
        out_ref[1:2] = jnp.where(first, c_ref[0:1], o_ref[0:1])

    return call(body, arr(own.shape, f32), (own, crossed))


def pick_rows(joined, came):
    def body(j_ref, c_ref, out_ref):
        me = lax.axis_index("tensor")
        out_ref[...] = jnp.where((me == 1) | (me == 2), j_ref[0:2], c_ref[0:2])

    return call(body, arr((2, joined.shape[1]), f32), (joined, came))


def per_device(
    hidden, targets, lengths, conv_filter, proj_weight, unembed, proj_in, proj_out, query_grads
):
    rows = hidden.shape[0]
    n_dp, n_t = lax.axis_size("dp"), lax.axis_size("tensor")
    assert n_t == 4 and rows == 2
    parts = min(n_dp, 8)

    def send(x, pairs):
        return lax.ppermute(x, "tensor", pairs)

    def cross(x):
        pairs = [(d * 4 + a, e * 4 + b) for d in range(n_dp) for a, e, b in (
            (0, d ^ 1, 0), (1, d, 2), (2, d, 1), (3, d ^ 1, 3))]
        return lax.ppermute(x, ("dp", "tensor"), pairs)

    def swap(x, axis, slot):
        return lax.ppermute(x, axis, [(i, i ^ slot) for i in range(lax.axis_size(axis))])

    start = own_rows(parts, unembed)
    came = {s: swap(start, "tensor", s) for s in (2, 3, 1)}
    mixed, shares, folding, weight = local_work(
        hidden, conv_filter, proj_in.T, proj_out.T, query_grads, start, proj_weight
    )
    shares_near = send(shares, NEAR)
    for s in (2, 1, 3):
        folding = fold_more(folding, came[s], weight, s, bf16 if s == 3 else f32)
    block, step, half = query_grads.size // 128, start.shape[0], hidden.shape[1]
    across, keep_side = relay_shares(shares, shares_near, block, step, half)
    folded = {s: swap(folding, "dp", s) for s in reversed(range(2, parts, 2))}
    folded[0] = folding
    folded |= {s + 1: swap(x, "dp", 1) for s, x in folded.items()}
    first = pass_on(send(first_logits(folded[0], folded[1], mixed), FAR))
    whole, side_in = gather_shares(across, cross(across), keep_side, block, step)
    keep, near_logits, other_logits, rest = logit_rows(folded, mixed, side_in, first)
    pieces = (keep, send(near_logits, NEAR), cross(other_logits), send(rest, FAR))
    queries = None
    if n_dp != parts:
        queries = lax.all_gather(whole[: 4 * block], "dp", axis=0)
    ours = stack([whole] + [swap(whole, "dp", s) for s in range(2, parts, 2)])
    joint = token_grads(parts, pieces, first, side_in, targets, lengths)
    scores = row_scores(parts, joint, ours, swap(ours, "dp", 1), queries)
    joined = join_rows(scores, cross(scores))
    return pick_rows(joined, send(joined, NEAR))


def solution(mesh):
    in_specs = (
        P("dp", None, "tensor"),
        P("dp", None),
        P("dp"),
        P(None, "tensor"),
        P("tensor", None),
        P(None, "tensor"),
        P("tensor", None),
        P("tensor", None),
        P("dp", "tensor"),
    )
    return jax.shard_map(
        per_device, mesh=mesh, in_specs=in_specs, out_specs=P("dp", None), check_vma=False
    )
```

time: 282 us -> 52.6 us (0.19)
  waiting for transfers between devices: 225 us -> 12 us
  starting transfers between devices: 0.09 us -> 27.7 us
  blocking collectives: 19.8 us -> 0 us
  matrix products: 14.9 us -> 0 us
  between operations: 13.2 us -> 0.18 us
  Pallas kernels: 0 us -> 11 us
  local copies, waits for them, and re-layouts: 5.74 us -> 1.53 us
  other arithmetic: 2.97 us -> 0 us
    reduce_scatter x1 -> x0, waiting for transfers between devices: 147 us -> none  [per_device(): lax.psum_scatter(lax.dot_general(proj_weight, mixed, (((0,), (1,)), ((),...]
    psum x2 -> x0, waiting for transfers between devices: 77.2 us -> none  [the longest x1 51.5 us: per_device(): logits = lax.psum(partial_logits, 'tensor')]
    ppermute x0 -> x22, starting transfers between devices: none -> 27.7 us  [the longest x5 14.2 us: send(): return lax.ppermute(x, 'tensor', pairs)]
    dot_general x6 -> x0, matrix products: 14.9 us -> none  [the longest x1 6.75 us: per_device(): lax.dot_general(proj_weight, mixed, (((0,), (1,)), ((), ())), preferred_e...]
    ppermute x0 -> x22, waiting for transfers between devices: none -> 12 us  [the longest x14 9.36 us: swap(): lax.ppermute(x, axis, [(i, i ^ slot) for i in range(lax.axis_size(axis))])]
    pallas_call x0 -> x15, Pallas kernels: none -> 11 us  [call(): pl.pallas_call(body, out_shape=outs, in_specs=in_specs or [VM] * len(args...]
    psum x1 -> x0, blocking collectives: 10.5 us -> none  [per_device(): inner, norms = lax.psum((partial_scores, row_norm), 'tensor')]
    all_gather x1 -> x0, blocking collectives: 9.28 us -> none  [per_device(): lax.all_gather(query_grads, 'dp', axis=0, tiled=True)]
  transfers between devices with their start and end apart: 3 -> 22, of which waited for: 3 -> 7; matrix products, arithmetic and copies ran while one was open for 0% -> 0% of each run, Pallas kernels for 0% -> 17%
where the time goes in v1:
time: 52.6 us; the launch traced here: 52.4 us
  starting transfers between devices  27.7 us (53%)
  waiting for transfers between devices  12 us (23%)
  Pallas kernels  11 us (21%)
  local copies, waits for them, and re-layouts  1.53 us (3%)
    ppermute x5, starting transfers between devices, send(): return lax.ppermute(x, 'tensor', pairs)  14.2 us
    ppermute x14, starting transfers between devices, swap(): lax.ppermute(x, axis, [(i, i ^ slot) for i in range(lax.axis_size(axis))])  13.3 us
    pallas_call x15, Pallas kernels, call(): pl.pallas_call(body, out_shape=outs, in_specs=in_specs or [VM] * len(args...  11 us
    ppermute x14, waiting for transfers between devices, swap(): lax.ppermute(x, axis, [(i, i ^ slot) for i in range(lax.axis_size(axis))])  9.36 us
    ppermute x5, waiting for transfers between devices, send(): return lax.ppermute(x, 'tensor', pairs)  1.59 us
    unnamed x8, local copies, waits for them, and re-layouts  1.46 us
  transfers between devices with their start and end apart: 22, of which 7 were waited for; matrix products, arithmetic and copies ran while one was open for 0% of the time, Pallas kernels for 17%

profile of v1, /device:TPU:0, one launch (start us, length us, event | category | flops | bytes accessed | tf_op | source)
XLA Modules:
  0.0 52.4 jit_solution(7280005945379132825)
XLA Ops:
  0.0 0.9 %shard_map.91.b_ref = bf16[64,1024]{1,0:T(8,128)(2,1)S(1)} custom-call(bf16[512,1024]{1,0:T(8,128)(2,1)} %e_ref.1), custom_call_target="tpu_custom_call" | custom-call | bytes 1048576 | tf_op jit(solution)/shard_map/pallas_call | solution.py:30
  0.9 4.1 %collective-permute-start = (bf16[64,1024]{1,0:T(8,128)(2,1)S(1)}, bf16[64,1024]{1,0:T(8,128)(2,1)S(1)}, u32[]{:S(2)}, u32[]{:S(2)}) collective-permute-start(bf16[64,1024]{1,0:T(8,128)(2,1)S(1)} %shard_map.91.b_ref), channel_id=1, source_target_pairs={{0,2},{1,3},{2,0},{3,1},{4,6},{5,7},{6,4},{7,5},{8,10},{9,11},{10,... | collective-permute-start | bytes 393224 | tf_op jit(solution)/shard_map/ppermute | solution.py:374
  5.0 1.6 %collective-permute-start.1 = (bf16[64,1024]{1,0:T(8,128)(2,1)S(1)}, bf16[64,1024]{1,0:T(8,128)(2,1)S(1)}, u32[]{:S(2)}, u32[]{:S(2)}) collective-permute-start(bf16[64,1024]{1,0:T(8,128)(2,1)S(1)} %shard_map.91.b_ref), channel_id=1, source_target_pairs={{0,1},{1,0},{2,3},{3,2},{4,5},{5,4},{6,7},{7,6},{8,9},{9,8},{10,11... | collective-permute-start | bytes 393224 | tf_op jit(solution)/shard_map/ppermute | solution.py:374
  6.6 0.8 %copy-done = bf16[16,1024]{1,0:T(8,128)(2,1)S(1)} copy-done((bf16[16,1024]{1,0:T(8,128)(2,1)S(1)}, bf16[16,1024]{1,0:T(8,128)(2,1)}, u32[]{:S(2)}) %copy-start) | copy-done | bytes 32792
  7.4 0.7 %copy-done.1 = bf16[3,1024]{1,0:T(4,128)(2,1)S(1)} copy-done((bf16[3,1024]{1,0:T(4,128)(2,1)S(1)}, bf16[3,1024]{1,0:T(4,128)(2,1)}, u32[]{:S(2)}) %copy-start.1) | copy-done | bytes 6168
  8.1 4.6 %shard_map.92 = (bf16[512,1024]{1,0:T(8,128)(2,1)S(1)}, bf16[704,128]{1,0:T(8,128)(2,1)S(1)}, f32[64,1024]{1,0:T(8,128)S(1)}, bf16[1024,4096]{1,0:T(8,128)(2,1)S(1)}) custom-call(bf16[2,256,1024]{2,1,0:T(8,128)(2,1)} %h_any.1, bf16[64,1024]{1,0:T(8,128)(2,1)} %bitcast.2, bf16[64,1024]{1,0:T(8,128)(2,1)} %bitcast.3, bf16[1024,4096]{1,0:T(8,128)(2,1)} %w_any.1, ...), custom_call_target="tpu_custom_call" | custom-call | flops 201326592 | bytes 9869312 | tf_op jit(solution)/shard_map/pallas_call | solution.py:30
  12.7 1.0 %collective-permute-start.10 = (bf16[704,128]{1,0:T(8,128)(2,1)S(1)}, bf16[704,128]{1,0:T(8,128)(2,1)S(1)}, u32[]{:S(2)}, u32[]{:S(2)}) collective-permute-start(bf16[704,128]{1,0:T(8,128)(2,1)S(1)} %get-tuple-element.20.o_ref), channel_id=1, source_target_pairs={{0,1},{1,0},{2,3},{3,2},{4,5},{5,4},{6,7},{7,6},{8,9},{9,8},{10,11... | collective-permute-start | bytes 540680 | tf_op jit(solution)/shard_map/ppermute | solution.py:366
  13.6 0.8 %shard_map.93.f_ref = f32[64,1024]{1,0:T(8,128)S(1)} custom-call(f32[64,1024]{1,0:T(8,128)S(1)} %get-tuple-element.17.f_ref, bf16[64,1024]{1,0:T(8,128)(2,1)S(1)} %collective-permute-done.b_ref, bf16[1024,4096]{1,0:T(8,128)(2,1)S(1)} %get-tuple-element.18.w_ref), custom_call_target="tpu_custom_call" | custom-call | flops 134217728 | bytes 8781824 | tf_op jit(solution)/shard_map/pallas_call | solution.py:30
  14.4 0.8 %shard_map.94.f_ref = f32[64,1024]{1,0:T(8,128)S(1)} custom-call(f32[64,1024]{1,0:T(8,128)S(1)} %shard_map.93.f_ref, bf16[64,1024]{1,0:T(8,128)(2,1)S(1)} %collective-permute-done.1.b_ref, bf16[1024,4096]{1,0:T(8,128)(2,1)S(1)} %get-tuple-element.18.w_ref), custom_call_target="tpu_custom_call" | custom-call | flops 134217728 | bytes 8781824 | tf_op jit(solution)/shard_map/pallas_call | solution.py:30
  15.2 0.0 copy-start.2
  15.2 0.2 collective-permute-done.2.b_ref
  15.4 0.8 %shard_map.95.a_ref.refs_3_ = bf16[64,1024]{1,0:T(8,128)(2,1)S(1)} custom-call(f32[64,1024]{1,0:T(8,128)S(1)} %shard_map.94.f_ref, bf16[64,1024]{1,0:T(8,128)(2,1)S(1)} %collective-permute-done.2.b_ref, bf16[1024,4096]{1,0:T(8,128)(2,1)S(1)} %get-tuple-element.18.w_ref), custom_call_target="tpu_custom_call" | custom-call | flops 134217728 | bytes 8781824 | tf_op jit(solution)/shard_map/pallas_call | solution.py:30
  16.2 0.1 collective-permute-start.9
  16.3 2.5 %collective-permute-start.3 = (bf16[64,1024]{1,0:T(8,128)(2,1)S(1)}, bf16[64,1024]{1,0:T(8,128)(2,1)S(1)}, u32[]{:S(2)}, u32[]{:S(2)}) collective-permute-start(bf16[64,1024]{1,0:T(8,128)(2,1)S(1)} %shard_map.95.a_ref.refs_3_), channel_id=1, source_target_pairs={{0,24},{4,28},{8,16},{12,20},{16,8},{20,12},{24,0},{28,4},{1,25},{... | collective-permute-start | bytes 393224 | tf_op jit(solution)/shard_map/ppermute | solution.py:374
  18.8 0.5 collective-permute-start.4
  19.3 0.5 %collective-permute-start.5 = (bf16[64,1024]{1,0:T(8,128)(2,1)S(1)}, bf16[64,1024]{1,0:T(8,128)(2,1)S(1)}, u32[]{:S(2)}, u32[]{:S(2)}) collective-permute-start(bf16[64,1024]{1,0:T(8,128)(2,1)S(1)} %shard_map.95.a_ref.refs_3_), channel_id=1, source_target_pairs={{0,8},{4,12},{8,0},{12,4},{16,24},{20,28},{24,16},{28,20},{1,9},{5... | collective-permute-start | bytes 393224 | tf_op jit(solution)/shard_map/ppermute | solution.py:374
  19.8 0.0 collective-permute-done.10.n_ref
  19.8 0.2 shard_map.96
  20.0 0.0 collective-permute-start.11
  20.0 0.0 collective-permute-done.9.b_ref.refs_7_
  20.0 0.3 shard_map.98
  20.3 4.2 %collective-permute-start.12 = (bf16[128,256]{1,0:T(8,128)(2,1)S(1)}, bf16[128,256]{1,0:T(8,128)(2,1)S(1)}, u32[]{:S(2)}, u32[]{:S(2)}) collective-permute-start(bf16[128,256]{1,0:T(8,128)(2,1)S(1)} %shard_map.98), channel_id=1, source_target_pairs={{0,2},{3,1},{1,0},{2,3},{4,6},{7,5},{5,4},{6,7},{8,10},{11,9},{9,8... | collective-permute-start | bytes 196616 | tf_op jit(solution)/shard_map/ppermute | solution.py:366
  24.5 0.0 collective-permute-done.3.refs_0_
  24.5 0.0 collective-permute-start.6
  24.5 1.3 %collective-permute-done.4.refs_1_ = bf16[64,1024]{1,0:T(8,128)(2,1)S(1)} collective-permute-done((bf16[64,1024]{1,0:T(8,128)(2,1)S(1)}, bf16[64,1024]{1,0:T(8,128)(2,1)S(1)}, u32[]{:S(2)}, u32[]{:S(2)}) %collective-permute-start.4) | collective-permute-done | bytes 131104 | tf_op jit(solution)/shard_map/ppermute | solution.py:374
  25.9 0.0 collective-permute-start.7
  25.9 0.1 collective-permute-done.5.refs_2_
  26.0 0.4 collective-permute-start.8
  26.4 0.0 collective-permute-done.11.c_ref
  26.4 0.2 shard_map.97
  26.6 1.5 %collective-permute-start.16 = (bf16[576,128]{1,0:T(8,128)(2,1)S(1)}, bf16[576,128]{1,0:T(8,128)(2,1)S(1)}, u32[]{:S(2)}, u32[]{:S(2)}) collective-permute-start(bf16[576,128]{1,0:T(8,128)(2,1)S(1)} %get-tuple-element.28.refs_0_), channel_id=1, source_target_pairs={{0,8},{4,12},{8,0},{12,4},{16,24},{20,28},{24,16},{28,20},{1,9},{5... | collective-permute-start | bytes 442376 | tf_op jit(solution)/shard_map/ppermute | solution.py:374
  28.1 0.0 collective-permute-done.12.x_ref
  28.1 0.8 %shard_map.100 = (f32[512,256]{1,0:T(8,128)S(1)}, bf16[512,256]{1,0:T(8,128)(2,1)S(1)}, bf16[512,256]{1,0:T(8,128)(2,1)S(1)}, bf16[384,256]{1,0:T(8,128)(2,1)S(1)}) custom-call(bf16[64,1024]{1,0:T(8,128)(2,1)S(1)} %collective-permute-done.3.refs_0_, bf16[64,1024]{1,0:T(8,128)(2,1)S(1)} %collective-permute-done.4.refs_1_, ...), custom_call_target="tpu_custom_call" | custom-call | flops 536870912 | bytes 2228224 | tf_op jit(solution)/shard_map/pallas_call | solution.py:30
  28.9 2.7 %collective-permute-start.13 = (bf16[512,256]{1,0:T(8,128)(2,1)S(1)}, bf16[512,256]{1,0:T(8,128)(2,1)S(1)}, u32[]{:S(2)}, u32[]{:S(2)}) collective-permute-start(bf16[512,256]{1,0:T(8,128)(2,1)S(1)} %get-tuple-element.25), channel_id=1, source_target_pairs={{0,1},{1,0},{2,3},{3,2},{4,5},{5,4},{6,7},{7,6},{8,9},{9,8},{10,11... | collective-permute-start | bytes 786440 | tf_op jit(solution)/shard_map/ppermute | solution.py:366
  31.6 2.0 %collective-permute-start.15 = (bf16[384,256]{1,0:T(8,128)(2,1)S(1)}, bf16[384,256]{1,0:T(8,128)(2,1)S(1)}, u32[]{:S(2)}, u32[]{:S(2)}) collective-permute-start(bf16[384,256]{1,0:T(8,128)(2,1)S(1)} %get-tuple-element.27), channel_id=1, source_target_pairs={{0,2},{3,1},{1,0},{2,3},{4,6},{7,5},{5,4},{6,7},{8,10},{11,9},{9,8... | collective-permute-start | bytes 589832 | tf_op jit(solution)/shard_map/ppermute | solution.py:366
  33.6 1.5 %collective-permute-start.17 = (bf16[576,128]{1,0:T(8,128)(2,1)S(1)}, bf16[576,128]{1,0:T(8,128)(2,1)S(1)}, u32[]{:S(2)}, u32[]{:S(2)}) collective-permute-start(bf16[576,128]{1,0:T(8,128)(2,1)S(1)} %get-tuple-element.28.refs_0_), channel_id=1, source_target_pairs={{0,16},{4,20},{8,24},{12,28},{16,0},{20,4},{24,8},{28,12},{1,17},{... | collective-permute-start | bytes 442376 | tf_op jit(solution)/shard_map/ppermute | solution.py:374
  35.1 0.5 collective-permute-start.18
  35.6 6.3 %collective-permute-done.17.refs_2_ = bf16[576,128]{1,0:T(8,128)(2,1)S(1)} collective-permute-done((bf16[576,128]{1,0:T(8,128)(2,1)S(1)}, bf16[576,128]{1,0:T(8,128)(2,1)S(1)}, u32[]{:S(2)}, u32[]{:S(2)}) %collective-permute-start.17) | collective-permute-done | bytes 147488 | tf_op jit(solution)/shard_map/ppermute | solution.py:374
  41.9 0.1 collective-permute-start.19
  42.1 0.1 broadcast_in_dim.2.live_ref
  42.1 0.4 shard_map.101.j_ref
  42.6 1.4 %collective-permute-done.19.b_ref = bf16[2304,128]{1,0:T(8,128)(2,1)S(1)} collective-permute-done((bf16[2304,128]{1,0:T(8,128)(2,1)S(1)}, bf16[2304,128]{1,0:T(8,128)(2,1)S(1)}, u32[]{:S(2)}, u32[]{:S(2)}) %collective-permute-start.19) | collective-permute-done | bytes 589856 | tf_op jit(solution)/shard_map/ppermute | solution.py:374
  44.0 0.7 %shard_map.103.o_ref = f32[8,128]{1,0:T(8,128)S(1)} custom-call(bf16[128,512]{1,0:T(8,128)(2,1)S(1)} %shard_map.101.j_ref, bf16[2304,128]{1,0:T(8,128)(2,1)S(1)} %shard_map.102.a_ref, bf16[2304,128]{1,0:T(8,128)(2,1)S(1)} %collective-permute-done.19.b_ref), custom_call_target="tpu_custom_call" | custom-call | flops 4194304 | bytes 1310720 | tf_op jit(solution)/shard_map/pallas_call | solution.py:30
  44.7 0.1 collective-permute-start.20
  44.9 1.0 %collective-permute-done.20.c_ref = f32[8,128]{1,0:T(8,128)S(1)} collective-permute-done((f32[8,128]{1,0:T(8,128)S(1)}, f32[8,128]{1,0:T(8,128)S(1)}, u32[]{:S(2)}, u32[]{:S(2)}) %collective-permute-start.20) | collective-permute-done | bytes 4128 | tf_op jit(solution)/shard_map/ppermute | solution.py:371
  45.9 4.3 %collective-permute-start.21 = (f32[8,128]{1,0:T(8,128)S(1)}, f32[8,128]{1,0:T(8,128)S(1)}, u32[]{:S(2)}, u32[]{:S(2)}) collective-permute-start(f32[8,128]{1,0:T(8,128)S(1)} %shard_map.104.j_ref), channel_id=1, source_target_pairs={{0,1},{1,0},{2,3},{3,2},{4,5},{5,4},{6,7},{7,6},{8,9},{9,8},{10,11... | collective-permute-start | bytes 12296 | tf_op jit(solution)/shard_map/ppermute | solution.py:366
  50.2 1.6 %collective-permute-done.21.c_ref = f32[8,128]{1,0:T(8,128)S(1)} collective-permute-done((f32[8,128]{1,0:T(8,128)S(1)}, f32[8,128]{1,0:T(8,128)S(1)}, u32[]{:S(2)}, u32[]{:S(2)}) %collective-permute-start.21) | collective-permute-done | bytes 4128 | tf_op jit(solution)/shard_map/ppermute | solution.py:366
  51.8 0.6 %shard_map.105 = f32[2,128]{1,0:T(2,128)} custom-call(f32[8,128]{1,0:T(8,128)S(1)} %shard_map.104.j_ref, f32[8,128]{1,0:T(8,128)S(1)} %collective-permute-done.21.c_ref), custom_call_target="tpu_custom_call" | custom-call | bytes 8192 | tf_op jit(solution)/shard_map/pallas_call | solution.py:30
  (20 shorter events, 0.1 us)
Async XLA Ops:
  0.9 12.7 %collective-permute-start = (bf16[64,1024]{1,0:T(8,128)(2,1)S(1)}, bf16[64,1024]{1,0:T(8,128)(2,1)S(1)}, u32[]{:S(2)}, u32[]{:S(2)}) collective-permute-start(bf16[64,1024]{1,0:T(8,128)(2,1)S(1)} %shard_map.91.b_ref), channel_id=1, source_target_pairs={{0,2},{1,3},{2,0},{3,1},{4,6},{5,7},{6,4},{7,5},{8,10},{9,11},{10,... | collective-permute-start | bytes 393224 | tf_op jit(solution)/shard_map/ppermute | solution.py:374
  5.0 9.4 %collective-permute-start.1 = (bf16[64,1024]{1,0:T(8,128)(2,1)S(1)}, bf16[64,1024]{1,0:T(8,128)(2,1)S(1)}, u32[]{:S(2)}, u32[]{:S(2)}) collective-permute-start(bf16[64,1024]{1,0:T(8,128)(2,1)S(1)} %shard_map.91.b_ref), channel_id=1, source_target_pairs={{0,1},{1,0},{2,3},{3,2},{4,5},{5,4},{6,7},{7,6},{8,9},{9,8},{10,11... | collective-permute-start | bytes 393224 | tf_op jit(solution)/shard_map/ppermute | solution.py:374
  6.6 8.8 %collective-permute-start.2 = (bf16[64,1024]{1,0:T(8,128)(2,1)S(1)}, bf16[64,1024]{1,0:T(8,128)(2,1)S(1)}, u32[]{:S(2)}, u32[]{:S(2)}) collective-permute-start(bf16[64,1024]{1,0:T(8,128)(2,1)S(1)} %shard_map.91.b_ref), channel_id=1, source_target_pairs={{0,3},{1,2},{2,1},{3,0},{4,7},{5,6},{6,5},{7,4},{8,11},{9,10},{10,... | collective-permute-start | bytes 393224 | tf_op jit(solution)/shard_map/ppermute | solution.py:374
  6.6 0.8 %copy-start = (bf16[16,1024]{1,0:T(8,128)(2,1)S(1)}, bf16[16,1024]{1,0:T(8,128)(2,1)}, u32[]{:S(2)}) copy-start(bf16[16,1024]{1,0:T(8,128)(2,1)} %q_ref.1) | copy-start | bytes 98308
  7.4 0.7 %copy-start.1 = (bf16[3,1024]{1,0:T(4,128)(2,1)S(1)}, bf16[3,1024]{1,0:T(4,128)(2,1)}, u32[]{:S(2)}) copy-start(bf16[3,1024]{1,0:T(4,128)(2,1)} %c_ref.1) | copy-start | bytes 18436
  12.7 7.2 %collective-permute-start.10 = (bf16[704,128]{1,0:T(8,128)(2,1)S(1)}, bf16[704,128]{1,0:T(8,128)(2,1)S(1)}, u32[]{:S(2)}, u32[]{:S(2)}) collective-permute-start(bf16[704,128]{1,0:T(8,128)(2,1)S(1)} %get-tuple-element.20.o_ref), channel_id=1, source_target_pairs={{0,1},{1,0},{2,3},{3,2},{4,5},{5,4},{6,7},{7,6},{8,9},{9,8},{10,11... | collective-permute-start | bytes 540680 | tf_op jit(solution)/shard_map/ppermute | solution.py:366
  15.2 26.9 %copy-start.3 = (s32[2]{0:T(128)S(1)}, s32[2]{0:T(128)}, u32[]{:S(2)}) copy-start(s32[2]{0:T(128)} %param.11) | copy-start | bytes 28
  15.2 27.0 %copy-start.2 = (s32[2,256]{1,0:T(2,128)S(1)}, s32[2,256]{1,0:T(2,128)}, u32[]{:S(2)}) copy-start(s32[2,256]{1,0:T(2,128)} %t_ref.1) | copy-start | bytes 6148
  16.2 3.8 %collective-permute-start.9 = (bf16[64,1024]{1,0:T(8,128)(2,1)S(1)}, bf16[64,1024]{1,0:T(8,128)(2,1)S(1)}, u32[]{:S(2)}, u32[]{:S(2)}) collective-permute-start(bf16[64,1024]{1,0:T(8,128)(2,1)S(1)} %shard_map.95.a_ref.refs_3_), channel_id=1, source_target_pairs={{0,4},{4,0},{8,12},{12,8},{16,20},{20,16},{24,28},{28,24},{1,5},{5... | collective-permute-start | bytes 393224 | tf_op jit(solution)/shard_map/ppermute | solution.py:374
  16.3 8.3 %collective-permute-start.3 = (bf16[64,1024]{1,0:T(8,128)(2,1)S(1)}, bf16[64,1024]{1,0:T(8,128)(2,1)S(1)}, u32[]{:S(2)}, u32[]{:S(2)}) collective-permute-start(bf16[64,1024]{1,0:T(8,128)(2,1)S(1)} %shard_map.95.a_ref.refs_3_), channel_id=1, source_target_pairs={{0,24},{4,28},{8,16},{12,20},{16,8},{20,12},{24,0},{28,4},{1,25},{... | collective-permute-start | bytes 393224 | tf_op jit(solution)/shard_map/ppermute | solution.py:374
  18.8 7.1 %collective-permute-start.4 = (bf16[64,1024]{1,0:T(8,128)(2,1)S(1)}, bf16[64,1024]{1,0:T(8,128)(2,1)S(1)}, u32[]{:S(2)}, u32[]{:S(2)}) collective-permute-start(bf16[64,1024]{1,0:T(8,128)(2,1)S(1)} %shard_map.95.a_ref.refs_3_), channel_id=1, source_target_pairs={{0,16},{4,20},{8,24},{12,28},{16,0},{20,4},{24,8},{28,12},{1,17},{... | collective-permute-start | bytes 393224 | tf_op jit(solution)/shard_map/ppermute | solution.py:374
  19.3 6.7 %collective-permute-start.5 = (bf16[64,1024]{1,0:T(8,128)(2,1)S(1)}, bf16[64,1024]{1,0:T(8,128)(2,1)S(1)}, u32[]{:S(2)}, u32[]{:S(2)}) collective-permute-start(bf16[64,1024]{1,0:T(8,128)(2,1)S(1)} %shard_map.95.a_ref.refs_3_), channel_id=1, source_target_pairs={{0,8},{4,12},{8,0},{12,4},{16,24},{20,28},{24,16},{28,20},{1,9},{5... | collective-permute-start | bytes 393224 | tf_op jit(solution)/shard_map/ppermute | solution.py:374
  20.0 6.4 %collective-permute-start.11 = (bf16[576,128]{1,0:T(8,128)(2,1)S(1)}, bf16[576,128]{1,0:T(8,128)(2,1)S(1)}, u32[]{:S(2)}, u32[]{:S(2)}) collective-permute-start(bf16[576,128]{1,0:T(8,128)(2,1)S(1)} %get-tuple-element.21.o_ref), channel_id=1, source_target_pairs={{0,4},{1,2},{2,1},{3,7},{4,0},{5,6},{6,5},{7,3},{8,12},{9,10},{10,... | collective-permute-start | bytes 442376 | tf_op jit(solution)/shard_map/ppermute | solution.py:371
  20.3 7.7 %collective-permute-start.12 = (bf16[128,256]{1,0:T(8,128)(2,1)S(1)}, bf16[128,256]{1,0:T(8,128)(2,1)S(1)}, u32[]{:S(2)}, u32[]{:S(2)}) collective-permute-start(bf16[128,256]{1,0:T(8,128)(2,1)S(1)} %shard_map.98), channel_id=1, source_target_pairs={{0,2},{3,1},{1,0},{2,3},{4,6},{7,5},{5,4},{6,7},{8,10},{11,9},{9,8... | collective-permute-start | bytes 196616 | tf_op jit(solution)/shard_map/ppermute | solution.py:366
  24.5 3.5 %collective-permute-start.6 = (bf16[64,1024]{1,0:T(8,128)(2,1)S(1)}, bf16[64,1024]{1,0:T(8,128)(2,1)S(1)}, u32[]{:S(2)}, u32[]{:S(2)}) collective-permute-start(bf16[64,1024]{1,0:T(8,128)(2,1)S(1)} %collective-permute-done.3.refs_0_), channel_id=1, source_target_pairs={{0,4},{4,0},{8,12},{12,8},{16,20},{20,16},{24,28},{28,24},{1,5},{5... | collective-permute-start | bytes 393224 | tf_op jit(solution)/shard_map/ppermute | solution.py:374
  25.9 2.2 %collective-permute-start.7 = (bf16[64,1024]{1,0:T(8,128)(2,1)S(1)}, bf16[64,1024]{1,0:T(8,128)(2,1)S(1)}, u32[]{:S(2)}, u32[]{:S(2)}) collective-permute-start(bf16[64,1024]{1,0:T(8,128)(2,1)S(1)} %collective-permute-done.4.refs_1_), channel_id=1, source_target_pairs={{0,4},{4,0},{8,12},{12,8},{16,20},{20,16},{24,28},{28,24},{1,5},{5... | collective-permute-start | bytes 393224 | tf_op jit(solution)/shard_map/ppermute | solution.py:374
  26.0 2.1 %collective-permute-start.8 = (bf16[64,1024]{1,0:T(8,128)(2,1)S(1)}, bf16[64,1024]{1,0:T(8,128)(2,1)S(1)}, u32[]{:S(2)}, u32[]{:S(2)}) collective-permute-start(bf16[64,1024]{1,0:T(8,128)(2,1)S(1)} %collective-permute-done.5.refs_2_), channel_id=1, source_target_pairs={{0,4},{4,0},{8,12},{12,8},{16,20},{20,16},{24,28},{28,24},{1,5},{5... | collective-permute-start | bytes 393224 | tf_op jit(solution)/shard_map/ppermute | solution.py:374
  26.6 8.6 %collective-permute-start.16 = (bf16[576,128]{1,0:T(8,128)(2,1)S(1)}, bf16[576,128]{1,0:T(8,128)(2,1)S(1)}, u32[]{:S(2)}, u32[]{:S(2)}) collective-permute-start(bf16[576,128]{1,0:T(8,128)(2,1)S(1)} %get-tuple-element.28.refs_0_), channel_id=1, source_target_pairs={{0,8},{4,12},{8,0},{12,4},{16,24},{20,28},{24,16},{28,20},{1,9},{5... | collective-permute-start | bytes 442376 | tf_op jit(solution)/shard_map/ppermute | solution.py:374
  28.9 13.2 %collective-permute-start.13 = (bf16[512,256]{1,0:T(8,128)(2,1)S(1)}, bf16[512,256]{1,0:T(8,128)(2,1)S(1)}, u32[]{:S(2)}, u32[]{:S(2)}) collective-permute-start(bf16[512,256]{1,0:T(8,128)(2,1)S(1)} %get-tuple-element.25), channel_id=1, source_target_pairs={{0,1},{1,0},{2,3},{3,2},{4,5},{5,4},{6,7},{7,6},{8,9},{9,8},{10,11... | collective-permute-start | bytes 786440 | tf_op jit(solution)/shard_map/ppermute | solution.py:366
  31.6 10.5 %collective-permute-start.14 = (bf16[512,256]{1,0:T(8,128)(2,1)S(1)}, bf16[512,256]{1,0:T(8,128)(2,1)S(1)}, u32[]{:S(2)}, u32[]{:S(2)}) collective-permute-start(bf16[512,256]{1,0:T(8,128)(2,1)S(1)} %get-tuple-element.26), channel_id=1, source_target_pairs={{0,4},{1,2},{2,1},{3,7},{4,0},{5,6},{6,5},{7,3},{8,12},{9,10},{10,... | collective-permute-start | bytes 786440 | tf_op jit(solution)/shard_map/ppermute | solution.py:371
  31.6 10.5 %collective-permute-start.15 = (bf16[384,256]{1,0:T(8,128)(2,1)S(1)}, bf16[384,256]{1,0:T(8,128)(2,1)S(1)}, u32[]{:S(2)}, u32[]{:S(2)}) collective-permute-start(bf16[384,256]{1,0:T(8,128)(2,1)S(1)} %get-tuple-element.27), channel_id=1, source_target_pairs={{0,2},{3,1},{1,0},{2,3},{4,6},{7,5},{5,4},{6,7},{8,10},{11,9},{9,8... | collective-permute-start | bytes 589832 | tf_op jit(solution)/shard_map/ppermute | solution.py:366
  33.6 8.3 %collective-permute-start.17 = (bf16[576,128]{1,0:T(8,128)(2,1)S(1)}, bf16[576,128]{1,0:T(8,128)(2,1)S(1)}, u32[]{:S(2)}, u32[]{:S(2)}) collective-permute-start(bf16[576,128]{1,0:T(8,128)(2,1)S(1)} %get-tuple-element.28.refs_0_), channel_id=1, source_target_pairs={{0,16},{4,20},{8,24},{12,28},{16,0},{20,4},{24,8},{28,12},{1,17},{... | collective-permute-start | bytes 442376 | tf_op jit(solution)/shard_map/ppermute | solution.py:374
  35.1 6.8 %collective-permute-start.18 = (bf16[576,128]{1,0:T(8,128)(2,1)S(1)}, bf16[576,128]{1,0:T(8,128)(2,1)S(1)}, u32[]{:S(2)}, u32[]{:S(2)}) collective-permute-start(bf16[576,128]{1,0:T(8,128)(2,1)S(1)} %get-tuple-element.28.refs_0_), channel_id=1, source_target_pairs={{0,24},{4,28},{8,16},{12,20},{16,8},{20,12},{24,0},{28,4},{1,25},{... | collective-permute-start | bytes 442376 | tf_op jit(solution)/shard_map/ppermute | solution.py:374
  41.9 2.1 %collective-permute-start.19 = (bf16[2304,128]{1,0:T(8,128)(2,1)S(1)}, bf16[2304,128]{1,0:T(8,128)(2,1)S(1)}, u32[]{:S(2)}, u32[]{:S(2)}) collective-permute-start(bf16[2304,128]{1,0:T(8,128)(2,1)S(1)} %shard_map.102.a_ref), channel_id=1, source_target_pairs={{0,4},{4,0},{8,12},{12,8},{16,20},{20,16},{24,28},{28,24},{1,5},{5... | collective-permute-start | bytes 1769480 | tf_op jit(solution)/shard_map/ppermute | solution.py:374
  44.7 1.2 %collective-permute-start.20 = (f32[8,128]{1,0:T(8,128)S(1)}, f32[8,128]{1,0:T(8,128)S(1)}, u32[]{:S(2)}, u32[]{:S(2)}) collective-permute-start(f32[8,128]{1,0:T(8,128)S(1)} %shard_map.103.o_ref), channel_id=1, source_target_pairs={{0,4},{1,2},{2,1},{3,7},{4,0},{5,6},{6,5},{7,3},{8,12},{9,10},{10,... | collective-permute-start | bytes 12296 | tf_op jit(solution)/shard_map/ppermute | solution.py:371
  45.9 5.9 %collective-permute-start.21 = (f32[8,128]{1,0:T(8,128)S(1)}, f32[8,128]{1,0:T(8,128)S(1)}, u32[]{:S(2)}, u32[]{:S(2)}) collective-permute-start(f32[8,128]{1,0:T(8,128)S(1)} %shard_map.104.j_ref), channel_id=1, source_target_pairs={{0,1},{1,0},{2,3},{3,2},{4,5},{5,4},{6,7},{7,6},{8,9},{9,8},{10,11... | collective-permute-start | bytes 12296 | tf_op jit(solution)/shard_map/ppermute | solution.py:366

commit v2 on v1

--- a/solution.py
+++ b/solution.py
@@ -229,13 +229,14 @@
 
 
 def stack(pieces):
-    high = pieces[0].shape[0]
+    high, wide = pieces[0].shape
+    places = [slot // 2 * high for slot in pieces]
 
     def body(*refs):
-        for k, ref in enumerate(refs[:-1]):
-            refs[-1][k * high : (k + 1) * high, :] = ref[...]
-
-    return call(body, arr((high * len(pieces), pieces[0].shape[1]), bf16), tuple(pieces))
+        for begin, ref in zip(places, refs):
+            refs[-1][begin : begin + high, :] = ref[...]
+
+    return call(body, arr((high * len(pieces), wide), bf16), tuple(pieces.values()))
 
 
 def logit_rows(folded, mixed, *after):
@@ -393,7 +394,7 @@
     queries = None
     if n_dp != parts:
         queries = lax.all_gather(whole[: 4 * block], "dp", axis=0)
-    ours = stack([whole] + [swap(whole, "dp", s) for s in range(2, parts, 2)])
+    ours = stack({0: whole} | {s: swap(whole, "dp", s) for s in (2, 6, 4)})
     joint = token_grads(parts, pieces, first, side_in, targets, lengths)
     scores = row_scores(parts, joint, ours, swap(ours, "dp", 1), queries)
     joined = join_rows(scores, cross(scores))

time: 52.6 us -> 52.9 us (level)
  waiting for transfers between devices: 12 us -> 12.7 us
    ppermute x14, waiting for transfers between devices: 9.36 us -> 10.1 us  [swap(): lax.ppermute(x, axis, [(i, i ^ slot) for i in range(lax.axis_size(axis))])]
  transfers between devices with their start and end apart: 22 -> 22, of which waited for: 7 -> 8; matrix products, arithmetic and copies ran while one was open for 0% -> 0% of each run, Pallas kernels for 17% -> 17%
where the time goes in v2:
time: 52.9 us; the launch traced here: 52.7 us
  starting transfers between devices  27.3 us (52%)
  waiting for transfers between devices  12.7 us (24%)
  Pallas kernels  11 us (21%)
  local copies, waits for them, and re-layouts  1.53 us (3%)
    ppermute x5, starting transfers between devices, send(): return lax.ppermute(x, 'tensor', pairs)  13.8 us
    ppermute x14, starting transfers between devices, swap(): lax.ppermute(x, axis, [(i, i ^ slot) for i in range(lax.axis_size(axis))])  13.3 us
    pallas_call x15, Pallas kernels, call(): pl.pallas_call(body, out_shape=outs, in_specs=in_specs or [VM] * len(args...  11 us
    ppermute x14, waiting for transfers between devices, swap(): lax.ppermute(x, axis, [(i, i ^ slot) for i in range(lax.axis_size(axis))])  10.1 us
    ppermute x5, waiting for transfers between devices, send(): return lax.ppermute(x, 'tensor', pairs)  1.59 us
    unnamed x8, local copies, waits for them, and re-layouts  1.46 us
  transfers between devices with their start and end apart: 22, of which 8 were waited for; matrix products, arithmetic and copies ran while one was open for 0% of the time, Pallas kernels for 17%

profile of v2, /device:TPU:0, one launch (start us, length us, event | category | flops | bytes accessed | tf_op | source)
XLA Modules:
  0.0 52.7 jit_solution(13557319223499685757)
XLA Ops:
  0.0 0.9 %shard_map.91.b_ref = bf16[64,1024]{1,0:T(8,128)(2,1)S(1)} custom-call(bf16[512,1024]{1,0:T(8,128)(2,1)} %e_ref.1), custom_call_target="tpu_custom_call" | custom-call | bytes 1048576 | tf_op jit(solution)/shard_map/pallas_call | solution.py:30
  0.9 4.1 %collective-permute-start = (bf16[64,1024]{1,0:T(8,128)(2,1)S(1)}, bf16[64,1024]{1,0:T(8,128)(2,1)S(1)}, u32[]{:S(2)}, u32[]{:S(2)}) collective-permute-start(bf16[64,1024]{1,0:T(8,128)(2,1)S(1)} %shard_map.91.b_ref), channel_id=1, source_target_pairs={{0,2},{1,3},{2,0},{3,1},{4,6},{5,7},{6,4},{7,5},{8,10},{9,11},{10,... | collective-permute-start | bytes 393224 | tf_op jit(solution)/shard_map/ppermute | solution.py:375
  5.0 1.6 %collective-permute-start.1 = (bf16[64,1024]{1,0:T(8,128)(2,1)S(1)}, bf16[64,1024]{1,0:T(8,128)(2,1)S(1)}, u32[]{:S(2)}, u32[]{:S(2)}) collective-permute-start(bf16[64,1024]{1,0:T(8,128)(2,1)S(1)} %shard_map.91.b_ref), channel_id=1, source_target_pairs={{0,1},{1,0},{2,3},{3,2},{4,5},{5,4},{6,7},{7,6},{8,9},{9,8},{10,11... | collective-permute-start | bytes 393224 | tf_op jit(solution)/shard_map/ppermute | solution.py:375
  6.6 0.0 collective-permute-start.2
  6.6 0.8 %copy-done = bf16[16,1024]{1,0:T(8,128)(2,1)S(1)} copy-done((bf16[16,1024]{1,0:T(8,128)(2,1)S(1)}, bf16[16,1024]{1,0:T(8,128)(2,1)}, u32[]{:S(2)}) %copy-start) | copy-done | bytes 32792
  7.4 0.7 %copy-done.1 = bf16[3,1024]{1,0:T(4,128)(2,1)S(1)} copy-done((bf16[3,1024]{1,0:T(4,128)(2,1)S(1)}, bf16[3,1024]{1,0:T(4,128)(2,1)}, u32[]{:S(2)}) %copy-start.1) | copy-done | bytes 6168
  8.1 4.6 %shard_map.92 = (bf16[512,1024]{1,0:T(8,128)(2,1)S(1)}, bf16[704,128]{1,0:T(8,128)(2,1)S(1)}, f32[64,1024]{1,0:T(8,128)S(1)}, bf16[1024,4096]{1,0:T(8,128)(2,1)S(1)}) custom-call(bf16[2,256,1024]{2,1,0:T(8,128)(2,1)} %h_any.1, bf16[64,1024]{1,0:T(8,128)(2,1)} %bitcast.2, bf16[64,1024]{1,0:T(8,128)(2,1)} %bitcast.3, bf16[1024,4096]{1,0:T(8,128)(2,1)} %w_any.1, ...), custom_call_target="tpu_custom_call" | custom-call | flops 201326592 | bytes 9869312 | tf_op jit(solution)/shard_map/pallas_call | solution.py:30
  12.7 1.0 %collective-permute-start.10 = (bf16[704,128]{1,0:T(8,128)(2,1)S(1)}, bf16[704,128]{1,0:T(8,128)(2,1)S(1)}, u32[]{:S(2)}, u32[]{:S(2)}) collective-permute-start(bf16[704,128]{1,0:T(8,128)(2,1)S(1)} %get-tuple-element.20.o_ref), channel_id=1, source_target_pairs={{0,1},{1,0},{2,3},{3,2},{4,5},{5,4},{6,7},{7,6},{8,9},{9,8},{10,11... | collective-permute-start | bytes 540680 | tf_op jit(solution)/shard_map/ppermute | solution.py:367
  13.6 0.0 collective-permute-done.b_ref
  13.6 0.8 %shard_map.93.f_ref = f32[64,1024]{1,0:T(8,128)S(1)} custom-call(f32[64,1024]{1,0:T(8,128)S(1)} %get-tuple-element.17.f_ref, bf16[64,1024]{1,0:T(8,128)(2,1)S(1)} %collective-permute-done.b_ref, bf16[1024,4096]{1,0:T(8,128)(2,1)S(1)} %get-tuple-element.18.w_ref), custom_call_target="tpu_custom_call" | custom-call | flops 134217728 | bytes 8781824 | tf_op jit(solution)/shard_map/pallas_call | solution.py:30
  14.4 0.8 %shard_map.94.f_ref = f32[64,1024]{1,0:T(8,128)S(1)} custom-call(f32[64,1024]{1,0:T(8,128)S(1)} %shard_map.93.f_ref, bf16[64,1024]{1,0:T(8,128)(2,1)S(1)} %collective-permute-done.1.b_ref, bf16[1024,4096]{1,0:T(8,128)(2,1)S(1)} %get-tuple-element.18.w_ref), custom_call_target="tpu_custom_call" | custom-call | flops 134217728 | bytes 8781824 | tf_op jit(solution)/shard_map/pallas_call | solution.py:30
  15.2 0.0 copy-start.2
  15.2 0.2 collective-permute-done.2.b_ref
  15.4 0.8 %shard_map.95.a_ref.refs_3_ = bf16[64,1024]{1,0:T(8,128)(2,1)S(1)} custom-call(f32[64,1024]{1,0:T(8,128)S(1)} %shard_map.94.f_ref, bf16[64,1024]{1,0:T(8,128)(2,1)S(1)} %collective-permute-done.2.b_ref, bf16[1024,4096]{1,0:T(8,128)(2,1)S(1)} %get-tuple-element.18.w_ref), custom_call_target="tpu_custom_call" | custom-call | flops 134217728 | bytes 8781824 | tf_op jit(solution)/shard_map/pallas_call | solution.py:30
  16.2 0.1 collective-permute-start.9
  16.3 2.5 %collective-permute-start.3 = (bf16[64,1024]{1,0:T(8,128)(2,1)S(1)}, bf16[64,1024]{1,0:T(8,128)(2,1)S(1)}, u32[]{:S(2)}, u32[]{:S(2)}) collective-permute-start(bf16[64,1024]{1,0:T(8,128)(2,1)S(1)} %shard_map.95.a_ref.refs_3_), channel_id=1, source_target_pairs={{0,24},{4,28},{8,16},{12,20},{16,8},{20,12},{24,0},{28,4},{1,25},{... | collective-permute-start | bytes 393224 | tf_op jit(solution)/shard_map/ppermute | solution.py:375
  18.8 0.5 collective-permute-start.4
  19.3 0.5 %collective-permute-start.5 = (bf16[64,1024]{1,0:T(8,128)(2,1)S(1)}, bf16[64,1024]{1,0:T(8,128)(2,1)S(1)}, u32[]{:S(2)}, u32[]{:S(2)}) collective-permute-start(bf16[64,1024]{1,0:T(8,128)(2,1)S(1)} %shard_map.95.a_ref.refs_3_), channel_id=1, source_target_pairs={{0,8},{4,12},{8,0},{12,4},{16,24},{20,28},{24,16},{28,20},{1,9},{5... | collective-permute-start | bytes 393224 | tf_op jit(solution)/shard_map/ppermute | solution.py:375
  19.8 0.2 shard_map.96
  20.0 0.0 collective-permute-start.11
  20.0 0.0 collective-permute-done.9.b_ref.refs_7_
  20.0 0.3 shard_map.98
  20.3 4.2 %collective-permute-start.12 = (bf16[128,256]{1,0:T(8,128)(2,1)S(1)}, bf16[128,256]{1,0:T(8,128)(2,1)S(1)}, u32[]{:S(2)}, u32[]{:S(2)}) collective-permute-start(bf16[128,256]{1,0:T(8,128)(2,1)S(1)} %shard_map.98), channel_id=1, source_target_pairs={{0,2},{3,1},{1,0},{2,3},{4,6},{7,5},{5,4},{6,7},{8,10},{11,9},{9,8... | collective-permute-start | bytes 196616 | tf_op jit(solution)/shard_map/ppermute | solution.py:367
  24.5 1.3 %collective-permute-done.4.refs_1_ = bf16[64,1024]{1,0:T(8,128)(2,1)S(1)} collective-permute-done((bf16[64,1024]{1,0:T(8,128)(2,1)S(1)}, bf16[64,1024]{1,0:T(8,128)(2,1)S(1)}, u32[]{:S(2)}, u32[]{:S(2)}) %collective-permute-start.4) | collective-permute-done | bytes 131104 | tf_op jit(solution)/shard_map/ppermute | solution.py:375
  25.9 0.0 collective-permute-start.7
  25.9 0.1 collective-permute-done.5.refs_2_
  26.0 0.4 collective-permute-start.8
  26.4 0.0 collective-permute-done.11.c_ref
  26.4 0.2 shard_map.97
  26.6 1.5 %collective-permute-start.16 = (bf16[576,128]{1,0:T(8,128)(2,1)S(1)}, bf16[576,128]{1,0:T(8,128)(2,1)S(1)}, u32[]{:S(2)}, u32[]{:S(2)}) collective-permute-start(bf16[576,128]{1,0:T(8,128)(2,1)S(1)} %get-tuple-element.28.refs_0_), channel_id=1, source_target_pairs={{0,8},{4,12},{8,0},{12,4},{16,24},{20,28},{24,16},{28,20},{1,9},{5... | collective-permute-start | bytes 442376 | tf_op jit(solution)/shard_map/ppermute | solution.py:375
  28.1 0.0 collective-permute-done.7.refs_5_
  28.1 0.8 %shard_map.100 = (f32[512,256]{1,0:T(8,128)S(1)}, bf16[512,256]{1,0:T(8,128)(2,1)S(1)}, bf16[512,256]{1,0:T(8,128)(2,1)S(1)}, bf16[384,256]{1,0:T(8,128)(2,1)S(1)}) custom-call(bf16[64,1024]{1,0:T(8,128)(2,1)S(1)} %collective-permute-done.3.refs_0_, bf16[64,1024]{1,0:T(8,128)(2,1)S(1)} %collective-permute-done.4.refs_1_, ...), custom_call_target="tpu_custom_call" | custom-call | flops 536870912 | bytes 2228224 | tf_op jit(solution)/shard_map/pallas_call | solution.py:30
  28.9 2.7 %collective-permute-start.13 = (bf16[512,256]{1,0:T(8,128)(2,1)S(1)}, bf16[512,256]{1,0:T(8,128)(2,1)S(1)}, u32[]{:S(2)}, u32[]{:S(2)}) collective-permute-start(bf16[512,256]{1,0:T(8,128)(2,1)S(1)} %get-tuple-element.25), channel_id=1, source_target_pairs={{0,1},{1,0},{2,3},{3,2},{4,5},{5,4},{6,7},{7,6},{8,9},{9,8},{10,11... | collective-permute-start | bytes 786440 | tf_op jit(solution)/shard_map/ppermute | solution.py:367
  31.6 2.0 %collective-permute-start.15 = (bf16[384,256]{1,0:T(8,128)(2,1)S(1)}, bf16[384,256]{1,0:T(8,128)(2,1)S(1)}, u32[]{:S(2)}, u32[]{:S(2)}) collective-permute-start(bf16[384,256]{1,0:T(8,128)(2,1)S(1)} %get-tuple-element.27), channel_id=1, source_target_pairs={{0,2},{3,1},{1,0},{2,3},{4,6},{7,5},{5,4},{6,7},{8,10},{11,9},{9,8... | collective-permute-start | bytes 589832 | tf_op jit(solution)/shard_map/ppermute | solution.py:367
  33.6 1.5 %collective-permute-start.17 = (bf16[576,128]{1,0:T(8,128)(2,1)S(1)}, bf16[576,128]{1,0:T(8,128)(2,1)S(1)}, u32[]{:S(2)}, u32[]{:S(2)}) collective-permute-start(bf16[576,128]{1,0:T(8,128)(2,1)S(1)} %get-tuple-element.28.refs_0_), channel_id=1, source_target_pairs={{0,24},{4,28},{8,16},{12,20},{16,8},{20,12},{24,0},{28,4},{1,25},{... | collective-permute-start | bytes 442376 | tf_op jit(solution)/shard_map/ppermute | solution.py:375
  35.1 0.5 collective-permute-start.18
  35.6 4.1 %collective-permute-done.17.refs_2_ = bf16[576,128]{1,0:T(8,128)(2,1)S(1)} collective-permute-done((bf16[576,128]{1,0:T(8,128)(2,1)S(1)}, bf16[576,128]{1,0:T(8,128)(2,1)S(1)}, u32[]{:S(2)}, u32[]{:S(2)}) %collective-permute-start.17) | collective-permute-done | bytes 147488 | tf_op jit(solution)/shard_map/ppermute | solution.py:375
  39.7 2.9 %collective-permute-done.18.refs_3_ = bf16[576,128]{1,0:T(8,128)(2,1)S(1)} collective-permute-done((bf16[576,128]{1,0:T(8,128)(2,1)S(1)}, bf16[576,128]{1,0:T(8,128)(2,1)S(1)}, u32[]{:S(2)}, u32[]{:S(2)}) %collective-permute-start.18) | collective-permute-done | bytes 147488 | tf_op jit(solution)/shard_map/ppermute | solution.py:375
  42.6 0.1 collective-permute-start.19
  42.8 0.1 broadcast_in_dim.2.live_ref
  42.8 0.4 shard_map.101.j_ref
  43.3 1.4 %collective-permute-done.19.b_ref = bf16[2304,128]{1,0:T(8,128)(2,1)S(1)} collective-permute-done((bf16[2304,128]{1,0:T(8,128)(2,1)S(1)}, bf16[2304,128]{1,0:T(8,128)(2,1)S(1)}, u32[]{:S(2)}, u32[]{:S(2)}) %collective-permute-start.19) | collective-permute-done | bytes 589856 | tf_op jit(solution)/shard_map/ppermute | solution.py:375
  44.7 0.7 %shard_map.103.o_ref = f32[8,128]{1,0:T(8,128)S(1)} custom-call(bf16[128,512]{1,0:T(8,128)(2,1)S(1)} %shard_map.101.j_ref, bf16[2304,128]{1,0:T(8,128)(2,1)S(1)} %shard_map.102.a_ref, bf16[2304,128]{1,0:T(8,128)(2,1)S(1)} %collective-permute-done.19.b_ref), custom_call_target="tpu_custom_call" | custom-call | flops 4194304 | bytes 1310720 | tf_op jit(solution)/shard_map/pallas_call | solution.py:30
  45.4 0.2 collective-permute-start.20
  45.6 1.0 %collective-permute-done.20.c_ref = f32[8,128]{1,0:T(8,128)S(1)} collective-permute-done((f32[8,128]{1,0:T(8,128)S(1)}, f32[8,128]{1,0:T(8,128)S(1)}, u32[]{:S(2)}, u32[]{:S(2)}) %collective-permute-start.20) | collective-permute-done | bytes 4128 | tf_op jit(solution)/shard_map/ppermute | solution.py:372
  46.6 3.9 %collective-permute-start.21 = (f32[8,128]{1,0:T(8,128)S(1)}, f32[8,128]{1,0:T(8,128)S(1)}, u32[]{:S(2)}, u32[]{:S(2)}) collective-permute-start(f32[8,128]{1,0:T(8,128)S(1)} %shard_map.104.j_ref), channel_id=1, source_target_pairs={{0,1},{1,0},{2,3},{3,2},{4,5},{5,4},{6,7},{7,6},{8,9},{9,8},{10,11... | collective-permute-start | bytes 12296 | tf_op jit(solution)/shard_map/ppermute | solution.py:367
  50.5 1.6 %collective-permute-done.21.c_ref = f32[8,128]{1,0:T(8,128)S(1)} collective-permute-done((f32[8,128]{1,0:T(8,128)S(1)}, f32[8,128]{1,0:T(8,128)S(1)}, u32[]{:S(2)}, u32[]{:S(2)}) %collective-permute-start.21) | collective-permute-done | bytes 4128 | tf_op jit(solution)/shard_map/ppermute | solution.py:367
  52.1 0.6 %shard_map.105 = f32[2,128]{1,0:T(2,128)} custom-call(f32[8,128]{1,0:T(8,128)S(1)} %shard_map.104.j_ref, f32[8,128]{1,0:T(8,128)S(1)} %collective-permute-done.21.c_ref), custom_call_target="tpu_custom_call" | custom-call | bytes 8192 | tf_op jit(solution)/shard_map/pallas_call | solution.py:30
  (20 shorter events, 0.1 us)
Async XLA Ops:
  0.9 12.7 %collective-permute-start = (bf16[64,1024]{1,0:T(8,128)(2,1)S(1)}, bf16[64,1024]{1,0:T(8,128)(2,1)S(1)}, u32[]{:S(2)}, u32[]{:S(2)}) collective-permute-start(bf16[64,1024]{1,0:T(8,128)(2,1)S(1)} %shard_map.91.b_ref), channel_id=1, source_target_pairs={{0,2},{1,3},{2,0},{3,1},{4,6},{5,7},{6,4},{7,5},{8,10},{9,11},{10,... | collective-permute-start | bytes 393224 | tf_op jit(solution)/shard_map/ppermute | solution.py:375
  5.0 9.4 %collective-permute-start.1 = (bf16[64,1024]{1,0:T(8,128)(2,1)S(1)}, bf16[64,1024]{1,0:T(8,128)(2,1)S(1)}, u32[]{:S(2)}, u32[]{:S(2)}) collective-permute-start(bf16[64,1024]{1,0:T(8,128)(2,1)S(1)} %shard_map.91.b_ref), channel_id=1, source_target_pairs={{0,1},{1,0},{2,3},{3,2},{4,5},{5,4},{6,7},{7,6},{8,9},{9,8},{10,11... | collective-permute-start | bytes 393224 | tf_op jit(solution)/shard_map/ppermute | solution.py:375
  6.6 8.8 %collective-permute-start.2 = (bf16[64,1024]{1,0:T(8,128)(2,1)S(1)}, bf16[64,1024]{1,0:T(8,128)(2,1)S(1)}, u32[]{:S(2)}, u32[]{:S(2)}) collective-permute-start(bf16[64,1024]{1,0:T(8,128)(2,1)S(1)} %shard_map.91.b_ref), channel_id=1, source_target_pairs={{0,3},{1,2},{2,1},{3,0},{4,7},{5,6},{6,5},{7,4},{8,11},{9,10},{10,... | collective-permute-start | bytes 393224 | tf_op jit(solution)/shard_map/ppermute | solution.py:375
  6.6 0.8 %copy-start = (bf16[16,1024]{1,0:T(8,128)(2,1)S(1)}, bf16[16,1024]{1,0:T(8,128)(2,1)}, u32[]{:S(2)}) copy-start(bf16[16,1024]{1,0:T(8,128)(2,1)} %q_ref.1) | copy-start | bytes 98308
  7.4 0.7 %copy-start.1 = (bf16[3,1024]{1,0:T(4,128)(2,1)S(1)}, bf16[3,1024]{1,0:T(4,128)(2,1)}, u32[]{:S(2)}) copy-start(bf16[3,1024]{1,0:T(4,128)(2,1)} %c_ref.1) | copy-start | bytes 18436
  12.7 7.2 %collective-permute-start.10 = (bf16[704,128]{1,0:T(8,128)(2,1)S(1)}, bf16[704,128]{1,0:T(8,128)(2,1)S(1)}, u32[]{:S(2)}, u32[]{:S(2)}) collective-permute-start(bf16[704,128]{1,0:T(8,128)(2,1)S(1)} %get-tuple-element.20.o_ref), channel_id=1, source_target_pairs={{0,1},{1,0},{2,3},{3,2},{4,5},{5,4},{6,7},{7,6},{8,9},{9,8},{10,11... | collective-permute-start | bytes 540680 | tf_op jit(solution)/shard_map/ppermute | solution.py:367
  15.2 27.6 %copy-start.3 = (s32[2]{0:T(128)S(1)}, s32[2]{0:T(128)}, u32[]{:S(2)}) copy-start(s32[2]{0:T(128)} %param.11) | copy-start | bytes 28
  15.2 27.7 %copy-start.2 = (s32[2,256]{1,0:T(2,128)S(1)}, s32[2,256]{1,0:T(2,128)}, u32[]{:S(2)}) copy-start(s32[2,256]{1,0:T(2,128)} %t_ref.1) | copy-start | bytes 6148
  16.2 3.8 %collective-permute-start.9 = (bf16[64,1024]{1,0:T(8,128)(2,1)S(1)}, bf16[64,1024]{1,0:T(8,128)(2,1)S(1)}, u32[]{:S(2)}, u32[]{:S(2)}) collective-permute-start(bf16[64,1024]{1,0:T(8,128)(2,1)S(1)} %shard_map.95.a_ref.refs_3_), channel_id=1, source_target_pairs={{0,4},{4,0},{8,12},{12,8},{16,20},{20,16},{24,28},{28,24},{1,5},{5... | collective-permute-start | bytes 393224 | tf_op jit(solution)/shard_map/ppermute | solution.py:375
  16.3 8.3 %collective-permute-start.3 = (bf16[64,1024]{1,0:T(8,128)(2,1)S(1)}, bf16[64,1024]{1,0:T(8,128)(2,1)S(1)}, u32[]{:S(2)}, u32[]{:S(2)}) collective-permute-start(bf16[64,1024]{1,0:T(8,128)(2,1)S(1)} %shard_map.95.a_ref.refs_3_), channel_id=1, source_target_pairs={{0,24},{4,28},{8,16},{12,20},{16,8},{20,12},{24,0},{28,4},{1,25},{... | collective-permute-start | bytes 393224 | tf_op jit(solution)/shard_map/ppermute | solution.py:375
  18.8 7.1 %collective-permute-start.4 = (bf16[64,1024]{1,0:T(8,128)(2,1)S(1)}, bf16[64,1024]{1,0:T(8,128)(2,1)S(1)}, u32[]{:S(2)}, u32[]{:S(2)}) collective-permute-start(bf16[64,1024]{1,0:T(8,128)(2,1)S(1)} %shard_map.95.a_ref.refs_3_), channel_id=1, source_target_pairs={{0,16},{4,20},{8,24},{12,28},{16,0},{20,4},{24,8},{28,12},{1,17},{... | collective-permute-start | bytes 393224 | tf_op jit(solution)/shard_map/ppermute | solution.py:375
  19.3 6.7 %collective-permute-start.5 = (bf16[64,1024]{1,0:T(8,128)(2,1)S(1)}, bf16[64,1024]{1,0:T(8,128)(2,1)S(1)}, u32[]{:S(2)}, u32[]{:S(2)}) collective-permute-start(bf16[64,1024]{1,0:T(8,128)(2,1)S(1)} %shard_map.95.a_ref.refs_3_), channel_id=1, source_target_pairs={{0,8},{4,12},{8,0},{12,4},{16,24},{20,28},{24,16},{28,20},{1,9},{5... | collective-permute-start | bytes 393224 | tf_op jit(solution)/shard_map/ppermute | solution.py:375
  20.0 6.4 %collective-permute-start.11 = (bf16[576,128]{1,0:T(8,128)(2,1)S(1)}, bf16[576,128]{1,0:T(8,128)(2,1)S(1)}, u32[]{:S(2)}, u32[]{:S(2)}) collective-permute-start(bf16[576,128]{1,0:T(8,128)(2,1)S(1)} %get-tuple-element.21.o_ref), channel_id=1, source_target_pairs={{0,4},{1,2},{2,1},{3,7},{4,0},{5,6},{6,5},{7,3},{8,12},{9,10},{10,... | collective-permute-start | bytes 442376 | tf_op jit(solution)/shard_map/ppermute | solution.py:372
  20.3 7.7 %collective-permute-start.12 = (bf16[128,256]{1,0:T(8,128)(2,1)S(1)}, bf16[128,256]{1,0:T(8,128)(2,1)S(1)}, u32[]{:S(2)}, u32[]{:S(2)}) collective-permute-start(bf16[128,256]{1,0:T(8,128)(2,1)S(1)} %shard_map.98), channel_id=1, source_target_pairs={{0,2},{3,1},{1,0},{2,3},{4,6},{7,5},{5,4},{6,7},{8,10},{11,9},{9,8... | collective-permute-start | bytes 196616 | tf_op jit(solution)/shard_map/ppermute | solution.py:367
  24.5 3.5 %collective-permute-start.6 = (bf16[64,1024]{1,0:T(8,128)(2,1)S(1)}, bf16[64,1024]{1,0:T(8,128)(2,1)S(1)}, u32[]{:S(2)}, u32[]{:S(2)}) collective-permute-start(bf16[64,1024]{1,0:T(8,128)(2,1)S(1)} %collective-permute-done.3.refs_0_), channel_id=1, source_target_pairs={{0,4},{4,0},{8,12},{12,8},{16,20},{20,16},{24,28},{28,24},{1,5},{5... | collective-permute-start | bytes 393224 | tf_op jit(solution)/shard_map/ppermute | solution.py:375
  25.9 2.2 %collective-permute-start.7 = (bf16[64,1024]{1,0:T(8,128)(2,1)S(1)}, bf16[64,1024]{1,0:T(8,128)(2,1)S(1)}, u32[]{:S(2)}, u32[]{:S(2)}) collective-permute-start(bf16[64,1024]{1,0:T(8,128)(2,1)S(1)} %collective-permute-done.4.refs_1_), channel_id=1, source_target_pairs={{0,4},{4,0},{8,12},{12,8},{16,20},{20,16},{24,28},{28,24},{1,5},{5... | collective-permute-start | bytes 393224 | tf_op jit(solution)/shard_map/ppermute | solution.py:375
  26.0 2.1 %collective-permute-start.8 = (bf16[64,1024]{1,0:T(8,128)(2,1)S(1)}, bf16[64,1024]{1,0:T(8,128)(2,1)S(1)}, u32[]{:S(2)}, u32[]{:S(2)}) collective-permute-start(bf16[64,1024]{1,0:T(8,128)(2,1)S(1)} %collective-permute-done.5.refs_2_), channel_id=1, source_target_pairs={{0,4},{4,0},{8,12},{12,8},{16,20},{20,16},{24,28},{28,24},{1,5},{5... | collective-permute-start | bytes 393224 | tf_op jit(solution)/shard_map/ppermute | solution.py:375
  26.6 8.5 %collective-permute-start.16 = (bf16[576,128]{1,0:T(8,128)(2,1)S(1)}, bf16[576,128]{1,0:T(8,128)(2,1)S(1)}, u32[]{:S(2)}, u32[]{:S(2)}) collective-permute-start(bf16[576,128]{1,0:T(8,128)(2,1)S(1)} %get-tuple-element.28.refs_0_), channel_id=1, source_target_pairs={{0,8},{4,12},{8,0},{12,4},{16,24},{20,28},{24,16},{28,20},{1,9},{5... | collective-permute-start | bytes 442376 | tf_op jit(solution)/shard_map/ppermute | solution.py:375
  28.9 13.9 %collective-permute-start.13 = (bf16[512,256]{1,0:T(8,128)(2,1)S(1)}, bf16[512,256]{1,0:T(8,128)(2,1)S(1)}, u32[]{:S(2)}, u32[]{:S(2)}) collective-permute-start(bf16[512,256]{1,0:T(8,128)(2,1)S(1)} %get-tuple-element.25), channel_id=1, source_target_pairs={{0,1},{1,0},{2,3},{3,2},{4,5},{5,4},{6,7},{7,6},{8,9},{9,8},{10,11... | collective-permute-start | bytes 786440 | tf_op jit(solution)/shard_map/ppermute | solution.py:367
  31.6 11.2 %collective-permute-start.14 = (bf16[512,256]{1,0:T(8,128)(2,1)S(1)}, bf16[512,256]{1,0:T(8,128)(2,1)S(1)}, u32[]{:S(2)}, u32[]{:S(2)}) collective-permute-start(bf16[512,256]{1,0:T(8,128)(2,1)S(1)} %get-tuple-element.26), channel_id=1, source_target_pairs={{0,4},{1,2},{2,1},{3,7},{4,0},{5,6},{6,5},{7,3},{8,12},{9,10},{10,... | collective-permute-start | bytes 786440 | tf_op jit(solution)/shard_map/ppermute | solution.py:372
  31.6 11.1 %collective-permute-start.15 = (bf16[384,256]{1,0:T(8,128)(2,1)S(1)}, bf16[384,256]{1,0:T(8,128)(2,1)S(1)}, u32[]{:S(2)}, u32[]{:S(2)}) collective-permute-start(bf16[384,256]{1,0:T(8,128)(2,1)S(1)} %get-tuple-element.27), channel_id=1, source_target_pairs={{0,2},{3,1},{1,0},{2,3},{4,6},{7,5},{5,4},{6,7},{8,10},{11,9},{9,8... | collective-permute-start | bytes 589832 | tf_op jit(solution)/shard_map/ppermute | solution.py:367
  33.6 6.1 %collective-permute-start.17 = (bf16[576,128]{1,0:T(8,128)(2,1)S(1)}, bf16[576,128]{1,0:T(8,128)(2,1)S(1)}, u32[]{:S(2)}, u32[]{:S(2)}) collective-permute-start(bf16[576,128]{1,0:T(8,128)(2,1)S(1)} %get-tuple-element.28.refs_0_), channel_id=1, source_target_pairs={{0,24},{4,28},{8,16},{12,20},{16,8},{20,12},{24,0},{28,4},{1,25},{... | collective-permute-start | bytes 442376 | tf_op jit(solution)/shard_map/ppermute | solution.py:375
  35.1 7.5 %collective-permute-start.18 = (bf16[576,128]{1,0:T(8,128)(2,1)S(1)}, bf16[576,128]{1,0:T(8,128)(2,1)S(1)}, u32[]{:S(2)}, u32[]{:S(2)}) collective-permute-start(bf16[576,128]{1,0:T(8,128)(2,1)S(1)} %get-tuple-element.28.refs_0_), channel_id=1, source_target_pairs={{0,16},{4,20},{8,24},{12,28},{16,0},{20,4},{24,8},{28,12},{1,17},{... | collective-permute-start | bytes 442376 | tf_op jit(solution)/shard_map/ppermute | solution.py:375
  42.6 2.1 %collective-permute-start.19 = (bf16[2304,128]{1,0:T(8,128)(2,1)S(1)}, bf16[2304,128]{1,0:T(8,128)(2,1)S(1)}, u32[]{:S(2)}, u32[]{:S(2)}) collective-permute-start(bf16[2304,128]{1,0:T(8,128)(2,1)S(1)} %shard_map.102.a_ref), channel_id=1, source_target_pairs={{0,4},{4,0},{8,12},{12,8},{16,20},{20,16},{24,28},{28,24},{1,5},{5... | collective-permute-start | bytes 1769480 | tf_op jit(solution)/shard_map/ppermute | solution.py:375
  45.4 1.2 %collective-permute-start.20 = (f32[8,128]{1,0:T(8,128)S(1)}, f32[8,128]{1,0:T(8,128)S(1)}, u32[]{:S(2)}, u32[]{:S(2)}) collective-permute-start(f32[8,128]{1,0:T(8,128)S(1)} %shard_map.103.o_ref), channel_id=1, source_target_pairs={{0,4},{1,2},{2,1},{3,7},{4,0},{5,6},{6,5},{7,3},{8,12},{9,10},{10,... | collective-permute-start | bytes 12296 | tf_op jit(solution)/shard_map/ppermute | solution.py:372
  46.6 5.5 %collective-permute-start.21 = (f32[8,128]{1,0:T(8,128)S(1)}, f32[8,128]{1,0:T(8,128)S(1)}, u32[]{:S(2)}, u32[]{:S(2)}) collective-permute-start(f32[8,128]{1,0:T(8,128)S(1)} %shard_map.104.j_ref), channel_id=1, source_target_pairs={{0,1},{1,0},{2,3},{3,2},{4,5},{5,4},{6,7},{7,6},{8,9},{9,8},{10,11... | collective-permute-start | bytes 12296 | tf_op jit(solution)/shard_map/ppermute | solution.py:367

commit v3 on v2

--- a/solution.py
+++ b/solution.py
@@ -394,7 +394,7 @@
     queries = None
     if n_dp != parts:
         queries = lax.all_gather(whole[: 4 * block], "dp", axis=0)
-    ours = stack({0: whole} | {s: swap(whole, "dp", s) for s in (2, 6, 4)})
+    ours = stack({0: whole} | {s: swap(whole, "dp", s) for s in (4, 6, 2)})
     joint = token_grads(parts, pieces, first, side_in, targets, lengths)
     scores = row_scores(parts, joint, ours, swap(ours, "dp", 1), queries)
     joined = join_rows(scores, cross(scores))

time: 52.9 us -> 52.6 us (level)
  no operation moved by 1% of the time
where the time goes in v3:
time: 52.6 us; the launch traced here: 52.4 us
  starting transfers between devices  27.2 us (52%)
  waiting for transfers between devices  12.5 us (24%)
  Pallas kernels  11 us (21%)
  local copies, waits for them, and re-layouts  1.53 us (3%)
    ppermute x5, starting transfers between devices, send(): return lax.ppermute(x, 'tensor', pairs)  13.6 us
    ppermute x14, starting transfers between devices, swap(): lax.ppermute(x, axis, [(i, i ^ slot) for i in range(lax.axis_size(axis))])  13.4 us
    pallas_call x15, Pallas kernels, call(): pl.pallas_call(body, out_shape=outs, in_specs=in_specs or [VM] * len(args...  11 us
    ppermute x14, waiting for transfers between devices, swap(): lax.ppermute(x, axis, [(i, i ^ slot) for i in range(lax.axis_size(axis))])  9.89 us
    ppermute x5, waiting for transfers between devices, send(): return lax.ppermute(x, 'tensor', pairs)  1.59 us
    unnamed x8, local copies, waits for them, and re-layouts  1.46 us
  transfers between devices with their start and end apart: 22, of which 8 were waited for; matrix products, arithmetic and copies ran while one was open for 0% of the time, Pallas kernels for 17%

profile of v3, /device:TPU:0, one launch (start us, length us, event | category | flops | bytes accessed | tf_op | source)
XLA Modules:
  0.0 52.4 jit_solution(13947032135523567213)
XLA Ops:
  0.0 0.9 %shard_map.91.b_ref = bf16[64,1024]{1,0:T(8,128)(2,1)S(1)} custom-call(bf16[512,1024]{1,0:T(8,128)(2,1)} %e_ref.1), custom_call_target="tpu_custom_call" | custom-call | bytes 1048576 | tf_op jit(solution)/shard_map/pallas_call | solution.py:30
  0.9 4.1 %collective-permute-start = (bf16[64,1024]{1,0:T(8,128)(2,1)S(1)}, bf16[64,1024]{1,0:T(8,128)(2,1)S(1)}, u32[]{:S(2)}, u32[]{:S(2)}) collective-permute-start(bf16[64,1024]{1,0:T(8,128)(2,1)S(1)} %shard_map.91.b_ref), channel_id=1, source_target_pairs={{0,2},{1,3},{2,0},{3,1},{4,6},{5,7},{6,4},{7,5},{8,10},{9,11},{10,... | collective-permute-start | bytes 393224 | tf_op jit(solution)/shard_map/ppermute | solution.py:375
  5.0 1.6 %collective-permute-start.1 = (bf16[64,1024]{1,0:T(8,128)(2,1)S(1)}, bf16[64,1024]{1,0:T(8,128)(2,1)S(1)}, u32[]{:S(2)}, u32[]{:S(2)}) collective-permute-start(bf16[64,1024]{1,0:T(8,128)(2,1)S(1)} %shard_map.91.b_ref), channel_id=1, source_target_pairs={{0,1},{1,0},{2,3},{3,2},{4,5},{5,4},{6,7},{7,6},{8,9},{9,8},{10,11... | collective-permute-start | bytes 393224 | tf_op jit(solution)/shard_map/ppermute | solution.py:375
  6.6 0.0 collective-permute-start.2
  6.6 0.8 %copy-done = bf16[16,1024]{1,0:T(8,128)(2,1)S(1)} copy-done((bf16[16,1024]{1,0:T(8,128)(2,1)S(1)}, bf16[16,1024]{1,0:T(8,128)(2,1)}, u32[]{:S(2)}) %copy-start) | copy-done | bytes 32792
  7.4 0.7 %copy-done.1 = bf16[3,1024]{1,0:T(4,128)(2,1)S(1)} copy-done((bf16[3,1024]{1,0:T(4,128)(2,1)S(1)}, bf16[3,1024]{1,0:T(4,128)(2,1)}, u32[]{:S(2)}) %copy-start.1) | copy-done | bytes 6168
  8.1 4.6 %shard_map.92 = (bf16[512,1024]{1,0:T(8,128)(2,1)S(1)}, bf16[704,128]{1,0:T(8,128)(2,1)S(1)}, f32[64,1024]{1,0:T(8,128)S(1)}, bf16[1024,4096]{1,0:T(8,128)(2,1)S(1)}) custom-call(bf16[2,256,1024]{2,1,0:T(8,128)(2,1)} %h_any.1, bf16[64,1024]{1,0:T(8,128)(2,1)} %bitcast.2, bf16[64,1024]{1,0:T(8,128)(2,1)} %bitcast.3, bf16[1024,4096]{1,0:T(8,128)(2,1)} %w_any.1, ...), custom_call_target="tpu_custom_call" | custom-call | flops 201326592 | bytes 9869312 | tf_op jit(solution)/shard_map/pallas_call | solution.py:30
  12.7 1.0 %collective-permute-start.10 = (bf16[704,128]{1,0:T(8,128)(2,1)S(1)}, bf16[704,128]{1,0:T(8,128)(2,1)S(1)}, u32[]{:S(2)}, u32[]{:S(2)}) collective-permute-start(bf16[704,128]{1,0:T(8,128)(2,1)S(1)} %get-tuple-element.20.o_ref), channel_id=1, source_target_pairs={{0,1},{1,0},{2,3},{3,2},{4,5},{5,4},{6,7},{7,6},{8,9},{9,8},{10,11... | collective-permute-start | bytes 540680 | tf_op jit(solution)/shard_map/ppermute | solution.py:367
  13.6 0.0 collective-permute-done.b_ref
  13.6 0.8 %shard_map.93.f_ref = f32[64,1024]{1,0:T(8,128)S(1)} custom-call(f32[64,1024]{1,0:T(8,128)S(1)} %get-tuple-element.17.f_ref, bf16[64,1024]{1,0:T(8,128)(2,1)S(1)} %collective-permute-done.b_ref, bf16[1024,4096]{1,0:T(8,128)(2,1)S(1)} %get-tuple-element.18.w_ref), custom_call_target="tpu_custom_call" | custom-call | flops 134217728 | bytes 8781824 | tf_op jit(solution)/shard_map/pallas_call | solution.py:30
  14.4 0.0 collective-permute-done.1.b_ref
  14.4 0.8 %shard_map.94.f_ref = f32[64,1024]{1,0:T(8,128)S(1)} custom-call(f32[64,1024]{1,0:T(8,128)S(1)} %shard_map.93.f_ref, bf16[64,1024]{1,0:T(8,128)(2,1)S(1)} %collective-permute-done.1.b_ref, bf16[1024,4096]{1,0:T(8,128)(2,1)S(1)} %get-tuple-element.18.w_ref), custom_call_target="tpu_custom_call" | custom-call | flops 134217728 | bytes 8781824 | tf_op jit(solution)/shard_map/pallas_call | solution.py:30
  15.2 0.0 copy-start.2
  15.2 0.2 collective-permute-done.2.b_ref
  15.4 0.8 %shard_map.95.a_ref.refs_3_ = bf16[64,1024]{1,0:T(8,128)(2,1)S(1)} custom-call(f32[64,1024]{1,0:T(8,128)S(1)} %shard_map.94.f_ref, bf16[64,1024]{1,0:T(8,128)(2,1)S(1)} %collective-permute-done.2.b_ref, bf16[1024,4096]{1,0:T(8,128)(2,1)S(1)} %get-tuple-element.18.w_ref), custom_call_target="tpu_custom_call" | custom-call | flops 134217728 | bytes 8781824 | tf_op jit(solution)/shard_map/pallas_call | solution.py:30
  16.2 0.1 collective-permute-start.9
  16.3 2.5 %collective-permute-start.3 = (bf16[64,1024]{1,0:T(8,128)(2,1)S(1)}, bf16[64,1024]{1,0:T(8,128)(2,1)S(1)}, u32[]{:S(2)}, u32[]{:S(2)}) collective-permute-start(bf16[64,1024]{1,0:T(8,128)(2,1)S(1)} %shard_map.95.a_ref.refs_3_), channel_id=1, source_target_pairs={{0,24},{4,28},{8,16},{12,20},{16,8},{20,12},{24,0},{28,4},{1,25},{... | collective-permute-start | bytes 393224 | tf_op jit(solution)/shard_map/ppermute | solution.py:375
  18.8 0.5 collective-permute-start.4
  19.3 0.5 %collective-permute-start.5 = (bf16[64,1024]{1,0:T(8,128)(2,1)S(1)}, bf16[64,1024]{1,0:T(8,128)(2,1)S(1)}, u32[]{:S(2)}, u32[]{:S(2)}) collective-permute-start(bf16[64,1024]{1,0:T(8,128)(2,1)S(1)} %shard_map.95.a_ref.refs_3_), channel_id=1, source_target_pairs={{0,8},{4,12},{8,0},{12,4},{16,24},{20,28},{24,16},{28,20},{1,9},{5... | collective-permute-start | bytes 393224 | tf_op jit(solution)/shard_map/ppermute | solution.py:375
  19.8 0.2 shard_map.96
  20.0 0.0 collective-permute-start.11
  20.0 0.3 shard_map.98
  20.3 4.2 %collective-permute-start.12 = (bf16[128,256]{1,0:T(8,128)(2,1)S(1)}, bf16[128,256]{1,0:T(8,128)(2,1)S(1)}, u32[]{:S(2)}, u32[]{:S(2)}) collective-permute-start(bf16[128,256]{1,0:T(8,128)(2,1)S(1)} %shard_map.98), channel_id=1, source_target_pairs={{0,2},{3,1},{1,0},{2,3},{4,6},{7,5},{5,4},{6,7},{8,10},{11,9},{9,8... | collective-permute-start | bytes 196616 | tf_op jit(solution)/shard_map/ppermute | solution.py:367
  24.5 1.3 %collective-permute-done.4.refs_1_ = bf16[64,1024]{1,0:T(8,128)(2,1)S(1)} collective-permute-done((bf16[64,1024]{1,0:T(8,128)(2,1)S(1)}, bf16[64,1024]{1,0:T(8,128)(2,1)S(1)}, u32[]{:S(2)}, u32[]{:S(2)}) %collective-permute-start.4) | collective-permute-done | bytes 131104 | tf_op jit(solution)/shard_map/ppermute | solution.py:375
  25.9 0.0 collective-permute-start.7
  25.9 0.1 collective-permute-done.5.refs_2_
  26.0 0.4 collective-permute-start.8
  26.4 0.0 collective-permute-done.11.c_ref
  26.4 0.2 shard_map.97
  26.6 1.5 %collective-permute-start.16 = (bf16[576,128]{1,0:T(8,128)(2,1)S(1)}, bf16[576,128]{1,0:T(8,128)(2,1)S(1)}, u32[]{:S(2)}, u32[]{:S(2)}) collective-permute-start(bf16[576,128]{1,0:T(8,128)(2,1)S(1)} %get-tuple-element.28.refs_0_), channel_id=1, source_target_pairs={{0,16},{4,20},{8,24},{12,28},{16,0},{20,4},{24,8},{28,12},{1,17},{... | collective-permute-start | bytes 442376 | tf_op jit(solution)/shard_map/ppermute | solution.py:375
  28.1 0.0 collective-permute-done.8.refs_6_
  28.1 0.8 %shard_map.100 = (f32[512,256]{1,0:T(8,128)S(1)}, bf16[512,256]{1,0:T(8,128)(2,1)S(1)}, bf16[512,256]{1,0:T(8,128)(2,1)S(1)}, bf16[384,256]{1,0:T(8,128)(2,1)S(1)}) custom-call(bf16[64,1024]{1,0:T(8,128)(2,1)S(1)} %collective-permute-done.3.refs_0_, bf16[64,1024]{1,0:T(8,128)(2,1)S(1)} %collective-permute-done.4.refs_1_, ...), custom_call_target="tpu_custom_call" | custom-call | flops 536870912 | bytes 2228224 | tf_op jit(solution)/shard_map/pallas_call | solution.py:30
  28.9 2.7 %collective-permute-start.13 = (bf16[512,256]{1,0:T(8,128)(2,1)S(1)}, bf16[512,256]{1,0:T(8,128)(2,1)S(1)}, u32[]{:S(2)}, u32[]{:S(2)}) collective-permute-start(bf16[512,256]{1,0:T(8,128)(2,1)S(1)} %get-tuple-element.25), channel_id=1, source_target_pairs={{0,1},{1,0},{2,3},{3,2},{4,5},{5,4},{6,7},{7,6},{8,9},{9,8},{10,11... | collective-permute-start | bytes 786440 | tf_op jit(solution)/shard_map/ppermute | solution.py:367
  31.6 2.0 %collective-permute-start.15 = (bf16[384,256]{1,0:T(8,128)(2,1)S(1)}, bf16[384,256]{1,0:T(8,128)(2,1)S(1)}, u32[]{:S(2)}, u32[]{:S(2)}) collective-permute-start(bf16[384,256]{1,0:T(8,128)(2,1)S(1)} %get-tuple-element.27), channel_id=1, source_target_pairs={{0,2},{3,1},{1,0},{2,3},{4,6},{7,5},{5,4},{6,7},{8,10},{11,9},{9,8... | collective-permute-start | bytes 589832 | tf_op jit(solution)/shard_map/ppermute | solution.py:367
  33.6 1.5 %collective-permute-start.17 = (bf16[576,128]{1,0:T(8,128)(2,1)S(1)}, bf16[576,128]{1,0:T(8,128)(2,1)S(1)}, u32[]{:S(2)}, u32[]{:S(2)}) collective-permute-start(bf16[576,128]{1,0:T(8,128)(2,1)S(1)} %get-tuple-element.28.refs_0_), channel_id=1, source_target_pairs={{0,24},{4,28},{8,16},{12,20},{16,8},{20,12},{24,0},{28,4},{1,25},{... | collective-permute-start | bytes 442376 | tf_op jit(solution)/shard_map/ppermute | solution.py:375
  35.1 0.5 %collective-permute-start.18 = (bf16[576,128]{1,0:T(8,128)(2,1)S(1)}, bf16[576,128]{1,0:T(8,128)(2,1)S(1)}, u32[]{:S(2)}, u32[]{:S(2)}) collective-permute-start(bf16[576,128]{1,0:T(8,128)(2,1)S(1)} %get-tuple-element.28.refs_0_), channel_id=1, source_target_pairs={{0,8},{4,12},{8,0},{12,4},{16,24},{20,28},{24,16},{28,20},{1,9},{5... | collective-permute-start | bytes 442376 | tf_op jit(solution)/shard_map/ppermute | solution.py:375
  35.6 5.4 %collective-permute-done.17.refs_2_ = bf16[576,128]{1,0:T(8,128)(2,1)S(1)} collective-permute-done((bf16[576,128]{1,0:T(8,128)(2,1)S(1)}, bf16[576,128]{1,0:T(8,128)(2,1)S(1)}, u32[]{:S(2)}, u32[]{:S(2)}) %collective-permute-start.17) | collective-permute-done | bytes 147488 | tf_op jit(solution)/shard_map/ppermute | solution.py:375
  41.0 1.5 %collective-permute-done.18.refs_3_ = bf16[576,128]{1,0:T(8,128)(2,1)S(1)} collective-permute-done((bf16[576,128]{1,0:T(8,128)(2,1)S(1)}, bf16[576,128]{1,0:T(8,128)(2,1)S(1)}, u32[]{:S(2)}, u32[]{:S(2)}) %collective-permute-start.18) | collective-permute-done | bytes 147488 | tf_op jit(solution)/shard_map/ppermute | solution.py:375
  42.5 0.1 collective-permute-start.19
  42.6 0.1 broadcast_in_dim.2.live_ref
  42.7 0.4 shard_map.101.j_ref
  43.1 1.4 %collective-permute-done.19.b_ref = bf16[2304,128]{1,0:T(8,128)(2,1)S(1)} collective-permute-done((bf16[2304,128]{1,0:T(8,128)(2,1)S(1)}, bf16[2304,128]{1,0:T(8,128)(2,1)S(1)}, u32[]{:S(2)}, u32[]{:S(2)}) %collective-permute-start.19) | collective-permute-done | bytes 589856 | tf_op jit(solution)/shard_map/ppermute | solution.py:375
  44.6 0.7 %shard_map.103.o_ref = f32[8,128]{1,0:T(8,128)S(1)} custom-call(bf16[128,512]{1,0:T(8,128)(2,1)S(1)} %shard_map.101.j_ref, bf16[2304,128]{1,0:T(8,128)(2,1)S(1)} %shard_map.102.a_ref, bf16[2304,128]{1,0:T(8,128)(2,1)S(1)} %collective-permute-done.19.b_ref), custom_call_target="tpu_custom_call" | custom-call | flops 4194304 | bytes 1310720 | tf_op jit(solution)/shard_map/pallas_call | solution.py:30
  45.3 0.2 collective-permute-start.20
  45.4 1.0 %collective-permute-done.20.c_ref = f32[8,128]{1,0:T(8,128)S(1)} collective-permute-done((f32[8,128]{1,0:T(8,128)S(1)}, f32[8,128]{1,0:T(8,128)S(1)}, u32[]{:S(2)}, u32[]{:S(2)}) %collective-permute-start.20) | collective-permute-done | bytes 4128 | tf_op jit(solution)/shard_map/ppermute | solution.py:372
  46.5 3.7 %collective-permute-start.21 = (f32[8,128]{1,0:T(8,128)S(1)}, f32[8,128]{1,0:T(8,128)S(1)}, u32[]{:S(2)}, u32[]{:S(2)}) collective-permute-start(f32[8,128]{1,0:T(8,128)S(1)} %shard_map.104.j_ref), channel_id=1, source_target_pairs={{0,1},{1,0},{2,3},{3,2},{4,5},{5,4},{6,7},{7,6},{8,9},{9,8},{10,11... | collective-permute-start | bytes 12296 | tf_op jit(solution)/shard_map/ppermute | solution.py:367
  50.2 1.6 %collective-permute-done.21.c_ref = f32[8,128]{1,0:T(8,128)S(1)} collective-permute-done((f32[8,128]{1,0:T(8,128)S(1)}, f32[8,128]{1,0:T(8,128)S(1)}, u32[]{:S(2)}, u32[]{:S(2)}) %collective-permute-start.21) | collective-permute-done | bytes 4128 | tf_op jit(solution)/shard_map/ppermute | solution.py:367
  51.8 0.6 %shard_map.105 = f32[2,128]{1,0:T(2,128)} custom-call(f32[8,128]{1,0:T(8,128)S(1)} %shard_map.104.j_ref, f32[8,128]{1,0:T(8,128)S(1)} %collective-permute-done.21.c_ref), custom_call_target="tpu_custom_call" | custom-call | bytes 8192 | tf_op jit(solution)/shard_map/pallas_call | solution.py:30
  (20 shorter events, 0.1 us)
Async XLA Ops:
  0.9 12.7 %collective-permute-start = (bf16[64,1024]{1,0:T(8,128)(2,1)S(1)}, bf16[64,1024]{1,0:T(8,128)(2,1)S(1)}, u32[]{:S(2)}, u32[]{:S(2)}) collective-permute-start(bf16[64,1024]{1,0:T(8,128)(2,1)S(1)} %shard_map.91.b_ref), channel_id=1, source_target_pairs={{0,2},{1,3},{2,0},{3,1},{4,6},{5,7},{6,4},{7,5},{8,10},{9,11},{10,... | collective-permute-start | bytes 393224 | tf_op jit(solution)/shard_map/ppermute | solution.py:375
  5.0 9.4 %collective-permute-start.1 = (bf16[64,1024]{1,0:T(8,128)(2,1)S(1)}, bf16[64,1024]{1,0:T(8,128)(2,1)S(1)}, u32[]{:S(2)}, u32[]{:S(2)}) collective-permute-start(bf16[64,1024]{1,0:T(8,128)(2,1)S(1)} %shard_map.91.b_ref), channel_id=1, source_target_pairs={{0,1},{1,0},{2,3},{3,2},{4,5},{5,4},{6,7},{7,6},{8,9},{9,8},{10,11... | collective-permute-start | bytes 393224 | tf_op jit(solution)/shard_map/ppermute | solution.py:375
  6.6 8.8 %collective-permute-start.2 = (bf16[64,1024]{1,0:T(8,128)(2,1)S(1)}, bf16[64,1024]{1,0:T(8,128)(2,1)S(1)}, u32[]{:S(2)}, u32[]{:S(2)}) collective-permute-start(bf16[64,1024]{1,0:T(8,128)(2,1)S(1)} %shard_map.91.b_ref), channel_id=1, source_target_pairs={{0,3},{1,2},{2,1},{3,0},{4,7},{5,6},{6,5},{7,4},{8,11},{9,10},{10,... | collective-permute-start | bytes 393224 | tf_op jit(solution)/shard_map/ppermute | solution.py:375
  6.6 0.8 %copy-start = (bf16[16,1024]{1,0:T(8,128)(2,1)S(1)}, bf16[16,1024]{1,0:T(8,128)(2,1)}, u32[]{:S(2)}) copy-start(bf16[16,1024]{1,0:T(8,128)(2,1)} %q_ref.1) | copy-start | bytes 98308
  7.4 0.7 %copy-start.1 = (bf16[3,1024]{1,0:T(4,128)(2,1)S(1)}, bf16[3,1024]{1,0:T(4,128)(2,1)}, u32[]{:S(2)}) copy-start(bf16[3,1024]{1,0:T(4,128)(2,1)} %c_ref.1) | copy-start | bytes 18436
  12.7 7.2 %collective-permute-start.10 = (bf16[704,128]{1,0:T(8,128)(2,1)S(1)}, bf16[704,128]{1,0:T(8,128)(2,1)S(1)}, u32[]{:S(2)}, u32[]{:S(2)}) collective-permute-start(bf16[704,128]{1,0:T(8,128)(2,1)S(1)} %get-tuple-element.20.o_ref), channel_id=1, source_target_pairs={{0,1},{1,0},{2,3},{3,2},{4,5},{5,4},{6,7},{7,6},{8,9},{9,8},{10,11... | collective-permute-start | bytes 540680 | tf_op jit(solution)/shard_map/ppermute | solution.py:367
  15.2 27.4 %copy-start.3 = (s32[2]{0:T(128)S(1)}, s32[2]{0:T(128)}, u32[]{:S(2)}) copy-start(s32[2]{0:T(128)} %param.11) | copy-start | bytes 28
  15.2 27.5 %copy-start.2 = (s32[2,256]{1,0:T(2,128)S(1)}, s32[2,256]{1,0:T(2,128)}, u32[]{:S(2)}) copy-start(s32[2,256]{1,0:T(2,128)} %t_ref.1) | copy-start | bytes 6148
  16.2 3.8 %collective-permute-start.9 = (bf16[64,1024]{1,0:T(8,128)(2,1)S(1)}, bf16[64,1024]{1,0:T(8,128)(2,1)S(1)}, u32[]{:S(2)}, u32[]{:S(2)}) collective-permute-start(bf16[64,1024]{1,0:T(8,128)(2,1)S(1)} %shard_map.95.a_ref.refs_3_), channel_id=1, source_target_pairs={{0,4},{4,0},{8,12},{12,8},{16,20},{20,16},{24,28},{28,24},{1,5},{5... | collective-permute-start | bytes 393224 | tf_op jit(solution)/shard_map/ppermute | solution.py:375
  16.3 8.3 %collective-permute-start.3 = (bf16[64,1024]{1,0:T(8,128)(2,1)S(1)}, bf16[64,1024]{1,0:T(8,128)(2,1)S(1)}, u32[]{:S(2)}, u32[]{:S(2)}) collective-permute-start(bf16[64,1024]{1,0:T(8,128)(2,1)S(1)} %shard_map.95.a_ref.refs_3_), channel_id=1, source_target_pairs={{0,24},{4,28},{8,16},{12,20},{16,8},{20,12},{24,0},{28,4},{1,25},{... | collective-permute-start | bytes 393224 | tf_op jit(solution)/shard_map/ppermute | solution.py:375
  18.8 7.1 %collective-permute-start.4 = (bf16[64,1024]{1,0:T(8,128)(2,1)S(1)}, bf16[64,1024]{1,0:T(8,128)(2,1)S(1)}, u32[]{:S(2)}, u32[]{:S(2)}) collective-permute-start(bf16[64,1024]{1,0:T(8,128)(2,1)S(1)} %shard_map.95.a_ref.refs_3_), channel_id=1, source_target_pairs={{0,16},{4,20},{8,24},{12,28},{16,0},{20,4},{24,8},{28,12},{1,17},{... | collective-permute-start | bytes 393224 | tf_op jit(solution)/shard_map/ppermute | solution.py:375
  19.3 6.7 %collective-permute-start.5 = (bf16[64,1024]{1,0:T(8,128)(2,1)S(1)}, bf16[64,1024]{1,0:T(8,128)(2,1)S(1)}, u32[]{:S(2)}, u32[]{:S(2)}) collective-permute-start(bf16[64,1024]{1,0:T(8,128)(2,1)S(1)} %shard_map.95.a_ref.refs_3_), channel_id=1, source_target_pairs={{0,8},{4,12},{8,0},{12,4},{16,24},{20,28},{24,16},{28,20},{1,9},{5... | collective-permute-start | bytes 393224 | tf_op jit(solution)/shard_map/ppermute | solution.py:375
  20.0 6.4 %collective-permute-start.11 = (bf16[576,128]{1,0:T(8,128)(2,1)S(1)}, bf16[576,128]{1,0:T(8,128)(2,1)S(1)}, u32[]{:S(2)}, u32[]{:S(2)}) collective-permute-start(bf16[576,128]{1,0:T(8,128)(2,1)S(1)} %get-tuple-element.21.o_ref), channel_id=1, source_target_pairs={{0,4},{1,2},{2,1},{3,7},{4,0},{5,6},{6,5},{7,3},{8,12},{9,10},{10,... | collective-permute-start | bytes 442376 | tf_op jit(solution)/shard_map/ppermute | solution.py:372
  20.3 7.8 %collective-permute-start.12 = (bf16[128,256]{1,0:T(8,128)(2,1)S(1)}, bf16[128,256]{1,0:T(8,128)(2,1)S(1)}, u32[]{:S(2)}, u32[]{:S(2)}) collective-permute-start(bf16[128,256]{1,0:T(8,128)(2,1)S(1)} %shard_map.98), channel_id=1, source_target_pairs={{0,2},{3,1},{1,0},{2,3},{4,6},{7,5},{5,4},{6,7},{8,10},{11,9},{9,8... | collective-permute-start | bytes 196616 | tf_op jit(solution)/shard_map/ppermute | solution.py:367
  24.5 3.6 %collective-permute-start.6 = (bf16[64,1024]{1,0:T(8,128)(2,1)S(1)}, bf16[64,1024]{1,0:T(8,128)(2,1)S(1)}, u32[]{:S(2)}, u32[]{:S(2)}) collective-permute-start(bf16[64,1024]{1,0:T(8,128)(2,1)S(1)} %collective-permute-done.3.refs_0_), channel_id=1, source_target_pairs={{0,4},{4,0},{8,12},{12,8},{16,20},{20,16},{24,28},{28,24},{1,5},{5... | collective-permute-start | bytes 393224 | tf_op jit(solution)/shard_map/ppermute | solution.py:375
  25.9 2.2 %collective-permute-start.7 = (bf16[64,1024]{1,0:T(8,128)(2,1)S(1)}, bf16[64,1024]{1,0:T(8,128)(2,1)S(1)}, u32[]{:S(2)}, u32[]{:S(2)}) collective-permute-start(bf16[64,1024]{1,0:T(8,128)(2,1)S(1)} %collective-permute-done.4.refs_1_), channel_id=1, source_target_pairs={{0,4},{4,0},{8,12},{12,8},{16,20},{20,16},{24,28},{28,24},{1,5},{5... | collective-permute-start | bytes 393224 | tf_op jit(solution)/shard_map/ppermute | solution.py:375
  26.0 2.1 %collective-permute-start.8 = (bf16[64,1024]{1,0:T(8,128)(2,1)S(1)}, bf16[64,1024]{1,0:T(8,128)(2,1)S(1)}, u32[]{:S(2)}, u32[]{:S(2)}) collective-permute-start(bf16[64,1024]{1,0:T(8,128)(2,1)S(1)} %collective-permute-done.5.refs_2_), channel_id=1, source_target_pairs={{0,4},{4,0},{8,12},{12,8},{16,20},{20,16},{24,28},{28,24},{1,5},{5... | collective-permute-start | bytes 393224 | tf_op jit(solution)/shard_map/ppermute | solution.py:375
  26.6 8.5 %collective-permute-start.16 = (bf16[576,128]{1,0:T(8,128)(2,1)S(1)}, bf16[576,128]{1,0:T(8,128)(2,1)S(1)}, u32[]{:S(2)}, u32[]{:S(2)}) collective-permute-start(bf16[576,128]{1,0:T(8,128)(2,1)S(1)} %get-tuple-element.28.refs_0_), channel_id=1, source_target_pairs={{0,16},{4,20},{8,24},{12,28},{16,0},{20,4},{24,8},{28,12},{1,17},{... | collective-permute-start | bytes 442376 | tf_op jit(solution)/shard_map/ppermute | solution.py:375
  28.9 13.7 %collective-permute-start.13 = (bf16[512,256]{1,0:T(8,128)(2,1)S(1)}, bf16[512,256]{1,0:T(8,128)(2,1)S(1)}, u32[]{:S(2)}, u32[]{:S(2)}) collective-permute-start(bf16[512,256]{1,0:T(8,128)(2,1)S(1)} %get-tuple-element.25), channel_id=1, source_target_pairs={{0,1},{1,0},{2,3},{3,2},{4,5},{5,4},{6,7},{7,6},{8,9},{9,8},{10,11... | collective-permute-start | bytes 786440 | tf_op jit(solution)/shard_map/ppermute | solution.py:367
  31.6 11.0 %collective-permute-start.14 = (bf16[512,256]{1,0:T(8,128)(2,1)S(1)}, bf16[512,256]{1,0:T(8,128)(2,1)S(1)}, u32[]{:S(2)}, u32[]{:S(2)}) collective-permute-start(bf16[512,256]{1,0:T(8,128)(2,1)S(1)} %get-tuple-element.26), channel_id=1, source_target_pairs={{0,4},{1,2},{2,1},{3,7},{4,0},{5,6},{6,5},{7,3},{8,12},{9,10},{10,... | collective-permute-start | bytes 786440 | tf_op jit(solution)/shard_map/ppermute | solution.py:372
  31.6 11.0 %collective-permute-start.15 = (bf16[384,256]{1,0:T(8,128)(2,1)S(1)}, bf16[384,256]{1,0:T(8,128)(2,1)S(1)}, u32[]{:S(2)}, u32[]{:S(2)}) collective-permute-start(bf16[384,256]{1,0:T(8,128)(2,1)S(1)} %get-tuple-element.27), channel_id=1, source_target_pairs={{0,2},{3,1},{1,0},{2,3},{4,6},{7,5},{5,4},{6,7},{8,10},{11,9},{9,8... | collective-permute-start | bytes 589832 | tf_op jit(solution)/shard_map/ppermute | solution.py:367
  33.6 7.4 %collective-permute-start.17 = (bf16[576,128]{1,0:T(8,128)(2,1)S(1)}, bf16[576,128]{1,0:T(8,128)(2,1)S(1)}, u32[]{:S(2)}, u32[]{:S(2)}) collective-permute-start(bf16[576,128]{1,0:T(8,128)(2,1)S(1)} %get-tuple-element.28.refs_0_), channel_id=1, source_target_pairs={{0,24},{4,28},{8,16},{12,20},{16,8},{20,12},{24,0},{28,4},{1,25},{... | collective-permute-start | bytes 442376 | tf_op jit(solution)/shard_map/ppermute | solution.py:375
  35.1 7.4 %collective-permute-start.18 = (bf16[576,128]{1,0:T(8,128)(2,1)S(1)}, bf16[576,128]{1,0:T(8,128)(2,1)S(1)}, u32[]{:S(2)}, u32[]{:S(2)}) collective-permute-start(bf16[576,128]{1,0:T(8,128)(2,1)S(1)} %get-tuple-element.28.refs_0_), channel_id=1, source_target_pairs={{0,8},{4,12},{8,0},{12,4},{16,24},{20,28},{24,16},{28,20},{1,9},{5... | collective-permute-start | bytes 442376 | tf_op jit(solution)/shard_map/ppermute | solution.py:375
  42.5 2.1 %collective-permute-start.19 = (bf16[2304,128]{1,0:T(8,128)(2,1)S(1)}, bf16[2304,128]{1,0:T(8,128)(2,1)S(1)}, u32[]{:S(2)}, u32[]{:S(2)}) collective-permute-start(bf16[2304,128]{1,0:T(8,128)(2,1)S(1)} %shard_map.102.a_ref), channel_id=1, source_target_pairs={{0,4},{4,0},{8,12},{12,8},{16,20},{20,16},{24,28},{28,24},{1,5},{5... | collective-permute-start | bytes 1769480 | tf_op jit(solution)/shard_map/ppermute | solution.py:375
  45.3 1.2 %collective-permute-start.20 = (f32[8,128]{1,0:T(8,128)S(1)}, f32[8,128]{1,0:T(8,128)S(1)}, u32[]{:S(2)}, u32[]{:S(2)}) collective-permute-start(f32[8,128]{1,0:T(8,128)S(1)} %shard_map.103.o_ref), channel_id=1, source_target_pairs={{0,4},{1,2},{2,1},{3,7},{4,0},{5,6},{6,5},{7,3},{8,12},{9,10},{10,... | collective-permute-start | bytes 12296 | tf_op jit(solution)/shard_map/ppermute | solution.py:372
  46.5 5.3 %collective-permute-start.21 = (f32[8,128]{1,0:T(8,128)S(1)}, f32[8,128]{1,0:T(8,128)S(1)}, u32[]{:S(2)}, u32[]{:S(2)}) collective-permute-start(f32[8,128]{1,0:T(8,128)S(1)} %shard_map.104.j_ref), channel_id=1, source_target_pairs={{0,1},{1,0},{2,3},{3,2},{4,5},{5,4},{6,7},{7,6},{8,9},{9,8},{10,11... | collective-permute-start | bytes 12296 | tf_op jit(solution)/shard_map/ppermute | solution.py:367

commit v4 on v1

--- a/solution.py
+++ b/solution.py
@@ -297,21 +297,23 @@
     )
 
 
-def row_scores(parts, joint, ours, theirs, queries):
+def row_scores(parts, joint, shares, queries):
     wide, vocab = joint.shape
     rank = wide // 2
     step = vocab // parts
     lines = rank // 2
     count = parts if queries is None else queries.shape[0]
-    high = ours.shape[0] // (parts // 2)
+    high = shares[0].shape[0] // 2
     rows = (high - step) // lines
     extra_args = () if queries is None else (queries,)
 
-    def body(j_ref, a_ref, b_ref, *refs):
+    def body(j_ref, a_ref, b_ref, c_ref, d_ref, *refs):
         q_ref, refs = (None, refs) if queries is None else (refs[0], refs[1:])
         out_ref, hold = refs
         own = lax.axis_index("dp") % parts
-        s_refs = [ref.at[pl.ds(k * high, high), :] for k in range(parts // 2) for ref in (a_ref, b_ref)]
+        s_refs = []
+        for begin, pair in ((0, (a_ref, b_ref)), (1, (c_ref, d_ref)), (1, (a_ref, b_ref)), (0, (c_ref, d_ref))):
+            s_refs += [ref.at[pl.ds(begin * high, high), :] for ref in pair]
         u = jnp.concatenate([ref[rows * lines :, :] for ref in s_refs], axis=0)
         grads = halve(jnp.dot(j_ref[...], u, preferred_element_type=f32))
         grads = grads[:, :rank] + grads[:, rank:]
@@ -331,7 +333,7 @@
     return call(
         body,
         arr((8, count * rows), f32),
-        (joint, ours, theirs, *extra_args),
+        (joint, *shares, *extra_args),
         2 * vocab * rank * rank,
         scratch=[pltpu.VMEM((count * rows, 2 * wide), bf16)],
     )
@@ -393,9 +395,11 @@
     queries = None
     if n_dp != parts:
         queries = lax.all_gather(whole[: 4 * block], "dp", axis=0)
-    ours = stack([whole] + [swap(whole, "dp", s) for s in range(2, parts, 2)])
+    others = {s: swap(whole, "dp", s) for s in range(2, parts, 2)}
+    pairs = stack((whole, others[4])), stack((others[6], others[2]))
+    shares = [y for x in pairs for y in (x, swap(x, "dp", 1))]
     joint = token_grads(parts, pieces, first, side_in, targets, lengths)
-    scores = row_scores(parts, joint, ours, swap(ours, "dp", 1), queries)
+    scores = row_scores(parts, joint, shares, queries)
     joined = join_rows(scores, cross(scores))
     return pick_rows(joined, send(joined, NEAR))
 

time: 52.6 us -> 52.6 us (level)
    ppermute x14 -> x15, waiting for transfers between devices: 9.36 us -> 9.41 us  [swap(): lax.ppermute(x, axis, [(i, i ^ slot) for i in range(lax.axis_size(axis))])]
    ppermute x14 -> x15, starting transfers between devices: 13.3 us -> 13.4 us  [swap(): lax.ppermute(x, axis, [(i, i ^ slot) for i in range(lax.axis_size(axis))])]
    pallas_call x15 -> x16, Pallas kernels: 11 us -> 11 us  [call(): pl.pallas_call(body, out_shape=outs, in_specs=in_specs or [VM] * len(args...]
  transfers between devices with their start and end apart: 22 -> 23, of which waited for: 7 -> 8; matrix products, arithmetic and copies ran while one was open for 0% -> 0% of each run, Pallas kernels for 17% -> 17%
where the time goes in v4:
time: 52.6 us; the launch traced here: 52.4 us
  starting transfers between devices  27.6 us (52%)
  waiting for transfers between devices  12 us (23%)
  Pallas kernels  11 us (21%)
  local copies, waits for them, and re-layouts  1.53 us (3%)
    ppermute x5, starting transfers between devices, send(): return lax.ppermute(x, 'tensor', pairs)  14.1 us
    ppermute x15, starting transfers between devices, swap(): lax.ppermute(x, axis, [(i, i ^ slot) for i in range(lax.axis_size(axis))])  13.4 us
    pallas_call x16, Pallas kernels, call(): pl.pallas_call(body, out_shape=outs, in_specs=in_specs or [VM] * len(args...  11 us
    ppermute x15, waiting for transfers between devices, swap(): lax.ppermute(x, axis, [(i, i ^ slot) for i in range(lax.axis_size(axis))])  9.41 us
    ppermute x5, waiting for transfers between devices, send(): return lax.ppermute(x, 'tensor', pairs)  1.59 us
    unnamed x8, local copies, waits for them, and re-layouts  1.46 us
  transfers between devices with their start and end apart: 23, of which 8 were waited for; matrix products, arithmetic and copies ran while one was open for 0% of the time, Pallas kernels for 17%

profile of v4, /device:TPU:0, one launch (start us, length us, event | category | flops | bytes accessed | tf_op | source)
XLA Modules:
  0.0 52.4 jit_solution(2220186942020685249)
XLA Ops:
  0.0 0.9 %shard_map.91.b_ref = bf16[64,1024]{1,0:T(8,128)(2,1)S(1)} custom-call(bf16[512,1024]{1,0:T(8,128)(2,1)} %e_ref.1), custom_call_target="tpu_custom_call" | custom-call | bytes 1048576 | tf_op jit(solution)/shard_map/pallas_call | solution.py:30
  0.9 4.1 %collective-permute-start = (bf16[64,1024]{1,0:T(8,128)(2,1)S(1)}, bf16[64,1024]{1,0:T(8,128)(2,1)S(1)}, u32[]{:S(2)}, u32[]{:S(2)}) collective-permute-start(bf16[64,1024]{1,0:T(8,128)(2,1)S(1)} %shard_map.91.b_ref), channel_id=1, source_target_pairs={{0,2},{1,3},{2,0},{3,1},{4,6},{5,7},{6,4},{7,5},{8,10},{9,11},{10,... | collective-permute-start | bytes 393224 | tf_op jit(solution)/shard_map/ppermute | solution.py:376
  5.0 1.6 %collective-permute-start.1 = (bf16[64,1024]{1,0:T(8,128)(2,1)S(1)}, bf16[64,1024]{1,0:T(8,128)(2,1)S(1)}, u32[]{:S(2)}, u32[]{:S(2)}) collective-permute-start(bf16[64,1024]{1,0:T(8,128)(2,1)S(1)} %shard_map.91.b_ref), channel_id=1, source_target_pairs={{0,1},{1,0},{2,3},{3,2},{4,5},{5,4},{6,7},{7,6},{8,9},{9,8},{10,11... | collective-permute-start | bytes 393224 | tf_op jit(solution)/shard_map/ppermute | solution.py:376
  6.6 0.0 collective-permute-start.2
  6.6 0.8 %copy-done = bf16[16,1024]{1,0:T(8,128)(2,1)S(1)} copy-done((bf16[16,1024]{1,0:T(8,128)(2,1)S(1)}, bf16[16,1024]{1,0:T(8,128)(2,1)}, u32[]{:S(2)}) %copy-start) | copy-done | bytes 32792
  7.4 0.7 %copy-done.1 = bf16[3,1024]{1,0:T(4,128)(2,1)S(1)} copy-done((bf16[3,1024]{1,0:T(4,128)(2,1)S(1)}, bf16[3,1024]{1,0:T(4,128)(2,1)}, u32[]{:S(2)}) %copy-start.1) | copy-done | bytes 6168
  8.1 4.6 %shard_map.92 = (bf16[512,1024]{1,0:T(8,128)(2,1)S(1)}, bf16[704,128]{1,0:T(8,128)(2,1)S(1)}, f32[64,1024]{1,0:T(8,128)S(1)}, bf16[1024,4096]{1,0:T(8,128)(2,1)S(1)}) custom-call(bf16[2,256,1024]{2,1,0:T(8,128)(2,1)} %h_any.1, bf16[64,1024]{1,0:T(8,128)(2,1)} %bitcast.2, bf16[64,1024]{1,0:T(8,128)(2,1)} %bitcast.3, bf16[1024,4096]{1,0:T(8,128)(2,1)} %w_any.1, ...), custom_call_target="tpu_custom_call" | custom-call | flops 201326592 | bytes 9869312 | tf_op jit(solution)/shard_map/pallas_call | solution.py:30
  12.7 1.0 %collective-permute-start.10 = (bf16[704,128]{1,0:T(8,128)(2,1)S(1)}, bf16[704,128]{1,0:T(8,128)(2,1)S(1)}, u32[]{:S(2)}, u32[]{:S(2)}) collective-permute-start(bf16[704,128]{1,0:T(8,128)(2,1)S(1)} %get-tuple-element.20.o_ref), channel_id=1, source_target_pairs={{0,1},{1,0},{2,3},{3,2},{4,5},{5,4},{6,7},{7,6},{8,9},{9,8},{10,11... | collective-permute-start | bytes 540680 | tf_op jit(solution)/shard_map/ppermute | solution.py:368
  13.6 0.0 collective-permute-done.b_ref
  13.6 0.8 %shard_map.93.f_ref = f32[64,1024]{1,0:T(8,128)S(1)} custom-call(f32[64,1024]{1,0:T(8,128)S(1)} %get-tuple-element.17.f_ref, bf16[64,1024]{1,0:T(8,128)(2,1)S(1)} %collective-permute-done.b_ref, bf16[1024,4096]{1,0:T(8,128)(2,1)S(1)} %get-tuple-element.18.w_ref), custom_call_target="tpu_custom_call" | custom-call | flops 134217728 | bytes 8781824 | tf_op jit(solution)/shard_map/pallas_call | solution.py:30
  14.4 0.0 collective-permute-done.1.b_ref
  14.4 0.8 %shard_map.94.f_ref = f32[64,1024]{1,0:T(8,128)S(1)} custom-call(f32[64,1024]{1,0:T(8,128)S(1)} %shard_map.93.f_ref, bf16[64,1024]{1,0:T(8,128)(2,1)S(1)} %collective-permute-done.1.b_ref, bf16[1024,4096]{1,0:T(8,128)(2,1)S(1)} %get-tuple-element.18.w_ref), custom_call_target="tpu_custom_call" | custom-call | flops 134217728 | bytes 8781824 | tf_op jit(solution)/shard_map/pallas_call | solution.py:30
  15.2 0.0 copy-start.2
  15.2 0.2 collective-permute-done.2.b_ref
  15.4 0.8 %shard_map.95.a_ref.refs_3_ = bf16[64,1024]{1,0:T(8,128)(2,1)S(1)} custom-call(f32[64,1024]{1,0:T(8,128)S(1)} %shard_map.94.f_ref, bf16[64,1024]{1,0:T(8,128)(2,1)S(1)} %collective-permute-done.2.b_ref, bf16[1024,4096]{1,0:T(8,128)(2,1)S(1)} %get-tuple-element.18.w_ref), custom_call_target="tpu_custom_call" | custom-call | flops 134217728 | bytes 8781824 | tf_op jit(solution)/shard_map/pallas_call | solution.py:30
  16.2 0.1 collective-permute-start.9
  16.3 2.5 %collective-permute-start.3 = (bf16[64,1024]{1,0:T(8,128)(2,1)S(1)}, bf16[64,1024]{1,0:T(8,128)(2,1)S(1)}, u32[]{:S(2)}, u32[]{:S(2)}) collective-permute-start(bf16[64,1024]{1,0:T(8,128)(2,1)S(1)} %shard_map.95.a_ref.refs_3_), channel_id=1, source_target_pairs={{0,24},{4,28},{8,16},{12,20},{16,8},{20,12},{24,0},{28,4},{1,25},{... | collective-permute-start | bytes 393224 | tf_op jit(solution)/shard_map/ppermute | solution.py:376
  18.8 0.5 collective-permute-start.4
  19.3 0.5 %collective-permute-start.5 = (bf16[64,1024]{1,0:T(8,128)(2,1)S(1)}, bf16[64,1024]{1,0:T(8,128)(2,1)S(1)}, u32[]{:S(2)}, u32[]{:S(2)}) collective-permute-start(bf16[64,1024]{1,0:T(8,128)(2,1)S(1)} %shard_map.95.a_ref.refs_3_), channel_id=1, source_target_pairs={{0,8},{4,12},{8,0},{12,4},{16,24},{20,28},{24,16},{28,20},{1,9},{5... | collective-permute-start | bytes 393224 | tf_op jit(solution)/shard_map/ppermute | solution.py:376
  19.8 0.2 shard_map.96
  20.0 0.0 collective-permute-start.11
  20.0 0.3 shard_map.98
  20.3 4.2 %collective-permute-start.12 = (bf16[128,256]{1,0:T(8,128)(2,1)S(1)}, bf16[128,256]{1,0:T(8,128)(2,1)S(1)}, u32[]{:S(2)}, u32[]{:S(2)}) collective-permute-start(bf16[128,256]{1,0:T(8,128)(2,1)S(1)} %shard_map.98), channel_id=1, source_target_pairs={{0,2},{3,1},{1,0},{2,3},{4,6},{7,5},{5,4},{6,7},{8,10},{11,9},{9,8... | collective-permute-start | bytes 196616 | tf_op jit(solution)/shard_map/ppermute | solution.py:368
  24.5 1.3 %collective-permute-done.4.refs_1_ = bf16[64,1024]{1,0:T(8,128)(2,1)S(1)} collective-permute-done((bf16[64,1024]{1,0:T(8,128)(2,1)S(1)}, bf16[64,1024]{1,0:T(8,128)(2,1)S(1)}, u32[]{:S(2)}, u32[]{:S(2)}) %collective-permute-start.4) | collective-permute-done | bytes 131104 | tf_op jit(solution)/shard_map/ppermute | solution.py:376
  25.9 0.0 collective-permute-start.7
  25.9 0.1 collective-permute-done.5.refs_2_
  26.0 0.4 collective-permute-start.8
  26.4 0.2 shard_map.97
  26.6 1.5 %collective-permute-start.16 = (bf16[576,128]{1,0:T(8,128)(2,1)S(1)}, bf16[576,128]{1,0:T(8,128)(2,1)S(1)}, u32[]{:S(2)}, u32[]{:S(2)}) collective-permute-start(bf16[576,128]{1,0:T(8,128)(2,1)S(1)} %get-tuple-element.28.refs_0_), channel_id=1, source_target_pairs={{0,16},{4,20},{8,24},{12,28},{16,0},{20,4},{24,8},{28,12},{1,17},{... | collective-permute-start | bytes 442376 | tf_op jit(solution)/shard_map/ppermute | solution.py:376
  28.1 0.0 collective-permute-done.7.refs_5_
  28.1 0.0 collective-permute-done.8.refs_6_
  28.1 0.8 %shard_map.100 = (f32[512,256]{1,0:T(8,128)S(1)}, bf16[512,256]{1,0:T(8,128)(2,1)S(1)}, bf16[512,256]{1,0:T(8,128)(2,1)S(1)}, bf16[384,256]{1,0:T(8,128)(2,1)S(1)}) custom-call(bf16[64,1024]{1,0:T(8,128)(2,1)S(1)} %collective-permute-done.3.refs_0_, bf16[64,1024]{1,0:T(8,128)(2,1)S(1)} %collective-permute-done.4.refs_1_, ...), custom_call_target="tpu_custom_call" | custom-call | flops 536870912 | bytes 2228224 | tf_op jit(solution)/shard_map/pallas_call | solution.py:30
  28.9 2.7 %collective-permute-start.13 = (bf16[512,256]{1,0:T(8,128)(2,1)S(1)}, bf16[512,256]{1,0:T(8,128)(2,1)S(1)}, u32[]{:S(2)}, u32[]{:S(2)}) collective-permute-start(bf16[512,256]{1,0:T(8,128)(2,1)S(1)} %get-tuple-element.25), channel_id=1, source_target_pairs={{0,1},{1,0},{2,3},{3,2},{4,5},{5,4},{6,7},{7,6},{8,9},{9,8},{10,11... | collective-permute-start | bytes 786440 | tf_op jit(solution)/shard_map/ppermute | solution.py:368
  31.6 2.0 %collective-permute-start.15 = (bf16[384,256]{1,0:T(8,128)(2,1)S(1)}, bf16[384,256]{1,0:T(8,128)(2,1)S(1)}, u32[]{:S(2)}, u32[]{:S(2)}) collective-permute-start(bf16[384,256]{1,0:T(8,128)(2,1)S(1)} %get-tuple-element.27), channel_id=1, source_target_pairs={{0,2},{3,1},{1,0},{2,3},{4,6},{7,5},{5,4},{6,7},{8,10},{11,9},{9,8... | collective-permute-start | bytes 589832 | tf_op jit(solution)/shard_map/ppermute | solution.py:368
  33.6 1.5 %collective-permute-start.18 = (bf16[576,128]{1,0:T(8,128)(2,1)S(1)}, bf16[576,128]{1,0:T(8,128)(2,1)S(1)}, u32[]{:S(2)}, u32[]{:S(2)}) collective-permute-start(bf16[576,128]{1,0:T(8,128)(2,1)S(1)} %get-tuple-element.28.refs_0_), channel_id=1, source_target_pairs={{0,24},{4,28},{8,16},{12,20},{16,8},{20,12},{24,0},{28,4},{1,25},{... | collective-permute-start | bytes 442376 | tf_op jit(solution)/shard_map/ppermute | solution.py:376
  35.1 0.5 %collective-permute-start.19 = (bf16[576,128]{1,0:T(8,128)(2,1)S(1)}, bf16[576,128]{1,0:T(8,128)(2,1)S(1)}, u32[]{:S(2)}, u32[]{:S(2)}) collective-permute-start(bf16[576,128]{1,0:T(8,128)(2,1)S(1)} %get-tuple-element.28.refs_0_), channel_id=1, source_target_pairs={{0,8},{4,12},{8,0},{12,4},{16,24},{20,28},{24,16},{28,20},{1,9},{5... | collective-permute-start | bytes 442376 | tf_op jit(solution)/shard_map/ppermute | solution.py:376
  35.7 5.3 %collective-permute-done.18.refs_0_ = bf16[576,128]{1,0:T(8,128)(2,1)S(1)} collective-permute-done((bf16[576,128]{1,0:T(8,128)(2,1)S(1)}, bf16[576,128]{1,0:T(8,128)(2,1)S(1)}, u32[]{:S(2)}, u32[]{:S(2)}) %collective-permute-start.18) | collective-permute-done | bytes 147488 | tf_op jit(solution)/shard_map/ppermute | solution.py:376
  41.0 1.5 %collective-permute-done.19.refs_1_ = bf16[576,128]{1,0:T(8,128)(2,1)S(1)} collective-permute-done((bf16[576,128]{1,0:T(8,128)(2,1)S(1)}, bf16[576,128]{1,0:T(8,128)(2,1)S(1)}, u32[]{:S(2)}, u32[]{:S(2)}) %collective-permute-start.19) | collective-permute-done | bytes 147488 | tf_op jit(solution)/shard_map/ppermute | solution.py:376
  42.5 0.1 collective-permute-start.20
  42.6 0.1 broadcast_in_dim.2.live_ref
  42.7 0.5 shard_map.101.j_ref
  43.2 1.0 %collective-permute-done.20.d_ref = bf16[1152,128]{1,0:T(8,128)(2,1)S(1)} collective-permute-done((bf16[1152,128]{1,0:T(8,128)(2,1)S(1)}, bf16[1152,128]{1,0:T(8,128)(2,1)S(1)}, u32[]{:S(2)}, u32[]{:S(2)}) %collective-permute-start.20) | collective-permute-done | bytes 294944 | tf_op jit(solution)/shard_map/ppermute | solution.py:376
  44.1 0.7 %shard_map.104.o_ref = f32[8,128]{1,0:T(8,128)S(1)} custom-call(bf16[128,512]{1,0:T(8,128)(2,1)S(1)} %shard_map.101.j_ref, bf16[1152,128]{1,0:T(8,128)(2,1)S(1)} %shard_map.102.a_ref, bf16[1152,128]{1,0:T(8,128)(2,1)S(1)} %collective-permute-done.17.b_ref, bf16[1152,128]{1,0:T(8,128)(2,1)S(1)} %shard_map.103.c_ref, ...), custom_call_target="tpu_custom_call" | custom-call | flops 4194304 | bytes 1310720 | tf_op jit(solution)/shard_map/pallas_call | solution.py:30
  44.8 0.2 collective-permute-start.21
  45.0 1.0 %collective-permute-done.21.c_ref = f32[8,128]{1,0:T(8,128)S(1)} collective-permute-done((f32[8,128]{1,0:T(8,128)S(1)}, f32[8,128]{1,0:T(8,128)S(1)}, u32[]{:S(2)}, u32[]{:S(2)}) %collective-permute-start.21) | collective-permute-done | bytes 4128 | tf_op jit(solution)/shard_map/ppermute | solution.py:373
  46.0 4.2 %collective-permute-start.22 = (f32[8,128]{1,0:T(8,128)S(1)}, f32[8,128]{1,0:T(8,128)S(1)}, u32[]{:S(2)}, u32[]{:S(2)}) collective-permute-start(f32[8,128]{1,0:T(8,128)S(1)} %shard_map.105.j_ref), channel_id=1, source_target_pairs={{0,1},{1,0},{2,3},{3,2},{4,5},{5,4},{6,7},{7,6},{8,9},{9,8},{10,11... | collective-permute-start | bytes 12296 | tf_op jit(solution)/shard_map/ppermute | solution.py:368
  50.2 1.6 %collective-permute-done.22.c_ref = f32[8,128]{1,0:T(8,128)S(1)} collective-permute-done((f32[8,128]{1,0:T(8,128)S(1)}, f32[8,128]{1,0:T(8,128)S(1)}, u32[]{:S(2)}, u32[]{:S(2)}) %collective-permute-start.22) | collective-permute-done | bytes 4128 | tf_op jit(solution)/shard_map/ppermute | solution.py:368
  51.8 0.6 %shard_map.106 = f32[2,128]{1,0:T(2,128)} custom-call(f32[8,128]{1,0:T(8,128)S(1)} %shard_map.105.j_ref, f32[8,128]{1,0:T(8,128)S(1)} %collective-permute-done.22.c_ref), custom_call_target="tpu_custom_call" | custom-call | bytes 8192 | tf_op jit(solution)/shard_map/pallas_call | solution.py:30
  (23 shorter events, 0.1 us)
Async XLA Ops:
  0.9 12.7 %collective-permute-start = (bf16[64,1024]{1,0:T(8,128)(2,1)S(1)}, bf16[64,1024]{1,0:T(8,128)(2,1)S(1)}, u32[]{:S(2)}, u32[]{:S(2)}) collective-permute-start(bf16[64,1024]{1,0:T(8,128)(2,1)S(1)} %shard_map.91.b_ref), channel_id=1, source_target_pairs={{0,2},{1,3},{2,0},{3,1},{4,6},{5,7},{6,4},{7,5},{8,10},{9,11},{10,... | collective-permute-start | bytes 393224 | tf_op jit(solution)/shard_map/ppermute | solution.py:376
  5.0 9.4 %collective-permute-start.1 = (bf16[64,1024]{1,0:T(8,128)(2,1)S(1)}, bf16[64,1024]{1,0:T(8,128)(2,1)S(1)}, u32[]{:S(2)}, u32[]{:S(2)}) collective-permute-start(bf16[64,1024]{1,0:T(8,128)(2,1)S(1)} %shard_map.91.b_ref), channel_id=1, source_target_pairs={{0,1},{1,0},{2,3},{3,2},{4,5},{5,4},{6,7},{7,6},{8,9},{9,8},{10,11... | collective-permute-start | bytes 393224 | tf_op jit(solution)/shard_map/ppermute | solution.py:376
  6.6 8.8 %collective-permute-start.2 = (bf16[64,1024]{1,0:T(8,128)(2,1)S(1)}, bf16[64,1024]{1,0:T(8,128)(2,1)S(1)}, u32[]{:S(2)}, u32[]{:S(2)}) collective-permute-start(bf16[64,1024]{1,0:T(8,128)(2,1)S(1)} %shard_map.91.b_ref), channel_id=1, source_target_pairs={{0,3},{1,2},{2,1},{3,0},{4,7},{5,6},{6,5},{7,4},{8,11},{9,10},{10,... | collective-permute-start | bytes 393224 | tf_op jit(solution)/shard_map/ppermute | solution.py:376
  6.6 0.8 %copy-start = (bf16[16,1024]{1,0:T(8,128)(2,1)S(1)}, bf16[16,1024]{1,0:T(8,128)(2,1)}, u32[]{:S(2)}) copy-start(bf16[16,1024]{1,0:T(8,128)(2,1)} %q_ref.1) | copy-start | bytes 98308
  7.4 0.7 %copy-start.1 = (bf16[3,1024]{1,0:T(4,128)(2,1)S(1)}, bf16[3,1024]{1,0:T(4,128)(2,1)}, u32[]{:S(2)}) copy-start(bf16[3,1024]{1,0:T(4,128)(2,1)} %c_ref.1) | copy-start | bytes 18436
  12.7 7.2 %collective-permute-start.10 = (bf16[704,128]{1,0:T(8,128)(2,1)S(1)}, bf16[704,128]{1,0:T(8,128)(2,1)S(1)}, u32[]{:S(2)}, u32[]{:S(2)}) collective-permute-start(bf16[704,128]{1,0:T(8,128)(2,1)S(1)} %get-tuple-element.20.o_ref), channel_id=1, source_target_pairs={{0,1},{1,0},{2,3},{3,2},{4,5},{5,4},{6,7},{7,6},{8,9},{9,8},{10,11... | collective-permute-start | bytes 540680 | tf_op jit(solution)/shard_map/ppermute | solution.py:368
  15.2 27.4 %copy-start.3 = (s32[2]{0:T(128)S(1)}, s32[2]{0:T(128)}, u32[]{:S(2)}) copy-start(s32[2]{0:T(128)} %param.11) | copy-start | bytes 28
  15.2 27.5 %copy-start.2 = (s32[2,256]{1,0:T(2,128)S(1)}, s32[2,256]{1,0:T(2,128)}, u32[]{:S(2)}) copy-start(s32[2,256]{1,0:T(2,128)} %t_ref.1) | copy-start | bytes 6148
  16.2 3.8 %collective-permute-start.9 = (bf16[64,1024]{1,0:T(8,128)(2,1)S(1)}, bf16[64,1024]{1,0:T(8,128)(2,1)S(1)}, u32[]{:S(2)}, u32[]{:S(2)}) collective-permute-start(bf16[64,1024]{1,0:T(8,128)(2,1)S(1)} %shard_map.95.a_ref.refs_3_), channel_id=1, source_target_pairs={{0,4},{4,0},{8,12},{12,8},{16,20},{20,16},{24,28},{28,24},{1,5},{5... | collective-permute-start | bytes 393224 | tf_op jit(solution)/shard_map/ppermute | solution.py:376
  16.3 8.3 %collective-permute-start.3 = (bf16[64,1024]{1,0:T(8,128)(2,1)S(1)}, bf16[64,1024]{1,0:T(8,128)(2,1)S(1)}, u32[]{:S(2)}, u32[]{:S(2)}) collective-permute-start(bf16[64,1024]{1,0:T(8,128)(2,1)S(1)} %shard_map.95.a_ref.refs_3_), channel_id=1, source_target_pairs={{0,24},{4,28},{8,16},{12,20},{16,8},{20,12},{24,0},{28,4},{1,25},{... | collective-permute-start | bytes 393224 | tf_op jit(solution)/shard_map/ppermute | solution.py:376
  18.8 7.1 %collective-permute-start.4 = (bf16[64,1024]{1,0:T(8,128)(2,1)S(1)}, bf16[64,1024]{1,0:T(8,128)(2,1)S(1)}, u32[]{:S(2)}, u32[]{:S(2)}) collective-permute-start(bf16[64,1024]{1,0:T(8,128)(2,1)S(1)} %shard_map.95.a_ref.refs_3_), channel_id=1, source_target_pairs={{0,16},{4,20},{8,24},{12,28},{16,0},{20,4},{24,8},{28,12},{1,17},{... | collective-permute-start | bytes 393224 | tf_op jit(solution)/shard_map/ppermute | solution.py:376
  19.3 6.7 %collective-permute-start.5 = (bf16[64,1024]{1,0:T(8,128)(2,1)S(1)}, bf16[64,1024]{1,0:T(8,128)(2,1)S(1)}, u32[]{:S(2)}, u32[]{:S(2)}) collective-permute-start(bf16[64,1024]{1,0:T(8,128)(2,1)S(1)} %shard_map.95.a_ref.refs_3_), channel_id=1, source_target_pairs={{0,8},{4,12},{8,0},{12,4},{16,24},{20,28},{24,16},{28,20},{1,9},{5... | collective-permute-start | bytes 393224 | tf_op jit(solution)/shard_map/ppermute | solution.py:376
  20.0 6.4 %collective-permute-start.11 = (bf16[576,128]{1,0:T(8,128)(2,1)S(1)}, bf16[576,128]{1,0:T(8,128)(2,1)S(1)}, u32[]{:S(2)}, u32[]{:S(2)}) collective-permute-start(bf16[576,128]{1,0:T(8,128)(2,1)S(1)} %get-tuple-element.21.o_ref), channel_id=1, source_target_pairs={{0,4},{1,2},{2,1},{3,7},{4,0},{5,6},{6,5},{7,3},{8,12},{9,10},{10,... | collective-permute-start | bytes 442376 | tf_op jit(solution)/shard_map/ppermute | solution.py:373
  20.3 7.8 %collective-permute-start.12 = (bf16[128,256]{1,0:T(8,128)(2,1)S(1)}, bf16[128,256]{1,0:T(8,128)(2,1)S(1)}, u32[]{:S(2)}, u32[]{:S(2)}) collective-permute-start(bf16[128,256]{1,0:T(8,128)(2,1)S(1)} %shard_map.98), channel_id=1, source_target_pairs={{0,2},{3,1},{1,0},{2,3},{4,6},{7,5},{5,4},{6,7},{8,10},{11,9},{9,8... | collective-permute-start | bytes 196616 | tf_op jit(solution)/shard_map/ppermute | solution.py:368
  24.5 3.6 %collective-permute-start.6 = (bf16[64,1024]{1,0:T(8,128)(2,1)S(1)}, bf16[64,1024]{1,0:T(8,128)(2,1)S(1)}, u32[]{:S(2)}, u32[]{:S(2)}) collective-permute-start(bf16[64,1024]{1,0:T(8,128)(2,1)S(1)} %collective-permute-done.3.refs_0_), channel_id=1, source_target_pairs={{0,4},{4,0},{8,12},{12,8},{16,20},{20,16},{24,28},{28,24},{1,5},{5... | collective-permute-start | bytes 393224 | tf_op jit(solution)/shard_map/ppermute | solution.py:376
  25.9 2.2 %collective-permute-start.7 = (bf16[64,1024]{1,0:T(8,128)(2,1)S(1)}, bf16[64,1024]{1,0:T(8,128)(2,1)S(1)}, u32[]{:S(2)}, u32[]{:S(2)}) collective-permute-start(bf16[64,1024]{1,0:T(8,128)(2,1)S(1)} %collective-permute-done.4.refs_1_), channel_id=1, source_target_pairs={{0,4},{4,0},{8,12},{12,8},{16,20},{20,16},{24,28},{28,24},{1,5},{5... | collective-permute-start | bytes 393224 | tf_op jit(solution)/shard_map/ppermute | solution.py:376
  26.0 2.1 %collective-permute-start.8 = (bf16[64,1024]{1,0:T(8,128)(2,1)S(1)}, bf16[64,1024]{1,0:T(8,128)(2,1)S(1)}, u32[]{:S(2)}, u32[]{:S(2)}) collective-permute-start(bf16[64,1024]{1,0:T(8,128)(2,1)S(1)} %collective-permute-done.5.refs_2_), channel_id=1, source_target_pairs={{0,4},{4,0},{8,12},{12,8},{16,20},{20,16},{24,28},{28,24},{1,5},{5... | collective-permute-start | bytes 393224 | tf_op jit(solution)/shard_map/ppermute | solution.py:376
  26.6 8.5 %collective-permute-start.16 = (bf16[576,128]{1,0:T(8,128)(2,1)S(1)}, bf16[576,128]{1,0:T(8,128)(2,1)S(1)}, u32[]{:S(2)}, u32[]{:S(2)}) collective-permute-start(bf16[576,128]{1,0:T(8,128)(2,1)S(1)} %get-tuple-element.28.refs_0_), channel_id=1, source_target_pairs={{0,16},{4,20},{8,24},{12,28},{16,0},{20,4},{24,8},{28,12},{1,17},{... | collective-permute-start | bytes 442376 | tf_op jit(solution)/shard_map/ppermute | solution.py:376
  28.9 13.7 %collective-permute-start.13 = (bf16[512,256]{1,0:T(8,128)(2,1)S(1)}, bf16[512,256]{1,0:T(8,128)(2,1)S(1)}, u32[]{:S(2)}, u32[]{:S(2)}) collective-permute-start(bf16[512,256]{1,0:T(8,128)(2,1)S(1)} %get-tuple-element.25), channel_id=1, source_target_pairs={{0,1},{1,0},{2,3},{3,2},{4,5},{5,4},{6,7},{7,6},{8,9},{9,8},{10,11... | collective-permute-start | bytes 786440 | tf_op jit(solution)/shard_map/ppermute | solution.py:368
  31.6 11.0 %collective-permute-start.14 = (bf16[512,256]{1,0:T(8,128)(2,1)S(1)}, bf16[512,256]{1,0:T(8,128)(2,1)S(1)}, u32[]{:S(2)}, u32[]{:S(2)}) collective-permute-start(bf16[512,256]{1,0:T(8,128)(2,1)S(1)} %get-tuple-element.26), channel_id=1, source_target_pairs={{0,4},{1,2},{2,1},{3,7},{4,0},{5,6},{6,5},{7,3},{8,12},{9,10},{10,... | collective-permute-start | bytes 786440 | tf_op jit(solution)/shard_map/ppermute | solution.py:373
  31.6 11.0 %collective-permute-start.15 = (bf16[384,256]{1,0:T(8,128)(2,1)S(1)}, bf16[384,256]{1,0:T(8,128)(2,1)S(1)}, u32[]{:S(2)}, u32[]{:S(2)}) collective-permute-start(bf16[384,256]{1,0:T(8,128)(2,1)S(1)} %get-tuple-element.27), channel_id=1, source_target_pairs={{0,2},{3,1},{1,0},{2,3},{4,6},{7,5},{5,4},{6,7},{8,10},{11,9},{9,8... | collective-permute-start | bytes 589832 | tf_op jit(solution)/shard_map/ppermute | solution.py:368
  33.6 7.4 %collective-permute-start.18 = (bf16[576,128]{1,0:T(8,128)(2,1)S(1)}, bf16[576,128]{1,0:T(8,128)(2,1)S(1)}, u32[]{:S(2)}, u32[]{:S(2)}) collective-permute-start(bf16[576,128]{1,0:T(8,128)(2,1)S(1)} %get-tuple-element.28.refs_0_), channel_id=1, source_target_pairs={{0,24},{4,28},{8,16},{12,20},{16,8},{20,12},{24,0},{28,4},{1,25},{... | collective-permute-start | bytes 442376 | tf_op jit(solution)/shard_map/ppermute | solution.py:376
  35.1 7.4 %collective-permute-start.19 = (bf16[576,128]{1,0:T(8,128)(2,1)S(1)}, bf16[576,128]{1,0:T(8,128)(2,1)S(1)}, u32[]{:S(2)}, u32[]{:S(2)}) collective-permute-start(bf16[576,128]{1,0:T(8,128)(2,1)S(1)} %get-tuple-element.28.refs_0_), channel_id=1, source_target_pairs={{0,8},{4,12},{8,0},{12,4},{16,24},{20,28},{24,16},{28,20},{1,9},{5... | collective-permute-start | bytes 442376 | tf_op jit(solution)/shard_map/ppermute | solution.py:376
  41.0 2.2 %collective-permute-start.17 = (bf16[1152,128]{1,0:T(8,128)(2,1)S(1)}, bf16[1152,128]{1,0:T(8,128)(2,1)S(1)}, u32[]{:S(2)}, u32[]{:S(2)}) collective-permute-start(bf16[1152,128]{1,0:T(8,128)(2,1)S(1)} %shard_map.102.a_ref), channel_id=1, source_target_pairs={{0,4},{4,0},{8,12},{12,8},{16,20},{20,16},{24,28},{28,24},{1,5},{5... | collective-permute-start | bytes 884744 | tf_op jit(solution)/shard_map/ppermute | solution.py:376
  42.5 1.6 %collective-permute-start.20 = (bf16[1152,128]{1,0:T(8,128)(2,1)S(1)}, bf16[1152,128]{1,0:T(8,128)(2,1)S(1)}, u32[]{:S(2)}, u32[]{:S(2)}) collective-permute-start(bf16[1152,128]{1,0:T(8,128)(2,1)S(1)} %shard_map.103.c_ref), channel_id=1, source_target_pairs={{0,4},{4,0},{8,12},{12,8},{16,20},{20,16},{24,28},{28,24},{1,5},{5... | collective-permute-start | bytes 884744 | tf_op jit(solution)/shard_map/ppermute | solution.py:376
  44.8 1.2 %collective-permute-start.21 = (f32[8,128]{1,0:T(8,128)S(1)}, f32[8,128]{1,0:T(8,128)S(1)}, u32[]{:S(2)}, u32[]{:S(2)}) collective-permute-start(f32[8,128]{1,0:T(8,128)S(1)} %shard_map.104.o_ref), channel_id=1, source_target_pairs={{0,4},{1,2},{2,1},{3,7},{4,0},{5,6},{6,5},{7,3},{8,12},{9,10},{10,... | collective-permute-start | bytes 12296 | tf_op jit(solution)/shard_map/ppermute | solution.py:373
  46.0 5.8 %collective-permute-start.22 = (f32[8,128]{1,0:T(8,128)S(1)}, f32[8,128]{1,0:T(8,128)S(1)}, u32[]{:S(2)}, u32[]{:S(2)}) collective-permute-start(f32[8,128]{1,0:T(8,128)S(1)} %shard_map.105.j_ref), channel_id=1, source_target_pairs={{0,1},{1,0},{2,3},{3,2},{4,5},{5,4},{6,7},{7,6},{8,9},{9,8},{10,11... | collective-permute-start | bytes 12296 | tf_op jit(solution)/shard_map/ppermute | solution.py:368

commit v5 on v4

--- a/solution.py
+++ b/solution.py
@@ -267,16 +267,28 @@
     )
 
 
-def token_grads(parts, pieces, first, side_in, targets, lengths):
+def join(first, rest):
+    high = first.shape[0]
+    shape = (high + rest.shape[0], first.shape[1])
+
+    def body(a_ref, b_ref, out_ref):
+        out_ref[:high, :] = a_ref[...]
+        out_ref[high:, :] = b_ref[...]
+
+    return call(body, arr(shape, bf16), (first, rest), 1 << 30)
+
+
+def token_grads(parts, pieces, side_in, targets, lengths):
     vocab, length = pieces[0].shape
     rank = side_in.shape[0]
     step = vocab // parts
 
-    def body(k_ref, n_ref, c_ref, f_ref, l_ref, side_ref, t_ref, live_ref, out_ref):
+    def body(k_ref, f_ref, c_ref, n_ref, side_ref, t_ref, live_ref, out_ref):
         row = lax.axis_index("tensor") // 2
         own = lax.axis_index("dp") % parts
-        total = k_ref[...] + n_ref[...].astype(f32) + c_ref[...].astype(f32)
-        total += jnp.concatenate([l_ref[...], f_ref[...]], axis=0).astype(f32)
+        total = k_ref[...]
+        for ref in (f_ref, c_ref, n_ref):
+            total += ref[...].astype(f32)
         expo = jnp.exp(total)
         targets_here = jnp.where(row == 0, t_ref[0:1, :], t_ref[1:2, :])
         lengths_here = jnp.where(row == 0, live_ref[0:1, :], live_ref[1:2, :])
@@ -292,7 +304,7 @@
     return call(
         body,
         arr((2 * rank, vocab), bf16),
-        (*pieces, first, side_in, targets, spread),
+        (*pieces, side_in, targets, spread),
         1 << 34,
     )
 
@@ -391,14 +403,15 @@
     first = pass_on(send(first_logits(folded[0], folded[1], mixed), FAR))
     whole, side_in = gather_shares(across, cross(across), keep_side, block, step)
     keep, near_logits, other_logits, rest = logit_rows(folded, mixed, side_in, first)
-    pieces = (keep, send(near_logits, NEAR), cross(other_logits), send(rest, FAR))
+    far_logits = join(first, send(rest, FAR))
+    pieces = (keep, far_logits, cross(other_logits), send(near_logits, NEAR))
     queries = None
     if n_dp != parts:
         queries = lax.all_gather(whole[: 4 * block], "dp", axis=0)
     others = {s: swap(whole, "dp", s) for s in range(2, parts, 2)}
     pairs = stack((whole, others[4])), stack((others[6], others[2]))
     shares = [y for x in pairs for y in (x, swap(x, "dp", 1))]
-    joint = token_grads(parts, pieces, first, side_in, targets, lengths)
+    joint = token_grads(parts, pieces, side_in, targets, lengths)
     scores = row_scores(parts, joint, shares, queries)
     joined = join_rows(scores, cross(scores))
     return pick_rows(joined, send(joined, NEAR))

time: 52.6 us -> 53 us (level)
    pallas_call x16 -> x17, Pallas kernels: 11 us -> 11 us  [call(): pl.pallas_call(body, out_shape=outs, in_specs=in_specs or [VM] * len(args...]
where the time goes in v5:
time: 53 us; the launch traced here: 52.8 us
  starting transfers between devices  28.1 us (53%)
  waiting for transfers between devices  12 us (23%)
  Pallas kernels  11 us (21%)
  local copies, waits for them, and re-layouts  1.53 us (3%)
    ppermute x5, starting transfers between devices, send(): return lax.ppermute(x, 'tensor', pairs)  14.6 us
    ppermute x15, starting transfers between devices, swap(): lax.ppermute(x, axis, [(i, i ^ slot) for i in range(lax.axis_size(axis))])  13.3 us
    pallas_call x17, Pallas kernels, call(): pl.pallas_call(body, out_shape=outs, in_specs=in_specs or [VM] * len(args...  11 us
    ppermute x15, waiting for transfers between devices, swap(): lax.ppermute(x, axis, [(i, i ^ slot) for i in range(lax.axis_size(axis))])  9.33 us
    ppermute x5, waiting for transfers between devices, send(): return lax.ppermute(x, 'tensor', pairs)  1.59 us
    unnamed x8, local copies, waits for them, and re-layouts  1.46 us
  transfers between devices with their start and end apart: 23, of which 8 were waited for; matrix products, arithmetic and copies ran while one was open for 0% of the time, Pallas kernels for 17%

profile of v5, /device:TPU:0, one launch (start us, length us, event | category | flops | bytes accessed | tf_op | source)
XLA Modules:
  0.0 52.8 jit_solution(8514059552540782793)
XLA Ops:
  0.0 0.9 %shard_map.91.b_ref = bf16[64,1024]{1,0:T(8,128)(2,1)S(1)} custom-call(bf16[512,1024]{1,0:T(8,128)(2,1)} %e_ref.1), custom_call_target="tpu_custom_call" | custom-call | bytes 1048576 | tf_op jit(solution)/shard_map/pallas_call | solution.py:30
  0.9 4.1 %collective-permute-start = (bf16[64,1024]{1,0:T(8,128)(2,1)S(1)}, bf16[64,1024]{1,0:T(8,128)(2,1)S(1)}, u32[]{:S(2)}, u32[]{:S(2)}) collective-permute-start(bf16[64,1024]{1,0:T(8,128)(2,1)S(1)} %shard_map.91.b_ref), channel_id=1, source_target_pairs={{0,2},{1,3},{2,0},{3,1},{4,6},{5,7},{6,4},{7,5},{8,10},{9,11},{10,... | collective-permute-start | bytes 393224 | tf_op jit(solution)/shard_map/ppermute | solution.py:388
  5.0 1.6 %collective-permute-start.1 = (bf16[64,1024]{1,0:T(8,128)(2,1)S(1)}, bf16[64,1024]{1,0:T(8,128)(2,1)S(1)}, u32[]{:S(2)}, u32[]{:S(2)}) collective-permute-start(bf16[64,1024]{1,0:T(8,128)(2,1)S(1)} %shard_map.91.b_ref), channel_id=1, source_target_pairs={{0,1},{1,0},{2,3},{3,2},{4,5},{5,4},{6,7},{7,6},{8,9},{9,8},{10,11... | collective-permute-start | bytes 393224 | tf_op jit(solution)/shard_map/ppermute | solution.py:388
  6.6 0.8 %copy-done = bf16[16,1024]{1,0:T(8,128)(2,1)S(1)} copy-done((bf16[16,1024]{1,0:T(8,128)(2,1)S(1)}, bf16[16,1024]{1,0:T(8,128)(2,1)}, u32[]{:S(2)}) %copy-start) | copy-done | bytes 32792
  7.4 0.7 %copy-done.1 = bf16[3,1024]{1,0:T(4,128)(2,1)S(1)} copy-done((bf16[3,1024]{1,0:T(4,128)(2,1)S(1)}, bf16[3,1024]{1,0:T(4,128)(2,1)}, u32[]{:S(2)}) %copy-start.1) | copy-done | bytes 6168
  8.1 4.6 %shard_map.92 = (bf16[512,1024]{1,0:T(8,128)(2,1)S(1)}, bf16[704,128]{1,0:T(8,128)(2,1)S(1)}, f32[64,1024]{1,0:T(8,128)S(1)}, bf16[1024,4096]{1,0:T(8,128)(2,1)S(1)}) custom-call(bf16[2,256,1024]{2,1,0:T(8,128)(2,1)} %h_any.1, bf16[64,1024]{1,0:T(8,128)(2,1)} %bitcast.2, bf16[64,1024]{1,0:T(8,128)(2,1)} %bitcast.3, bf16[1024,4096]{1,0:T(8,128)(2,1)} %w_any.1, ...), custom_call_target="tpu_custom_call" | custom-call | flops 201326592 | bytes 9869312 | tf_op jit(solution)/shard_map/pallas_call | solution.py:30
  12.7 1.0 %collective-permute-start.10 = (bf16[704,128]{1,0:T(8,128)(2,1)S(1)}, bf16[704,128]{1,0:T(8,128)(2,1)S(1)}, u32[]{:S(2)}, u32[]{:S(2)}) collective-permute-start(bf16[704,128]{1,0:T(8,128)(2,1)S(1)} %get-tuple-element.20.o_ref), channel_id=1, source_target_pairs={{0,1},{1,0},{2,3},{3,2},{4,5},{5,4},{6,7},{7,6},{8,9},{9,8},{10,11... | collective-permute-start | bytes 540680 | tf_op jit(solution)/shard_map/ppermute | solution.py:380
  13.6 0.0 collective-permute-done.b_ref
  13.6 0.8 %shard_map.93.f_ref = f32[64,1024]{1,0:T(8,128)S(1)} custom-call(f32[64,1024]{1,0:T(8,128)S(1)} %get-tuple-element.17.f_ref, bf16[64,1024]{1,0:T(8,128)(2,1)S(1)} %collective-permute-done.b_ref, bf16[1024,4096]{1,0:T(8,128)(2,1)S(1)} %get-tuple-element.18.w_ref), custom_call_target="tpu_custom_call" | custom-call | flops 134217728 | bytes 8781824 | tf_op jit(solution)/shard_map/pallas_call | solution.py:30
  14.4 0.0 collective-permute-done.1.b_ref
  14.4 0.8 %shard_map.94.f_ref = f32[64,1024]{1,0:T(8,128)S(1)} custom-call(f32[64,1024]{1,0:T(8,128)S(1)} %shard_map.93.f_ref, bf16[64,1024]{1,0:T(8,128)(2,1)S(1)} %collective-permute-done.1.b_ref, bf16[1024,4096]{1,0:T(8,128)(2,1)S(1)} %get-tuple-element.18.w_ref), custom_call_target="tpu_custom_call" | custom-call | flops 134217728 | bytes 8781824 | tf_op jit(solution)/shard_map/pallas_call | solution.py:30
  15.2 0.3 collective-permute-done.2.b_ref
  15.4 0.8 %shard_map.95.a_ref.refs_3_ = bf16[64,1024]{1,0:T(8,128)(2,1)S(1)} custom-call(f32[64,1024]{1,0:T(8,128)S(1)} %shard_map.94.f_ref, bf16[64,1024]{1,0:T(8,128)(2,1)S(1)} %collective-permute-done.2.b_ref, bf16[1024,4096]{1,0:T(8,128)(2,1)S(1)} %get-tuple-element.18.w_ref), custom_call_target="tpu_custom_call" | custom-call | flops 134217728 | bytes 8781824 | tf_op jit(solution)/shard_map/pallas_call | solution.py:30
  16.2 0.0 copy-start.2
  16.2 0.1 collective-permute-start.9
  16.3 2.5 %collective-permute-start.3 = (bf16[64,1024]{1,0:T(8,128)(2,1)S(1)}, bf16[64,1024]{1,0:T(8,128)(2,1)S(1)}, u32[]{:S(2)}, u32[]{:S(2)}) collective-permute-start(bf16[64,1024]{1,0:T(8,128)(2,1)S(1)} %shard_map.95.a_ref.refs_3_), channel_id=1, source_target_pairs={{0,24},{4,28},{8,16},{12,20},{16,8},{20,12},{24,0},{28,4},{1,25},{... | collective-permute-start | bytes 393224 | tf_op jit(solution)/shard_map/ppermute | solution.py:388
  18.8 0.5 collective-permute-start.4
  19.3 0.5 %collective-permute-start.5 = (bf16[64,1024]{1,0:T(8,128)(2,1)S(1)}, bf16[64,1024]{1,0:T(8,128)(2,1)S(1)}, u32[]{:S(2)}, u32[]{:S(2)}) collective-permute-start(bf16[64,1024]{1,0:T(8,128)(2,1)S(1)} %shard_map.95.a_ref.refs_3_), channel_id=1, source_target_pairs={{0,8},{4,12},{8,0},{12,4},{16,24},{20,28},{24,16},{28,20},{1,9},{5... | collective-permute-start | bytes 393224 | tf_op jit(solution)/shard_map/ppermute | solution.py:388
  19.8 0.2 shard_map.96
  20.0 0.0 collective-permute-start.11
  20.0 0.0 collective-permute-done.9.b_ref.refs_7_
  20.0 0.3 shard_map.98
  20.3 4.2 %collective-permute-start.12 = (bf16[128,256]{1,0:T(8,128)(2,1)S(1)}, bf16[128,256]{1,0:T(8,128)(2,1)S(1)}, u32[]{:S(2)}, u32[]{:S(2)}) collective-permute-start(bf16[128,256]{1,0:T(8,128)(2,1)S(1)} %shard_map.98), channel_id=1, source_target_pairs={{0,2},{3,1},{1,0},{2,3},{4,6},{7,5},{5,4},{6,7},{8,10},{11,9},{9,8... | collective-permute-start | bytes 196616 | tf_op jit(solution)/shard_map/ppermute | solution.py:380
  24.6 0.0 collective-permute-done.3.refs_0_
  24.6 0.0 collective-permute-start.6
  24.6 1.3 %collective-permute-done.4.refs_1_ = bf16[64,1024]{1,0:T(8,128)(2,1)S(1)} collective-permute-done((bf16[64,1024]{1,0:T(8,128)(2,1)S(1)}, bf16[64,1024]{1,0:T(8,128)(2,1)S(1)}, u32[]{:S(2)}, u32[]{:S(2)}) %collective-permute-start.4) | collective-permute-done | bytes 131104 | tf_op jit(solution)/shard_map/ppermute | solution.py:388
  25.9 0.0 collective-permute-start.7
  25.9 0.1 collective-permute-done.5.refs_2_
  26.0 0.4 collective-permute-start.8
  26.4 0.2 shard_map.97
  26.6 1.5 %collective-permute-start.16 = (bf16[576,128]{1,0:T(8,128)(2,1)S(1)}, bf16[576,128]{1,0:T(8,128)(2,1)S(1)}, u32[]{:S(2)}, u32[]{:S(2)}) collective-permute-start(bf16[576,128]{1,0:T(8,128)(2,1)S(1)} %get-tuple-element.28.refs_0_), channel_id=1, source_target_pairs={{0,16},{4,20},{8,24},{12,28},{16,0},{20,4},{24,8},{28,12},{1,17},{... | collective-permute-start | bytes 442376 | tf_op jit(solution)/shard_map/ppermute | solution.py:388
  28.2 0.8 %shard_map.100 = (f32[512,256]{1,0:T(8,128)S(1)}, bf16[512,256]{1,0:T(8,128)(2,1)S(1)}, bf16[512,256]{1,0:T(8,128)(2,1)S(1)}, bf16[384,256]{1,0:T(8,128)(2,1)S(1)}) custom-call(bf16[64,1024]{1,0:T(8,128)(2,1)S(1)} %collective-permute-done.3.refs_0_, bf16[64,1024]{1,0:T(8,128)(2,1)S(1)} %collective-permute-done.4.refs_1_, ...), custom_call_target="tpu_custom_call" | custom-call | flops 536870912 | bytes 2228224 | tf_op jit(solution)/shard_map/pallas_call | solution.py:30
  28.9 4.6 %collective-permute-start.13 = (bf16[384,256]{1,0:T(8,128)(2,1)S(1)}, bf16[384,256]{1,0:T(8,128)(2,1)S(1)}, u32[]{:S(2)}, u32[]{:S(2)}) collective-permute-start(bf16[384,256]{1,0:T(8,128)(2,1)S(1)} %get-tuple-element.25), channel_id=1, source_target_pairs={{0,2},{3,1},{1,0},{2,3},{4,6},{7,5},{5,4},{6,7},{8,10},{11,9},{9,8... | collective-permute-start | bytes 589832 | tf_op jit(solution)/shard_map/ppermute | solution.py:380
  33.5 0.6 %collective-permute-start.15 = (bf16[512,256]{1,0:T(8,128)(2,1)S(1)}, bf16[512,256]{1,0:T(8,128)(2,1)S(1)}, u32[]{:S(2)}, u32[]{:S(2)}) collective-permute-start(bf16[512,256]{1,0:T(8,128)(2,1)S(1)} %get-tuple-element.27), channel_id=1, source_target_pairs={{0,1},{1,0},{2,3},{3,2},{4,5},{5,4},{6,7},{7,6},{8,9},{9,8},{10,11... | collective-permute-start | bytes 786440 | tf_op jit(solution)/shard_map/ppermute | solution.py:380
  34.1 1.4 %collective-permute-start.18 = (bf16[576,128]{1,0:T(8,128)(2,1)S(1)}, bf16[576,128]{1,0:T(8,128)(2,1)S(1)}, u32[]{:S(2)}, u32[]{:S(2)}) collective-permute-start(bf16[576,128]{1,0:T(8,128)(2,1)S(1)} %get-tuple-element.28.refs_0_), channel_id=1, source_target_pairs={{0,24},{4,28},{8,16},{12,20},{16,8},{20,12},{24,0},{28,4},{1,25},{... | collective-permute-start | bytes 442376 | tf_op jit(solution)/shard_map/ppermute | solution.py:388
  35.6 0.5 %collective-permute-start.19 = (bf16[576,128]{1,0:T(8,128)(2,1)S(1)}, bf16[576,128]{1,0:T(8,128)(2,1)S(1)}, u32[]{:S(2)}, u32[]{:S(2)}) collective-permute-start(bf16[576,128]{1,0:T(8,128)(2,1)S(1)} %get-tuple-element.28.refs_0_), channel_id=1, source_target_pairs={{0,8},{4,12},{8,0},{12,4},{16,24},{20,28},{24,16},{28,20},{1,9},{5... | collective-permute-start | bytes 442376 | tf_op jit(solution)/shard_map/ppermute | solution.py:388
  36.1 5.6 %collective-permute-done.18.refs_0_ = bf16[576,128]{1,0:T(8,128)(2,1)S(1)} collective-permute-done((bf16[576,128]{1,0:T(8,128)(2,1)S(1)}, bf16[576,128]{1,0:T(8,128)(2,1)S(1)}, u32[]{:S(2)}, u32[]{:S(2)}) %collective-permute-start.18) | collective-permute-done | bytes 147488 | tf_op jit(solution)/shard_map/ppermute | solution.py:388
  41.8 1.1 %collective-permute-done.19.refs_1_ = bf16[576,128]{1,0:T(8,128)(2,1)S(1)} collective-permute-done((bf16[576,128]{1,0:T(8,128)(2,1)S(1)}, bf16[576,128]{1,0:T(8,128)(2,1)S(1)}, u32[]{:S(2)}, u32[]{:S(2)}) %collective-permute-start.19) | collective-permute-done | bytes 147488 | tf_op jit(solution)/shard_map/ppermute | solution.py:388
  42.9 0.1 collective-permute-start.20
  43.0 0.1 broadcast_in_dim.2.live_ref
  43.1 0.5 shard_map.102.j_ref
  43.6 0.9 %collective-permute-done.20.d_ref = bf16[1152,128]{1,0:T(8,128)(2,1)S(1)} collective-permute-done((bf16[1152,128]{1,0:T(8,128)(2,1)S(1)}, bf16[1152,128]{1,0:T(8,128)(2,1)S(1)}, u32[]{:S(2)}, u32[]{:S(2)}) %collective-permute-start.20) | collective-permute-done | bytes 294944 | tf_op jit(solution)/shard_map/ppermute | solution.py:388
  44.5 0.7 %shard_map.105.o_ref = f32[8,128]{1,0:T(8,128)S(1)} custom-call(bf16[128,512]{1,0:T(8,128)(2,1)S(1)} %shard_map.102.j_ref, bf16[1152,128]{1,0:T(8,128)(2,1)S(1)} %shard_map.103.a_ref, bf16[1152,128]{1,0:T(8,128)(2,1)S(1)} %collective-permute-done.17.b_ref, bf16[1152,128]{1,0:T(8,128)(2,1)S(1)} %shard_map.104.c_ref, ...), custom_call_target="tpu_custom_call" | custom-call | flops 4194304 | bytes 1310720 | tf_op jit(solution)/shard_map/pallas_call | solution.py:30
  45.2 0.2 collective-permute-start.21
  45.4 1.0 %collective-permute-done.21.c_ref = f32[8,128]{1,0:T(8,128)S(1)} collective-permute-done((f32[8,128]{1,0:T(8,128)S(1)}, f32[8,128]{1,0:T(8,128)S(1)}, u32[]{:S(2)}, u32[]{:S(2)}) %collective-permute-start.21) | collective-permute-done | bytes 4128 | tf_op jit(solution)/shard_map/ppermute | solution.py:385
  46.4 4.2 %collective-permute-start.22 = (f32[8,128]{1,0:T(8,128)S(1)}, f32[8,128]{1,0:T(8,128)S(1)}, u32[]{:S(2)}, u32[]{:S(2)}) collective-permute-start(f32[8,128]{1,0:T(8,128)S(1)} %shard_map.106.j_ref), channel_id=1, source_target_pairs={{0,1},{1,0},{2,3},{3,2},{4,5},{5,4},{6,7},{7,6},{8,9},{9,8},{10,11... | collective-permute-start | bytes 12296 | tf_op jit(solution)/shard_map/ppermute | solution.py:380
  50.6 1.6 %collective-permute-done.22.c_ref = f32[8,128]{1,0:T(8,128)S(1)} collective-permute-done((f32[8,128]{1,0:T(8,128)S(1)}, f32[8,128]{1,0:T(8,128)S(1)}, u32[]{:S(2)}, u32[]{:S(2)}) %collective-permute-start.22) | collective-permute-done | bytes 4128 | tf_op jit(solution)/shard_map/ppermute | solution.py:380
  52.2 0.6 %shard_map.107 = f32[2,128]{1,0:T(2,128)} custom-call(f32[8,128]{1,0:T(8,128)S(1)} %shard_map.106.j_ref, f32[8,128]{1,0:T(8,128)S(1)} %collective-permute-done.22.c_ref), custom_call_target="tpu_custom_call" | custom-call | bytes 8192 | tf_op jit(solution)/shard_map/pallas_call | solution.py:30
  (24 shorter events, 0.1 us)
Async XLA Ops:
  0.9 12.7 %collective-permute-start = (bf16[64,1024]{1,0:T(8,128)(2,1)S(1)}, bf16[64,1024]{1,0:T(8,128)(2,1)S(1)}, u32[]{:S(2)}, u32[]{:S(2)}) collective-permute-start(bf16[64,1024]{1,0:T(8,128)(2,1)S(1)} %shard_map.91.b_ref), channel_id=1, source_target_pairs={{0,2},{1,3},{2,0},{3,1},{4,6},{5,7},{6,4},{7,5},{8,10},{9,11},{10,... | collective-permute-start | bytes 393224 | tf_op jit(solution)/shard_map/ppermute | solution.py:388
  5.0 9.4 %collective-permute-start.1 = (bf16[64,1024]{1,0:T(8,128)(2,1)S(1)}, bf16[64,1024]{1,0:T(8,128)(2,1)S(1)}, u32[]{:S(2)}, u32[]{:S(2)}) collective-permute-start(bf16[64,1024]{1,0:T(8,128)(2,1)S(1)} %shard_map.91.b_ref), channel_id=1, source_target_pairs={{0,1},{1,0},{2,3},{3,2},{4,5},{5,4},{6,7},{7,6},{8,9},{9,8},{10,11... | collective-permute-start | bytes 393224 | tf_op jit(solution)/shard_map/ppermute | solution.py:388
  6.6 8.8 %collective-permute-start.2 = (bf16[64,1024]{1,0:T(8,128)(2,1)S(1)}, bf16[64,1024]{1,0:T(8,128)(2,1)S(1)}, u32[]{:S(2)}, u32[]{:S(2)}) collective-permute-start(bf16[64,1024]{1,0:T(8,128)(2,1)S(1)} %shard_map.91.b_ref), channel_id=1, source_target_pairs={{0,3},{1,2},{2,1},{3,0},{4,7},{5,6},{6,5},{7,4},{8,11},{9,10},{10,... | collective-permute-start | bytes 393224 | tf_op jit(solution)/shard_map/ppermute | solution.py:388
  6.6 0.8 %copy-start = (bf16[16,1024]{1,0:T(8,128)(2,1)S(1)}, bf16[16,1024]{1,0:T(8,128)(2,1)}, u32[]{:S(2)}) copy-start(bf16[16,1024]{1,0:T(8,128)(2,1)} %q_ref.1) | copy-start | bytes 98308
  7.4 0.7 %copy-start.1 = (bf16[3,1024]{1,0:T(4,128)(2,1)S(1)}, bf16[3,1024]{1,0:T(4,128)(2,1)}, u32[]{:S(2)}) copy-start(bf16[3,1024]{1,0:T(4,128)(2,1)} %c_ref.1) | copy-start | bytes 18436
  12.7 7.2 %collective-permute-start.10 = (bf16[704,128]{1,0:T(8,128)(2,1)S(1)}, bf16[704,128]{1,0:T(8,128)(2,1)S(1)}, u32[]{:S(2)}, u32[]{:S(2)}) collective-permute-start(bf16[704,128]{1,0:T(8,128)(2,1)S(1)} %get-tuple-element.20.o_ref), channel_id=1, source_target_pairs={{0,1},{1,0},{2,3},{3,2},{4,5},{5,4},{6,7},{7,6},{8,9},{9,8},{10,11... | collective-permute-start | bytes 540680 | tf_op jit(solution)/shard_map/ppermute | solution.py:380
  16.2 26.8 %copy-start.3 = (s32[2]{0:T(128)S(1)}, s32[2]{0:T(128)}, u32[]{:S(2)}) copy-start(s32[2]{0:T(128)} %param.11) | copy-start | bytes 28
  16.2 26.9 %copy-start.2 = (s32[2,256]{1,0:T(2,128)S(1)}, s32[2,256]{1,0:T(2,128)}, u32[]{:S(2)}) copy-start(s32[2,256]{1,0:T(2,128)} %t_ref.1) | copy-start | bytes 6148
  16.2 3.8 %collective-permute-start.9 = (bf16[64,1024]{1,0:T(8,128)(2,1)S(1)}, bf16[64,1024]{1,0:T(8,128)(2,1)S(1)}, u32[]{:S(2)}, u32[]{:S(2)}) collective-permute-start(bf16[64,1024]{1,0:T(8,128)(2,1)S(1)} %shard_map.95.a_ref.refs_3_), channel_id=1, source_target_pairs={{0,4},{4,0},{8,12},{12,8},{16,20},{20,16},{24,28},{28,24},{1,5},{5... | collective-permute-start | bytes 393224 | tf_op jit(solution)/shard_map/ppermute | solution.py:388
  16.3 8.3 %collective-permute-start.3 = (bf16[64,1024]{1,0:T(8,128)(2,1)S(1)}, bf16[64,1024]{1,0:T(8,128)(2,1)S(1)}, u32[]{:S(2)}, u32[]{:S(2)}) collective-permute-start(bf16[64,1024]{1,0:T(8,128)(2,1)S(1)} %shard_map.95.a_ref.refs_3_), channel_id=1, source_target_pairs={{0,24},{4,28},{8,16},{12,20},{16,8},{20,12},{24,0},{28,4},{1,25},{... | collective-permute-start | bytes 393224 | tf_op jit(solution)/shard_map/ppermute | solution.py:388
  18.8 7.1 %collective-permute-start.4 = (bf16[64,1024]{1,0:T(8,128)(2,1)S(1)}, bf16[64,1024]{1,0:T(8,128)(2,1)S(1)}, u32[]{:S(2)}, u32[]{:S(2)}) collective-permute-start(bf16[64,1024]{1,0:T(8,128)(2,1)S(1)} %shard_map.95.a_ref.refs_3_), channel_id=1, source_target_pairs={{0,16},{4,20},{8,24},{12,28},{16,0},{20,4},{24,8},{28,12},{1,17},{... | collective-permute-start | bytes 393224 | tf_op jit(solution)/shard_map/ppermute | solution.py:388
  19.3 6.7 %collective-permute-start.5 = (bf16[64,1024]{1,0:T(8,128)(2,1)S(1)}, bf16[64,1024]{1,0:T(8,128)(2,1)S(1)}, u32[]{:S(2)}, u32[]{:S(2)}) collective-permute-start(bf16[64,1024]{1,0:T(8,128)(2,1)S(1)} %shard_map.95.a_ref.refs_3_), channel_id=1, source_target_pairs={{0,8},{4,12},{8,0},{12,4},{16,24},{20,28},{24,16},{28,20},{1,9},{5... | collective-permute-start | bytes 393224 | tf_op jit(solution)/shard_map/ppermute | solution.py:388
  20.0 6.4 %collective-permute-start.11 = (bf16[576,128]{1,0:T(8,128)(2,1)S(1)}, bf16[576,128]{1,0:T(8,128)(2,1)S(1)}, u32[]{:S(2)}, u32[]{:S(2)}) collective-permute-start(bf16[576,128]{1,0:T(8,128)(2,1)S(1)} %get-tuple-element.21.o_ref), channel_id=1, source_target_pairs={{0,4},{1,2},{2,1},{3,7},{4,0},{5,6},{6,5},{7,3},{8,12},{9,10},{10,... | collective-permute-start | bytes 442376 | tf_op jit(solution)/shard_map/ppermute | solution.py:385
  20.3 7.8 %collective-permute-start.12 = (bf16[128,256]{1,0:T(8,128)(2,1)S(1)}, bf16[128,256]{1,0:T(8,128)(2,1)S(1)}, u32[]{:S(2)}, u32[]{:S(2)}) collective-permute-start(bf16[128,256]{1,0:T(8,128)(2,1)S(1)} %shard_map.98), channel_id=1, source_target_pairs={{0,2},{3,1},{1,0},{2,3},{4,6},{7,5},{5,4},{6,7},{8,10},{11,9},{9,8... | collective-permute-start | bytes 196616 | tf_op jit(solution)/shard_map/ppermute | solution.py:380
  24.6 3.6 %collective-permute-start.6 = (bf16[64,1024]{1,0:T(8,128)(2,1)S(1)}, bf16[64,1024]{1,0:T(8,128)(2,1)S(1)}, u32[]{:S(2)}, u32[]{:S(2)}) collective-permute-start(bf16[64,1024]{1,0:T(8,128)(2,1)S(1)} %collective-permute-done.3.refs_0_), channel_id=1, source_target_pairs={{0,4},{4,0},{8,12},{12,8},{16,20},{20,16},{24,28},{28,24},{1,5},{5... | collective-permute-start | bytes 393224 | tf_op jit(solution)/shard_map/ppermute | solution.py:388
  25.9 2.2 %collective-permute-start.7 = (bf16[64,1024]{1,0:T(8,128)(2,1)S(1)}, bf16[64,1024]{1,0:T(8,128)(2,1)S(1)}, u32[]{:S(2)}, u32[]{:S(2)}) collective-permute-start(bf16[64,1024]{1,0:T(8,128)(2,1)S(1)} %collective-permute-done.4.refs_1_), channel_id=1, source_target_pairs={{0,4},{4,0},{8,12},{12,8},{16,20},{20,16},{24,28},{28,24},{1,5},{5... | collective-permute-start | bytes 393224 | tf_op jit(solution)/shard_map/ppermute | solution.py:388
  26.0 2.1 %collective-permute-start.8 = (bf16[64,1024]{1,0:T(8,128)(2,1)S(1)}, bf16[64,1024]{1,0:T(8,128)(2,1)S(1)}, u32[]{:S(2)}, u32[]{:S(2)}) collective-permute-start(bf16[64,1024]{1,0:T(8,128)(2,1)S(1)} %collective-permute-done.5.refs_2_), channel_id=1, source_target_pairs={{0,4},{4,0},{8,12},{12,8},{16,20},{20,16},{24,28},{28,24},{1,5},{5... | collective-permute-start | bytes 393224 | tf_op jit(solution)/shard_map/ppermute | solution.py:388
  26.6 9.0 %collective-permute-start.16 = (bf16[576,128]{1,0:T(8,128)(2,1)S(1)}, bf16[576,128]{1,0:T(8,128)(2,1)S(1)}, u32[]{:S(2)}, u32[]{:S(2)}) collective-permute-start(bf16[576,128]{1,0:T(8,128)(2,1)S(1)} %get-tuple-element.28.refs_0_), channel_id=1, source_target_pairs={{0,16},{4,20},{8,24},{12,28},{16,0},{20,4},{24,8},{28,12},{1,17},{... | collective-permute-start | bytes 442376 | tf_op jit(solution)/shard_map/ppermute | solution.py:388
  28.9 14.0 %collective-permute-start.13 = (bf16[384,256]{1,0:T(8,128)(2,1)S(1)}, bf16[384,256]{1,0:T(8,128)(2,1)S(1)}, u32[]{:S(2)}, u32[]{:S(2)}) collective-permute-start(bf16[384,256]{1,0:T(8,128)(2,1)S(1)} %get-tuple-element.25), channel_id=1, source_target_pairs={{0,2},{3,1},{1,0},{2,3},{4,6},{7,5},{5,4},{6,7},{8,10},{11,9},{9,8... | collective-permute-start | bytes 589832 | tf_op jit(solution)/shard_map/ppermute | solution.py:380
  33.5 9.5 %collective-permute-start.14 = (bf16[512,256]{1,0:T(8,128)(2,1)S(1)}, bf16[512,256]{1,0:T(8,128)(2,1)S(1)}, u32[]{:S(2)}, u32[]{:S(2)}) collective-permute-start(bf16[512,256]{1,0:T(8,128)(2,1)S(1)} %get-tuple-element.26), channel_id=1, source_target_pairs={{0,4},{1,2},{2,1},{3,7},{4,0},{5,6},{6,5},{7,3},{8,12},{9,10},{10,... | collective-permute-start | bytes 786440 | tf_op jit(solution)/shard_map/ppermute | solution.py:385
  33.5 9.5 %collective-permute-start.15 = (bf16[512,256]{1,0:T(8,128)(2,1)S(1)}, bf16[512,256]{1,0:T(8,128)(2,1)S(1)}, u32[]{:S(2)}, u32[]{:S(2)}) collective-permute-start(bf16[512,256]{1,0:T(8,128)(2,1)S(1)} %get-tuple-element.27), channel_id=1, source_target_pairs={{0,1},{1,0},{2,3},{3,2},{4,5},{5,4},{6,7},{7,6},{8,9},{9,8},{10,11... | collective-permute-start | bytes 786440 | tf_op jit(solution)/shard_map/ppermute | solution.py:380
  34.1 7.6 %collective-permute-start.18 = (bf16[576,128]{1,0:T(8,128)(2,1)S(1)}, bf16[576,128]{1,0:T(8,128)(2,1)S(1)}, u32[]{:S(2)}, u32[]{:S(2)}) collective-permute-start(bf16[576,128]{1,0:T(8,128)(2,1)S(1)} %get-tuple-element.28.refs_0_), channel_id=1, source_target_pairs={{0,24},{4,28},{8,16},{12,20},{16,8},{20,12},{24,0},{28,4},{1,25},{... | collective-permute-start | bytes 442376 | tf_op jit(solution)/shard_map/ppermute | solution.py:388
  35.6 7.3 %collective-permute-start.19 = (bf16[576,128]{1,0:T(8,128)(2,1)S(1)}, bf16[576,128]{1,0:T(8,128)(2,1)S(1)}, u32[]{:S(2)}, u32[]{:S(2)}) collective-permute-start(bf16[576,128]{1,0:T(8,128)(2,1)S(1)} %get-tuple-element.28.refs_0_), channel_id=1, source_target_pairs={{0,8},{4,12},{8,0},{12,4},{16,24},{20,28},{24,16},{28,20},{1,9},{5... | collective-permute-start | bytes 442376 | tf_op jit(solution)/shard_map/ppermute | solution.py:388
  41.8 1.8 %collective-permute-start.17 = (bf16[1152,128]{1,0:T(8,128)(2,1)S(1)}, bf16[1152,128]{1,0:T(8,128)(2,1)S(1)}, u32[]{:S(2)}, u32[]{:S(2)}) collective-permute-start(bf16[1152,128]{1,0:T(8,128)(2,1)S(1)} %shard_map.103.a_ref), channel_id=1, source_target_pairs={{0,4},{4,0},{8,12},{12,8},{16,20},{20,16},{24,28},{28,24},{1,5},{5... | collective-permute-start | bytes 884744 | tf_op jit(solution)/shard_map/ppermute | solution.py:388
  42.9 1.6 %collective-permute-start.20 = (bf16[1152,128]{1,0:T(8,128)(2,1)S(1)}, bf16[1152,128]{1,0:T(8,128)(2,1)S(1)}, u32[]{:S(2)}, u32[]{:S(2)}) collective-permute-start(bf16[1152,128]{1,0:T(8,128)(2,1)S(1)} %shard_map.104.c_ref), channel_id=1, source_target_pairs={{0,4},{4,0},{8,12},{12,8},{16,20},{20,16},{24,28},{28,24},{1,5},{5... | collective-permute-start | bytes 884744 | tf_op jit(solution)/shard_map/ppermute | solution.py:388
  45.2 1.2 %collective-permute-start.21 = (f32[8,128]{1,0:T(8,128)S(1)}, f32[8,128]{1,0:T(8,128)S(1)}, u32[]{:S(2)}, u32[]{:S(2)}) collective-permute-start(f32[8,128]{1,0:T(8,128)S(1)} %shard_map.105.o_ref), channel_id=1, source_target_pairs={{0,4},{1,2},{2,1},{3,7},{4,0},{5,6},{6,5},{7,3},{8,12},{9,10},{10,... | collective-permute-start | bytes 12296 | tf_op jit(solution)/shard_map/ppermute | solution.py:385
  46.4 5.8 %collective-permute-start.22 = (f32[8,128]{1,0:T(8,128)S(1)}, f32[8,128]{1,0:T(8,128)S(1)}, u32[]{:S(2)}, u32[]{:S(2)}) collective-permute-start(f32[8,128]{1,0:T(8,128)S(1)} %shard_map.106.j_ref), channel_id=1, source_target_pairs={{0,1},{1,0},{2,3},{3,2},{4,5},{5,4},{6,7},{7,6},{8,9},{9,8},{10,11... | collective-permute-start | bytes 12296 | tf_op jit(solution)/shard_map/ppermute | solution.py:380

commit v6 on v4

--- a/solution.py
+++ b/solution.py
@@ -106,8 +106,8 @@
             hold[k] = side[:, k * wide : (k + 1) * wide]
         for k in range(tokens // wide):
             pair = [hold[k, pl.ds(odd, rank // 2, stride=2), :] for odd in (0, 1)]
-            begin = side_begin + k * wide
-            out_ref[begin : begin + wide, :] = split2(jnp.concatenate(pair, axis=0), 0)
+            begin = side_begin + k * rank
+            out_ref[begin : begin + rank, :] = jnp.concatenate(pair, axis=0).astype(bf16)
         for k in range(lines):
             out_ref[k * q_rows : (k + 1) * q_rows, :] = q_ref[:, k * wide : (k + 1) * wide]
         copies[2].wait()
@@ -120,7 +120,7 @@
         body,
         (
             arr((tokens, width), bf16),
-            arr((side_begin + tokens, wide), bf16),
+            arr((side_begin + tokens // wide * rank, wide), bf16),
             arr((step, width), f32),
             pltpu.VMEM(proj_weight.shape, bf16),
         ),
@@ -157,6 +157,7 @@
 def relay_shares(own, near_by, block, step, half):
     wide = own.shape[1]
     begin = block + step
+    rank = wide // 2
     parts = half // wide
 
     def body(o_ref, n_ref, out_ref, keep_ref):
@@ -166,15 +167,20 @@
         u = o_ref[block:begin, :].astype(f32) + n_ref[block:begin, :].astype(f32)
         out_ref[2 * block : 2 * block + step, :] = split2(u[:, : wide // 2] + u[:, wide // 2 :], 1)
         for k in range(parts):
-            at = [pl.ds(pl.multiple_of(begin + (r * parts + k) * wide, wide // 2), wide) for r in (row, 1 - row)]
-            mine, other = [halve(o_ref[c, :].astype(f32) + n_ref[c, :].astype(f32)) for c in at]
+            mine, other = [
+                o_ref[at, :].astype(f32) + n_ref[at, :].astype(f32)
+                for at in [
+                    pl.ds(pl.multiple_of(begin + (r * parts + k) * rank, rank), rank)
+                    for r in (row, 1 - row)
+                ]
+            ]
             keep_ref[:, k * wide : (k + 1) * wide] = mine
-            place = 2 * block + step + k * wide
-            out_ref[place : place + wide, :] = split2(other, 0)
-
-    return call(
-        body,
-        (arr((2 * block + step + half, wide), bf16), arr((wide // 2, half), f32)),
+            place = 2 * block + step + k * rank
+            out_ref[place : place + rank, :] = other.astype(bf16)
+
+    return call(
+        body,
+        (arr((2 * block + step + parts * rank, wide), bf16), arr((rank, half), f32)),
         (own, near_by),
     )
 
@@ -210,8 +216,8 @@
         out_ref[4 * block :, :] = split2(u[:, : wide // 2] + u[:, wide // 2 :], 1)
         for k in range(parts):
             cols = slice(k * wide, (k + 1) * wide)
-            at = begin + step + k * wide
-            side_ref[:, cols] = k_ref[:, cols] + halve(c_ref[at : at + wide, :].astype(f32))
+            at = begin + step + k * (wide // 2)
+            side_ref[:, cols] = k_ref[:, cols] + c_ref[at : at + wide // 2, :].astype(f32)
 
     return call(
         body,

time: 52.6 us -> 52.6 us (level)
  no operation moved by 1% of the time
where the time goes in v6:
time: 52.6 us; the launch traced here: 52.4 us
  starting transfers between devices  27.6 us (52%)
  waiting for transfers between devices  12.1 us (23%)
  Pallas kernels  11 us (21%)
  local copies, waits for them, and re-layouts  1.53 us (3%)
    ppermute x5, starting transfers between devices, send(): return lax.ppermute(x, 'tensor', pairs)  13.7 us
    ppermute x15, starting transfers between devices, swap(): lax.ppermute(x, axis, [(i, i ^ slot) for i in range(lax.axis_size(axis))])  13.7 us
    pallas_call x16, Pallas kernels, call(): pl.pallas_call(body, out_shape=outs, in_specs=in_specs or [VM] * len(args...  11 us
    ppermute x15, waiting for transfers between devices, swap(): lax.ppermute(x, axis, [(i, i ^ slot) for i in range(lax.axis_size(axis))])  9.43 us
    ppermute x5, waiting for transfers between devices, send(): return lax.ppermute(x, 'tensor', pairs)  1.59 us
    unnamed x8, local copies, waits for them, and re-layouts  1.46 us
  transfers between devices with their start and end apart: 23, of which 8 were waited for; matrix products, arithmetic and copies ran while one was open for 0% of the time, Pallas kernels for 17%

profile of v6, /device:TPU:0, one launch (start us, length us, event | category | flops | bytes accessed | tf_op | source)
XLA Modules:
  0.0 52.4 jit_solution(2348183143495834377)
XLA Ops:
  0.0 0.9 %shard_map.91.b_ref = bf16[64,1024]{1,0:T(8,128)(2,1)S(1)} custom-call(bf16[512,1024]{1,0:T(8,128)(2,1)} %e_ref.1), custom_call_target="tpu_custom_call" | custom-call | bytes 1048576 | tf_op jit(solution)/shard_map/pallas_call | solution.py:30
  0.9 4.1 %collective-permute-start = (bf16[64,1024]{1,0:T(8,128)(2,1)S(1)}, bf16[64,1024]{1,0:T(8,128)(2,1)S(1)}, u32[]{:S(2)}, u32[]{:S(2)}) collective-permute-start(bf16[64,1024]{1,0:T(8,128)(2,1)S(1)} %shard_map.91.b_ref), channel_id=1, source_target_pairs={{0,2},{1,3},{2,0},{3,1},{4,6},{5,7},{6,4},{7,5},{8,10},{9,11},{10,... | collective-permute-start | bytes 393224 | tf_op jit(solution)/shard_map/ppermute | solution.py:382
  5.0 1.6 %collective-permute-start.1 = (bf16[64,1024]{1,0:T(8,128)(2,1)S(1)}, bf16[64,1024]{1,0:T(8,128)(2,1)S(1)}, u32[]{:S(2)}, u32[]{:S(2)}) collective-permute-start(bf16[64,1024]{1,0:T(8,128)(2,1)S(1)} %shard_map.91.b_ref), channel_id=1, source_target_pairs={{0,1},{1,0},{2,3},{3,2},{4,5},{5,4},{6,7},{7,6},{8,9},{9,8},{10,11... | collective-permute-start | bytes 393224 | tf_op jit(solution)/shard_map/ppermute | solution.py:382
  6.6 0.0 collective-permute-start.2
  6.6 0.8 %copy-done = bf16[16,1024]{1,0:T(8,128)(2,1)S(1)} copy-done((bf16[16,1024]{1,0:T(8,128)(2,1)S(1)}, bf16[16,1024]{1,0:T(8,128)(2,1)}, u32[]{:S(2)}) %copy-start) | copy-done | bytes 32792
  7.4 0.7 %copy-done.1 = bf16[3,1024]{1,0:T(4,128)(2,1)S(1)} copy-done((bf16[3,1024]{1,0:T(4,128)(2,1)S(1)}, bf16[3,1024]{1,0:T(4,128)(2,1)}, u32[]{:S(2)}) %copy-start.1) | copy-done | bytes 6168
  8.1 4.6 %shard_map.92 = (bf16[512,1024]{1,0:T(8,128)(2,1)S(1)}, bf16[448,128]{1,0:T(8,128)(2,1)S(1)}, f32[64,1024]{1,0:T(8,128)S(1)}, bf16[1024,4096]{1,0:T(8,128)(2,1)S(1)}) custom-call(bf16[2,256,1024]{2,1,0:T(8,128)(2,1)} %h_any.1, bf16[64,1024]{1,0:T(8,128)(2,1)} %bitcast.2, bf16[64,1024]{1,0:T(8,128)(2,1)} %bitcast.3, bf16[1024,4096]{1,0:T(8,128)(2,1)} %w_any.1, ...), custom_call_target="tpu_custom_call" | custom-call | flops 201326592 | bytes 9869312 | tf_op jit(solution)/shard_map/pallas_call | solution.py:30
  12.7 1.0 %collective-permute-start.10 = (bf16[448,128]{1,0:T(8,128)(2,1)S(1)}, bf16[448,128]{1,0:T(8,128)(2,1)S(1)}, u32[]{:S(2)}, u32[]{:S(2)}) collective-permute-start(bf16[448,128]{1,0:T(8,128)(2,1)S(1)} %get-tuple-element.20.o_ref), channel_id=1, source_target_pairs={{0,1},{1,0},{2,3},{3,2},{4,5},{5,4},{6,7},{7,6},{8,9},{9,8},{10,11... | collective-permute-start | bytes 344072 | tf_op jit(solution)/shard_map/ppermute | solution.py:374
  13.6 0.0 collective-permute-done.b_ref
  13.6 0.8 %shard_map.93.f_ref = f32[64,1024]{1,0:T(8,128)S(1)} custom-call(f32[64,1024]{1,0:T(8,128)S(1)} %get-tuple-element.17.f_ref, bf16[64,1024]{1,0:T(8,128)(2,1)S(1)} %collective-permute-done.b_ref, bf16[1024,4096]{1,0:T(8,128)(2,1)S(1)} %get-tuple-element.18.w_ref), custom_call_target="tpu_custom_call" | custom-call | flops 134217728 | bytes 8781824 | tf_op jit(solution)/shard_map/pallas_call | solution.py:30
  14.4 0.0 collective-permute-done.1.b_ref
  14.4 0.8 %shard_map.94.f_ref = f32[64,1024]{1,0:T(8,128)S(1)} custom-call(f32[64,1024]{1,0:T(8,128)S(1)} %shard_map.93.f_ref, bf16[64,1024]{1,0:T(8,128)(2,1)S(1)} %collective-permute-done.1.b_ref, bf16[1024,4096]{1,0:T(8,128)(2,1)S(1)} %get-tuple-element.18.w_ref), custom_call_target="tpu_custom_call" | custom-call | flops 134217728 | bytes 8781824 | tf_op jit(solution)/shard_map/pallas_call | solution.py:30
  15.2 0.0 copy-start.2
  15.2 0.2 collective-permute-done.2.b_ref
  15.4 0.8 %shard_map.95.a_ref.refs_3_ = bf16[64,1024]{1,0:T(8,128)(2,1)S(1)} custom-call(f32[64,1024]{1,0:T(8,128)S(1)} %shard_map.94.f_ref, bf16[64,1024]{1,0:T(8,128)(2,1)S(1)} %collective-permute-done.2.b_ref, bf16[1024,4096]{1,0:T(8,128)(2,1)S(1)} %get-tuple-element.18.w_ref), custom_call_target="tpu_custom_call" | custom-call | flops 134217728 | bytes 8781824 | tf_op jit(solution)/shard_map/pallas_call | solution.py:30
  16.2 0.1 collective-permute-start.9
  16.3 2.5 %collective-permute-start.3 = (bf16[64,1024]{1,0:T(8,128)(2,1)S(1)}, bf16[64,1024]{1,0:T(8,128)(2,1)S(1)}, u32[]{:S(2)}, u32[]{:S(2)}) collective-permute-start(bf16[64,1024]{1,0:T(8,128)(2,1)S(1)} %shard_map.95.a_ref.refs_3_), channel_id=1, source_target_pairs={{0,24},{4,28},{8,16},{12,20},{16,8},{20,12},{24,0},{28,4},{1,25},{... | collective-permute-start | bytes 393224 | tf_op jit(solution)/shard_map/ppermute | solution.py:382
  18.8 0.5 collective-permute-start.4
  19.3 0.5 %collective-permute-start.5 = (bf16[64,1024]{1,0:T(8,128)(2,1)S(1)}, bf16[64,1024]{1,0:T(8,128)(2,1)S(1)}, u32[]{:S(2)}, u32[]{:S(2)}) collective-permute-start(bf16[64,1024]{1,0:T(8,128)(2,1)S(1)} %shard_map.95.a_ref.refs_3_), channel_id=1, source_target_pairs={{0,8},{4,12},{8,0},{12,4},{16,24},{20,28},{24,16},{28,20},{1,9},{5... | collective-permute-start | bytes 393224 | tf_op jit(solution)/shard_map/ppermute | solution.py:382
  19.8 0.2 shard_map.96
  20.0 0.0 collective-permute-start.11
  20.0 0.3 shard_map.98
  20.3 4.2 %collective-permute-start.12 = (bf16[128,256]{1,0:T(8,128)(2,1)S(1)}, bf16[128,256]{1,0:T(8,128)(2,1)S(1)}, u32[]{:S(2)}, u32[]{:S(2)}) collective-permute-start(bf16[128,256]{1,0:T(8,128)(2,1)S(1)} %shard_map.98), channel_id=1, source_target_pairs={{0,2},{3,1},{1,0},{2,3},{4,6},{7,5},{5,4},{6,7},{8,10},{11,9},{9,8... | collective-permute-start | bytes 196616 | tf_op jit(solution)/shard_map/ppermute | solution.py:374
  24.5 1.3 %collective-permute-done.4.refs_1_ = bf16[64,1024]{1,0:T(8,128)(2,1)S(1)} collective-permute-done((bf16[64,1024]{1,0:T(8,128)(2,1)S(1)}, bf16[64,1024]{1,0:T(8,128)(2,1)S(1)}, u32[]{:S(2)}, u32[]{:S(2)}) %collective-permute-start.4) | collective-permute-done | bytes 131104 | tf_op jit(solution)/shard_map/ppermute | solution.py:382
  25.9 0.0 collective-permute-start.7
  25.9 0.1 collective-permute-done.5.refs_2_
  26.0 0.4 collective-permute-start.8
  26.4 0.0 collective-permute-done.11.c_ref
  26.4 0.2 shard_map.97
  26.6 1.5 %collective-permute-start.16 = (bf16[576,128]{1,0:T(8,128)(2,1)S(1)}, bf16[576,128]{1,0:T(8,128)(2,1)S(1)}, u32[]{:S(2)}, u32[]{:S(2)}) collective-permute-start(bf16[576,128]{1,0:T(8,128)(2,1)S(1)} %get-tuple-element.28.refs_0_), channel_id=1, source_target_pairs={{0,16},{4,20},{8,24},{12,28},{16,0},{20,4},{24,8},{28,12},{1,17},{... | collective-permute-start | bytes 442376 | tf_op jit(solution)/shard_map/ppermute | solution.py:382
  28.1 0.0 collective-permute-done.12.x_ref
  28.1 0.8 %shard_map.100 = (f32[512,256]{1,0:T(8,128)S(1)}, bf16[512,256]{1,0:T(8,128)(2,1)S(1)}, bf16[512,256]{1,0:T(8,128)(2,1)S(1)}, bf16[384,256]{1,0:T(8,128)(2,1)S(1)}) custom-call(bf16[64,1024]{1,0:T(8,128)(2,1)S(1)} %collective-permute-done.3.refs_0_, bf16[64,1024]{1,0:T(8,128)(2,1)S(1)} %collective-permute-done.4.refs_1_, ...), custom_call_target="tpu_custom_call" | custom-call | flops 536870912 | bytes 2228224 | tf_op jit(solution)/shard_map/pallas_call | solution.py:30
  28.9 2.3 %collective-permute-start.13 = (bf16[512,256]{1,0:T(8,128)(2,1)S(1)}, bf16[512,256]{1,0:T(8,128)(2,1)S(1)}, u32[]{:S(2)}, u32[]{:S(2)}) collective-permute-start(bf16[512,256]{1,0:T(8,128)(2,1)S(1)} %get-tuple-element.25), channel_id=1, source_target_pairs={{0,1},{1,0},{2,3},{3,2},{4,5},{5,4},{6,7},{7,6},{8,9},{9,8},{10,11... | collective-permute-start | bytes 786440 | tf_op jit(solution)/shard_map/ppermute | solution.py:374
  31.2 2.1 %collective-permute-start.15 = (bf16[384,256]{1,0:T(8,128)(2,1)S(1)}, bf16[384,256]{1,0:T(8,128)(2,1)S(1)}, u32[]{:S(2)}, u32[]{:S(2)}) collective-permute-start(bf16[384,256]{1,0:T(8,128)(2,1)S(1)} %get-tuple-element.27), channel_id=1, source_target_pairs={{0,2},{3,1},{1,0},{2,3},{4,6},{7,5},{5,4},{6,7},{8,10},{11,9},{9,8... | collective-permute-start | bytes 589832 | tf_op jit(solution)/shard_map/ppermute | solution.py:374
  33.3 1.8 %collective-permute-start.18 = (bf16[576,128]{1,0:T(8,128)(2,1)S(1)}, bf16[576,128]{1,0:T(8,128)(2,1)S(1)}, u32[]{:S(2)}, u32[]{:S(2)}) collective-permute-start(bf16[576,128]{1,0:T(8,128)(2,1)S(1)} %get-tuple-element.28.refs_0_), channel_id=1, source_target_pairs={{0,24},{4,28},{8,16},{12,20},{16,8},{20,12},{24,0},{28,4},{1,25},{... | collective-permute-start | bytes 442376 | tf_op jit(solution)/shard_map/ppermute | solution.py:382
  35.1 0.5 %collective-permute-start.19 = (bf16[576,128]{1,0:T(8,128)(2,1)S(1)}, bf16[576,128]{1,0:T(8,128)(2,1)S(1)}, u32[]{:S(2)}, u32[]{:S(2)}) collective-permute-start(bf16[576,128]{1,0:T(8,128)(2,1)S(1)} %get-tuple-element.28.refs_0_), channel_id=1, source_target_pairs={{0,8},{4,12},{8,0},{12,4},{16,24},{20,28},{24,16},{28,20},{1,9},{5... | collective-permute-start | bytes 442376 | tf_op jit(solution)/shard_map/ppermute | solution.py:382
  35.7 5.3 %collective-permute-done.18.refs_0_ = bf16[576,128]{1,0:T(8,128)(2,1)S(1)} collective-permute-done((bf16[576,128]{1,0:T(8,128)(2,1)S(1)}, bf16[576,128]{1,0:T(8,128)(2,1)S(1)}, u32[]{:S(2)}, u32[]{:S(2)}) %collective-permute-start.18) | collective-permute-done | bytes 147488 | tf_op jit(solution)/shard_map/ppermute | solution.py:382
  41.0 1.5 %collective-permute-done.19.refs_1_ = bf16[576,128]{1,0:T(8,128)(2,1)S(1)} collective-permute-done((bf16[576,128]{1,0:T(8,128)(2,1)S(1)}, bf16[576,128]{1,0:T(8,128)(2,1)S(1)}, u32[]{:S(2)}, u32[]{:S(2)}) %collective-permute-start.19) | collective-permute-done | bytes 147488 | tf_op jit(solution)/shard_map/ppermute | solution.py:382
  42.5 0.1 collective-permute-start.20
  42.6 0.1 broadcast_in_dim.2.live_ref
  42.7 0.4 shard_map.101.j_ref
  43.1 1.0 %collective-permute-done.20.d_ref = bf16[1152,128]{1,0:T(8,128)(2,1)S(1)} collective-permute-done((bf16[1152,128]{1,0:T(8,128)(2,1)S(1)}, bf16[1152,128]{1,0:T(8,128)(2,1)S(1)}, u32[]{:S(2)}, u32[]{:S(2)}) %collective-permute-start.20) | collective-permute-done | bytes 294944 | tf_op jit(solution)/shard_map/ppermute | solution.py:382
  44.1 0.7 %shard_map.104.o_ref = f32[8,128]{1,0:T(8,128)S(1)} custom-call(bf16[128,512]{1,0:T(8,128)(2,1)S(1)} %shard_map.101.j_ref, bf16[1152,128]{1,0:T(8,128)(2,1)S(1)} %shard_map.102.a_ref, bf16[1152,128]{1,0:T(8,128)(2,1)S(1)} %collective-permute-done.17.b_ref, bf16[1152,128]{1,0:T(8,128)(2,1)S(1)} %shard_map.103.c_ref, ...), custom_call_target="tpu_custom_call" | custom-call | flops 4194304 | bytes 1310720 | tf_op jit(solution)/shard_map/pallas_call | solution.py:30
  44.8 0.2 collective-permute-start.21
  45.0 1.0 %collective-permute-done.21.c_ref = f32[8,128]{1,0:T(8,128)S(1)} collective-permute-done((f32[8,128]{1,0:T(8,128)S(1)}, f32[8,128]{1,0:T(8,128)S(1)}, u32[]{:S(2)}, u32[]{:S(2)}) %collective-permute-start.21) | collective-permute-done | bytes 4128 | tf_op jit(solution)/shard_map/ppermute | solution.py:379
  46.0 4.2 %collective-permute-start.22 = (f32[8,128]{1,0:T(8,128)S(1)}, f32[8,128]{1,0:T(8,128)S(1)}, u32[]{:S(2)}, u32[]{:S(2)}) collective-permute-start(f32[8,128]{1,0:T(8,128)S(1)} %shard_map.105.j_ref), channel_id=1, source_target_pairs={{0,1},{1,0},{2,3},{3,2},{4,5},{5,4},{6,7},{7,6},{8,9},{9,8},{10,11... | collective-permute-start | bytes 12296 | tf_op jit(solution)/shard_map/ppermute | solution.py:374
  50.2 1.6 %collective-permute-done.22.c_ref = f32[8,128]{1,0:T(8,128)S(1)} collective-permute-done((f32[8,128]{1,0:T(8,128)S(1)}, f32[8,128]{1,0:T(8,128)S(1)}, u32[]{:S(2)}, u32[]{:S(2)}) %collective-permute-start.22) | collective-permute-done | bytes 4128 | tf_op jit(solution)/shard_map/ppermute | solution.py:374
  51.8 0.6 %shard_map.106 = f32[2,128]{1,0:T(2,128)} custom-call(f32[8,128]{1,0:T(8,128)S(1)} %shard_map.105.j_ref, f32[8,128]{1,0:T(8,128)S(1)} %collective-permute-done.22.c_ref), custom_call_target="tpu_custom_call" | custom-call | bytes 8192 | tf_op jit(solution)/shard_map/pallas_call | solution.py:30
  (23 shorter events, 0.1 us)
Async XLA Ops:
  0.9 12.7 %collective-permute-start = (bf16[64,1024]{1,0:T(8,128)(2,1)S(1)}, bf16[64,1024]{1,0:T(8,128)(2,1)S(1)}, u32[]{:S(2)}, u32[]{:S(2)}) collective-permute-start(bf16[64,1024]{1,0:T(8,128)(2,1)S(1)} %shard_map.91.b_ref), channel_id=1, source_target_pairs={{0,2},{1,3},{2,0},{3,1},{4,6},{5,7},{6,4},{7,5},{8,10},{9,11},{10,... | collective-permute-start | bytes 393224 | tf_op jit(solution)/shard_map/ppermute | solution.py:382
  5.0 9.4 %collective-permute-start.1 = (bf16[64,1024]{1,0:T(8,128)(2,1)S(1)}, bf16[64,1024]{1,0:T(8,128)(2,1)S(1)}, u32[]{:S(2)}, u32[]{:S(2)}) collective-permute-start(bf16[64,1024]{1,0:T(8,128)(2,1)S(1)} %shard_map.91.b_ref), channel_id=1, source_target_pairs={{0,1},{1,0},{2,3},{3,2},{4,5},{5,4},{6,7},{7,6},{8,9},{9,8},{10,11... | collective-permute-start | bytes 393224 | tf_op jit(solution)/shard_map/ppermute | solution.py:382
  6.6 8.8 %collective-permute-start.2 = (bf16[64,1024]{1,0:T(8,128)(2,1)S(1)}, bf16[64,1024]{1,0:T(8,128)(2,1)S(1)}, u32[]{:S(2)}, u32[]{:S(2)}) collective-permute-start(bf16[64,1024]{1,0:T(8,128)(2,1)S(1)} %shard_map.91.b_ref), channel_id=1, source_target_pairs={{0,3},{1,2},{2,1},{3,0},{4,7},{5,6},{6,5},{7,4},{8,11},{9,10},{10,... | collective-permute-start | bytes 393224 | tf_op jit(solution)/shard_map/ppermute | solution.py:382
  6.6 0.8 %copy-start = (bf16[16,1024]{1,0:T(8,128)(2,1)S(1)}, bf16[16,1024]{1,0:T(8,128)(2,1)}, u32[]{:S(2)}) copy-start(bf16[16,1024]{1,0:T(8,128)(2,1)} %q_ref.1) | copy-start | bytes 98308
  7.4 0.7 %copy-start.1 = (bf16[3,1024]{1,0:T(4,128)(2,1)S(1)}, bf16[3,1024]{1,0:T(4,128)(2,1)}, u32[]{:S(2)}) copy-start(bf16[3,1024]{1,0:T(4,128)(2,1)} %c_ref.1) | copy-start | bytes 18436
  12.7 7.2 %collective-permute-start.10 = (bf16[448,128]{1,0:T(8,128)(2,1)S(1)}, bf16[448,128]{1,0:T(8,128)(2,1)S(1)}, u32[]{:S(2)}, u32[]{:S(2)}) collective-permute-start(bf16[448,128]{1,0:T(8,128)(2,1)S(1)} %get-tuple-element.20.o_ref), channel_id=1, source_target_pairs={{0,1},{1,0},{2,3},{3,2},{4,5},{5,4},{6,7},{7,6},{8,9},{9,8},{10,11... | collective-permute-start | bytes 344072 | tf_op jit(solution)/shard_map/ppermute | solution.py:374
  15.2 27.4 %copy-start.3 = (s32[2]{0:T(128)S(1)}, s32[2]{0:T(128)}, u32[]{:S(2)}) copy-start(s32[2]{0:T(128)} %param.11) | copy-start | bytes 28
  15.2 27.5 %copy-start.2 = (s32[2,256]{1,0:T(2,128)S(1)}, s32[2,256]{1,0:T(2,128)}, u32[]{:S(2)}) copy-start(s32[2,256]{1,0:T(2,128)} %t_ref.1) | copy-start | bytes 6148
  16.2 3.8 %collective-permute-start.9 = (bf16[64,1024]{1,0:T(8,128)(2,1)S(1)}, bf16[64,1024]{1,0:T(8,128)(2,1)S(1)}, u32[]{:S(2)}, u32[]{:S(2)}) collective-permute-start(bf16[64,1024]{1,0:T(8,128)(2,1)S(1)} %shard_map.95.a_ref.refs_3_), channel_id=1, source_target_pairs={{0,4},{4,0},{8,12},{12,8},{16,20},{20,16},{24,28},{28,24},{1,5},{5... | collective-permute-start | bytes 393224 | tf_op jit(solution)/shard_map/ppermute | solution.py:382
  16.3 8.3 %collective-permute-start.3 = (bf16[64,1024]{1,0:T(8,128)(2,1)S(1)}, bf16[64,1024]{1,0:T(8,128)(2,1)S(1)}, u32[]{:S(2)}, u32[]{:S(2)}) collective-permute-start(bf16[64,1024]{1,0:T(8,128)(2,1)S(1)} %shard_map.95.a_ref.refs_3_), channel_id=1, source_target_pairs={{0,24},{4,28},{8,16},{12,20},{16,8},{20,12},{24,0},{28,4},{1,25},{... | collective-permute-start | bytes 393224 | tf_op jit(solution)/shard_map/ppermute | solution.py:382
  18.8 7.1 %collective-permute-start.4 = (bf16[64,1024]{1,0:T(8,128)(2,1)S(1)}, bf16[64,1024]{1,0:T(8,128)(2,1)S(1)}, u32[]{:S(2)}, u32[]{:S(2)}) collective-permute-start(bf16[64,1024]{1,0:T(8,128)(2,1)S(1)} %shard_map.95.a_ref.refs_3_), channel_id=1, source_target_pairs={{0,16},{4,20},{8,24},{12,28},{16,0},{20,4},{24,8},{28,12},{1,17},{... | collective-permute-start | bytes 393224 | tf_op jit(solution)/shard_map/ppermute | solution.py:382
  19.3 6.7 %collective-permute-start.5 = (bf16[64,1024]{1,0:T(8,128)(2,1)S(1)}, bf16[64,1024]{1,0:T(8,128)(2,1)S(1)}, u32[]{:S(2)}, u32[]{:S(2)}) collective-permute-start(bf16[64,1024]{1,0:T(8,128)(2,1)S(1)} %shard_map.95.a_ref.refs_3_), channel_id=1, source_target_pairs={{0,8},{4,12},{8,0},{12,4},{16,24},{20,28},{24,16},{28,20},{1,9},{5... | collective-permute-start | bytes 393224 | tf_op jit(solution)/shard_map/ppermute | solution.py:382
  20.0 6.4 %collective-permute-start.11 = (bf16[448,128]{1,0:T(8,128)(2,1)S(1)}, bf16[448,128]{1,0:T(8,128)(2,1)S(1)}, u32[]{:S(2)}, u32[]{:S(2)}) collective-permute-start(bf16[448,128]{1,0:T(8,128)(2,1)S(1)} %get-tuple-element.21.o_ref), channel_id=1, source_target_pairs={{0,4},{1,2},{2,1},{3,7},{4,0},{5,6},{6,5},{7,3},{8,12},{9,10},{10,... | collective-permute-start | bytes 344072 | tf_op jit(solution)/shard_map/ppermute | solution.py:379
  20.3 7.8 %collective-permute-start.12 = (bf16[128,256]{1,0:T(8,128)(2,1)S(1)}, bf16[128,256]{1,0:T(8,128)(2,1)S(1)}, u32[]{:S(2)}, u32[]{:S(2)}) collective-permute-start(bf16[128,256]{1,0:T(8,128)(2,1)S(1)} %shard_map.98), channel_id=1, source_target_pairs={{0,2},{3,1},{1,0},{2,3},{4,6},{7,5},{5,4},{6,7},{8,10},{11,9},{9,8... | collective-permute-start | bytes 196616 | tf_op jit(solution)/shard_map/ppermute | solution.py:374
  24.5 3.6 %collective-permute-start.6 = (bf16[64,1024]{1,0:T(8,128)(2,1)S(1)}, bf16[64,1024]{1,0:T(8,128)(2,1)S(1)}, u32[]{:S(2)}, u32[]{:S(2)}) collective-permute-start(bf16[64,1024]{1,0:T(8,128)(2,1)S(1)} %collective-permute-done.3.refs_0_), channel_id=1, source_target_pairs={{0,4},{4,0},{8,12},{12,8},{16,20},{20,16},{24,28},{28,24},{1,5},{5... | collective-permute-start | bytes 393224 | tf_op jit(solution)/shard_map/ppermute | solution.py:382
  25.9 2.2 %collective-permute-start.7 = (bf16[64,1024]{1,0:T(8,128)(2,1)S(1)}, bf16[64,1024]{1,0:T(8,128)(2,1)S(1)}, u32[]{:S(2)}, u32[]{:S(2)}) collective-permute-start(bf16[64,1024]{1,0:T(8,128)(2,1)S(1)} %collective-permute-done.4.refs_1_), channel_id=1, source_target_pairs={{0,4},{4,0},{8,12},{12,8},{16,20},{20,16},{24,28},{28,24},{1,5},{5... | collective-permute-start | bytes 393224 | tf_op jit(solution)/shard_map/ppermute | solution.py:382
  26.0 2.1 %collective-permute-start.8 = (bf16[64,1024]{1,0:T(8,128)(2,1)S(1)}, bf16[64,1024]{1,0:T(8,128)(2,1)S(1)}, u32[]{:S(2)}, u32[]{:S(2)}) collective-permute-start(bf16[64,1024]{1,0:T(8,128)(2,1)S(1)} %collective-permute-done.5.refs_2_), channel_id=1, source_target_pairs={{0,4},{4,0},{8,12},{12,8},{16,20},{20,16},{24,28},{28,24},{1,5},{5... | collective-permute-start | bytes 393224 | tf_op jit(solution)/shard_map/ppermute | solution.py:382
  26.6 8.5 %collective-permute-start.16 = (bf16[576,128]{1,0:T(8,128)(2,1)S(1)}, bf16[576,128]{1,0:T(8,128)(2,1)S(1)}, u32[]{:S(2)}, u32[]{:S(2)}) collective-permute-start(bf16[576,128]{1,0:T(8,128)(2,1)S(1)} %get-tuple-element.28.refs_0_), channel_id=1, source_target_pairs={{0,16},{4,20},{8,24},{12,28},{16,0},{20,4},{24,8},{28,12},{1,17},{... | collective-permute-start | bytes 442376 | tf_op jit(solution)/shard_map/ppermute | solution.py:382
  28.9 13.7 %collective-permute-start.13 = (bf16[512,256]{1,0:T(8,128)(2,1)S(1)}, bf16[512,256]{1,0:T(8,128)(2,1)S(1)}, u32[]{:S(2)}, u32[]{:S(2)}) collective-permute-start(bf16[512,256]{1,0:T(8,128)(2,1)S(1)} %get-tuple-element.25), channel_id=1, source_target_pairs={{0,1},{1,0},{2,3},{3,2},{4,5},{5,4},{6,7},{7,6},{8,9},{9,8},{10,11... | collective-permute-start | bytes 786440 | tf_op jit(solution)/shard_map/ppermute | solution.py:374
  31.2 11.4 %collective-permute-start.14 = (bf16[512,256]{1,0:T(8,128)(2,1)S(1)}, bf16[512,256]{1,0:T(8,128)(2,1)S(1)}, u32[]{:S(2)}, u32[]{:S(2)}) collective-permute-start(bf16[512,256]{1,0:T(8,128)(2,1)S(1)} %get-tuple-element.26), channel_id=1, source_target_pairs={{0,4},{1,2},{2,1},{3,7},{4,0},{5,6},{6,5},{7,3},{8,12},{9,10},{10,... | collective-permute-start | bytes 786440 | tf_op jit(solution)/shard_map/ppermute | solution.py:379
  31.2 11.4 %collective-permute-start.15 = (bf16[384,256]{1,0:T(8,128)(2,1)S(1)}, bf16[384,256]{1,0:T(8,128)(2,1)S(1)}, u32[]{:S(2)}, u32[]{:S(2)}) collective-permute-start(bf16[384,256]{1,0:T(8,128)(2,1)S(1)} %get-tuple-element.27), channel_id=1, source_target_pairs={{0,2},{3,1},{1,0},{2,3},{4,6},{7,5},{5,4},{6,7},{8,10},{11,9},{9,8... | collective-permute-start | bytes 589832 | tf_op jit(solution)/shard_map/ppermute | solution.py:374
  33.3 7.7 %collective-permute-start.18 = (bf16[576,128]{1,0:T(8,128)(2,1)S(1)}, bf16[576,128]{1,0:T(8,128)(2,1)S(1)}, u32[]{:S(2)}, u32[]{:S(2)}) collective-permute-start(bf16[576,128]{1,0:T(8,128)(2,1)S(1)} %get-tuple-element.28.refs_0_), channel_id=1, source_target_pairs={{0,24},{4,28},{8,16},{12,20},{16,8},{20,12},{24,0},{28,4},{1,25},{... | collective-permute-start | bytes 442376 | tf_op jit(solution)/shard_map/ppermute | solution.py:382
  35.1 7.4 %collective-permute-start.19 = (bf16[576,128]{1,0:T(8,128)(2,1)S(1)}, bf16[576,128]{1,0:T(8,128)(2,1)S(1)}, u32[]{:S(2)}, u32[]{:S(2)}) collective-permute-start(bf16[576,128]{1,0:T(8,128)(2,1)S(1)} %get-tuple-element.28.refs_0_), channel_id=1, source_target_pairs={{0,8},{4,12},{8,0},{12,4},{16,24},{20,28},{24,16},{28,20},{1,9},{5... | collective-permute-start | bytes 442376 | tf_op jit(solution)/shard_map/ppermute | solution.py:382
  41.0 2.2 %collective-permute-start.17 = (bf16[1152,128]{1,0:T(8,128)(2,1)S(1)}, bf16[1152,128]{1,0:T(8,128)(2,1)S(1)}, u32[]{:S(2)}, u32[]{:S(2)}) collective-permute-start(bf16[1152,128]{1,0:T(8,128)(2,1)S(1)} %shard_map.102.a_ref), channel_id=1, source_target_pairs={{0,4},{4,0},{8,12},{12,8},{16,20},{20,16},{24,28},{28,24},{1,5},{5... | collective-permute-start | bytes 884744 | tf_op jit(solution)/shard_map/ppermute | solution.py:382
  42.5 1.6 %collective-permute-start.20 = (bf16[1152,128]{1,0:T(8,128)(2,1)S(1)}, bf16[1152,128]{1,0:T(8,128)(2,1)S(1)}, u32[]{:S(2)}, u32[]{:S(2)}) collective-permute-start(bf16[1152,128]{1,0:T(8,128)(2,1)S(1)} %shard_map.103.c_ref), channel_id=1, source_target_pairs={{0,4},{4,0},{8,12},{12,8},{16,20},{20,16},{24,28},{28,24},{1,5},{5... | collective-permute-start | bytes 884744 | tf_op jit(solution)/shard_map/ppermute | solution.py:382
  44.8 1.2 %collective-permute-start.21 = (f32[8,128]{1,0:T(8,128)S(1)}, f32[8,128]{1,0:T(8,128)S(1)}, u32[]{:S(2)}, u32[]{:S(2)}) collective-permute-start(f32[8,128]{1,0:T(8,128)S(1)} %shard_map.104.o_ref), channel_id=1, source_target_pairs={{0,4},{1,2},{2,1},{3,7},{4,0},{5,6},{6,5},{7,3},{8,12},{9,10},{10,... | collective-permute-start | bytes 12296 | tf_op jit(solution)/shard_map/ppermute | solution.py:379
  46.0 5.8 %collective-permute-start.22 = (f32[8,128]{1,0:T(8,128)S(1)}, f32[8,128]{1,0:T(8,128)S(1)}, u32[]{:S(2)}, u32[]{:S(2)}) collective-permute-start(f32[8,128]{1,0:T(8,128)S(1)} %shard_map.105.j_ref), channel_id=1, source_target_pairs={{0,1},{1,0},{2,3},{3,2},{4,5},{5,4},{6,7},{7,6},{8,9},{9,8},{10,11... | collective-permute-start | bytes 12296 | tf_op jit(solution)/shard_map/ppermute | solution.py:374

commit v7 on v6

--- a/solution.py
+++ b/solution.py
@@ -273,16 +273,28 @@
     )
 
 
-def token_grads(parts, pieces, first, side_in, targets, lengths):
+def join(first, rest):
+    high = first.shape[0]
+    shape = (high + rest.shape[0], first.shape[1])
+
+    def body(a_ref, b_ref, out_ref):
+        out_ref[:high, :] = a_ref[...]
+        out_ref[high:, :] = b_ref[...]
+
+    return call(body, arr(shape, bf16), (first, rest), 1 << 30)
+
+
+def token_grads(parts, pieces, side_in, targets, lengths):
     vocab, length = pieces[0].shape
     rank = side_in.shape[0]
     step = vocab // parts
 
-    def body(k_ref, n_ref, c_ref, f_ref, l_ref, side_ref, t_ref, live_ref, out_ref):
+    def body(k_ref, f_ref, c_ref, n_ref, side_ref, t_ref, live_ref, out_ref):
         row = lax.axis_index("tensor") // 2
         own = lax.axis_index("dp") % parts
-        total = k_ref[...] + n_ref[...].astype(f32) + c_ref[...].astype(f32)
-        total += jnp.concatenate([l_ref[...], f_ref[...]], axis=0).astype(f32)
+        total = k_ref[...]
+        for ref in (f_ref, c_ref, n_ref):
+            total += ref[...].astype(f32)
         expo = jnp.exp(total)
         targets_here = jnp.where(row == 0, t_ref[0:1, :], t_ref[1:2, :])
         lengths_here = jnp.where(row == 0, live_ref[0:1, :], live_ref[1:2, :])
@@ -294,11 +306,10 @@
         joint = lax.dot_general(split2(side_ref[...], 0), grad, NT, preferred_element_type=f32)
         out_ref[...] = split2(halve(joint), 0)
 
-    spread = jnp.broadcast_to(lengths[:, None], targets.shape)
     return call(
         body,
         arr((2 * rank, vocab), bf16),
-        (*pieces, first, side_in, targets, spread),
+        (*pieces, side_in, targets, lengths[:, None]),
         1 << 34,
     )
 
@@ -397,14 +408,15 @@
     first = pass_on(send(first_logits(folded[0], folded[1], mixed), FAR))
     whole, side_in = gather_shares(across, cross(across), keep_side, block, step)
     keep, near_logits, other_logits, rest = logit_rows(folded, mixed, side_in, first)
-    pieces = (keep, send(near_logits, NEAR), cross(other_logits), send(rest, FAR))
+    far_logits = join(first, send(rest, FAR))
+    pieces = (keep, far_logits, cross(other_logits), send(near_logits, NEAR))
     queries = None
     if n_dp != parts:
         queries = lax.all_gather(whole[: 4 * block], "dp", axis=0)
     others = {s: swap(whole, "dp", s) for s in range(2, parts, 2)}
     pairs = stack((whole, others[4])), stack((others[6], others[2]))
     shares = [y for x in pairs for y in (x, swap(x, "dp", 1))]
-    joint = token_grads(parts, pieces, first, side_in, targets, lengths)
+    joint = token_grads(parts, pieces, side_in, targets, lengths)
     scores = row_scores(parts, joint, shares, queries)
     joined = join_rows(scores, cross(scores))
     return pick_rows(joined, send(joined, NEAR))

time: 52.6 us -> 52.9 us (level)
    pallas_call x16 -> x17, Pallas kernels: 11 us -> 11 us  [call(): pl.pallas_call(body, out_shape=outs, in_specs=in_specs or [VM] * len(args...]
where the time goes in v7:
time: 52.9 us; the launch traced here: 52.7 us
  starting transfers between devices  28 us (53%)
  waiting for transfers between devices  11.9 us (22%)
  Pallas kernels  11 us (21%)
  local copies, waits for them, and re-layouts  1.55 us (3%)
    ppermute x5, starting transfers between devices, send(): return lax.ppermute(x, 'tensor', pairs)  14.2 us
    ppermute x15, starting transfers between devices, swap(): lax.ppermute(x, axis, [(i, i ^ slot) for i in range(lax.axis_size(axis))])  13.6 us
    pallas_call x17, Pallas kernels, call(): pl.pallas_call(body, out_shape=outs, in_specs=in_specs or [VM] * len(args...  11 us
    ppermute x15, waiting for transfers between devices, swap(): lax.ppermute(x, axis, [(i, i ^ slot) for i in range(lax.axis_size(axis))])  9.31 us
    ppermute x5, waiting for transfers between devices, send(): return lax.ppermute(x, 'tensor', pairs)  1.59 us
    unnamed x8, local copies, waits for them, and re-layouts  1.46 us
  transfers between devices with their start and end apart: 23, of which 8 were waited for; matrix products, arithmetic and copies ran while one was open for 0% of the time, Pallas kernels for 17%

profile of v7, /device:TPU:0, one launch (start us, length us, event | category | flops | bytes accessed | tf_op | source)
XLA Modules:
  0.0 52.7 jit_solution(10674715644948929508)
XLA Ops:
  0.0 0.9 %shard_map.91.b_ref = bf16[64,1024]{1,0:T(8,128)(2,1)S(1)} custom-call(bf16[512,1024]{1,0:T(8,128)(2,1)} %e_ref.1), custom_call_target="tpu_custom_call" | custom-call | bytes 1048576 | tf_op jit(solution)/shard_map/pallas_call | solution.py:30
  0.9 4.1 %collective-permute-start = (bf16[64,1024]{1,0:T(8,128)(2,1)S(1)}, bf16[64,1024]{1,0:T(8,128)(2,1)S(1)}, u32[]{:S(2)}, u32[]{:S(2)}) collective-permute-start(bf16[64,1024]{1,0:T(8,128)(2,1)S(1)} %shard_map.91.b_ref), channel_id=1, source_target_pairs={{0,2},{1,3},{2,0},{3,1},{4,6},{5,7},{6,4},{7,5},{8,10},{9,11},{10,... | collective-permute-start | bytes 393224 | tf_op jit(solution)/shard_map/ppermute | solution.py:393
  5.0 1.6 %collective-permute-start.1 = (bf16[64,1024]{1,0:T(8,128)(2,1)S(1)}, bf16[64,1024]{1,0:T(8,128)(2,1)S(1)}, u32[]{:S(2)}, u32[]{:S(2)}) collective-permute-start(bf16[64,1024]{1,0:T(8,128)(2,1)S(1)} %shard_map.91.b_ref), channel_id=1, source_target_pairs={{0,1},{1,0},{2,3},{3,2},{4,5},{5,4},{6,7},{7,6},{8,9},{9,8},{10,11... | collective-permute-start | bytes 393224 | tf_op jit(solution)/shard_map/ppermute | solution.py:393
  6.6 0.0 collective-permute-start.2
  6.6 0.8 %copy-done = bf16[16,1024]{1,0:T(8,128)(2,1)S(1)} copy-done((bf16[16,1024]{1,0:T(8,128)(2,1)S(1)}, bf16[16,1024]{1,0:T(8,128)(2,1)}, u32[]{:S(2)}) %copy-start) | copy-done | bytes 32792
  7.4 0.7 %copy-done.1 = bf16[3,1024]{1,0:T(4,128)(2,1)S(1)} copy-done((bf16[3,1024]{1,0:T(4,128)(2,1)S(1)}, bf16[3,1024]{1,0:T(4,128)(2,1)}, u32[]{:S(2)}) %copy-start.1) | copy-done | bytes 6168
  8.1 4.6 %shard_map.92 = (bf16[512,1024]{1,0:T(8,128)(2,1)S(1)}, bf16[448,128]{1,0:T(8,128)(2,1)S(1)}, f32[64,1024]{1,0:T(8,128)S(1)}, bf16[1024,4096]{1,0:T(8,128)(2,1)S(1)}) custom-call(bf16[2,256,1024]{2,1,0:T(8,128)(2,1)} %h_any.1, bf16[64,1024]{1,0:T(8,128)(2,1)} %bitcast.3, bf16[64,1024]{1,0:T(8,128)(2,1)} %bitcast.4, bf16[1024,4096]{1,0:T(8,128)(2,1)} %w_any.1, ...), custom_call_target="tpu_custom_call" | custom-call | flops 201326592 | bytes 9869312 | tf_op jit(solution)/shard_map/pallas_call | solution.py:30
  12.7 1.0 %collective-permute-start.10 = (bf16[448,128]{1,0:T(8,128)(2,1)S(1)}, bf16[448,128]{1,0:T(8,128)(2,1)S(1)}, u32[]{:S(2)}, u32[]{:S(2)}) collective-permute-start(bf16[448,128]{1,0:T(8,128)(2,1)S(1)} %get-tuple-element.20.o_ref), channel_id=1, source_target_pairs={{0,1},{1,0},{2,3},{3,2},{4,5},{5,4},{6,7},{7,6},{8,9},{9,8},{10,11... | collective-permute-start | bytes 344072 | tf_op jit(solution)/shard_map/ppermute | solution.py:385
  13.6 0.0 collective-permute-done.b_ref
  13.6 0.8 %shard_map.93.f_ref = f32[64,1024]{1,0:T(8,128)S(1)} custom-call(f32[64,1024]{1,0:T(8,128)S(1)} %get-tuple-element.17.f_ref, bf16[64,1024]{1,0:T(8,128)(2,1)S(1)} %collective-permute-done.b_ref, bf16[1024,4096]{1,0:T(8,128)(2,1)S(1)} %get-tuple-element.18.w_ref), custom_call_target="tpu_custom_call" | custom-call | flops 134217728 | bytes 8781824 | tf_op jit(solution)/shard_map/pallas_call | solution.py:30
  14.4 0.0 collective-permute-done.1.b_ref
  14.4 0.8 %shard_map.94.f_ref = f32[64,1024]{1,0:T(8,128)S(1)} custom-call(f32[64,1024]{1,0:T(8,128)S(1)} %shard_map.93.f_ref, bf16[64,1024]{1,0:T(8,128)(2,1)S(1)} %collective-permute-done.1.b_ref, bf16[1024,4096]{1,0:T(8,128)(2,1)S(1)} %get-tuple-element.18.w_ref), custom_call_target="tpu_custom_call" | custom-call | flops 134217728 | bytes 8781824 | tf_op jit(solution)/shard_map/pallas_call | solution.py:30
  15.2 0.2 collective-permute-done.2.b_ref
  15.4 0.8 %shard_map.95.a_ref.refs_3_ = bf16[64,1024]{1,0:T(8,128)(2,1)S(1)} custom-call(f32[64,1024]{1,0:T(8,128)S(1)} %shard_map.94.f_ref, bf16[64,1024]{1,0:T(8,128)(2,1)S(1)} %collective-permute-done.2.b_ref, bf16[1024,4096]{1,0:T(8,128)(2,1)S(1)} %get-tuple-element.18.w_ref), custom_call_target="tpu_custom_call" | custom-call | flops 134217728 | bytes 8781824 | tf_op jit(solution)/shard_map/pallas_call | solution.py:30
  16.2 0.1 collective-permute-start.9
  16.3 2.5 %collective-permute-start.3 = (bf16[64,1024]{1,0:T(8,128)(2,1)S(1)}, bf16[64,1024]{1,0:T(8,128)(2,1)S(1)}, u32[]{:S(2)}, u32[]{:S(2)}) collective-permute-start(bf16[64,1024]{1,0:T(8,128)(2,1)S(1)} %shard_map.95.a_ref.refs_3_), channel_id=1, source_target_pairs={{0,24},{4,28},{8,16},{12,20},{16,8},{20,12},{24,0},{28,4},{1,25},{... | collective-permute-start | bytes 393224 | tf_op jit(solution)/shard_map/ppermute | solution.py:393
  18.8 0.5 collective-permute-start.4
  19.3 0.5 %collective-permute-start.5 = (bf16[64,1024]{1,0:T(8,128)(2,1)S(1)}, bf16[64,1024]{1,0:T(8,128)(2,1)S(1)}, u32[]{:S(2)}, u32[]{:S(2)}) collective-permute-start(bf16[64,1024]{1,0:T(8,128)(2,1)S(1)} %shard_map.95.a_ref.refs_3_), channel_id=1, source_target_pairs={{0,8},{4,12},{8,0},{12,4},{16,24},{20,28},{24,16},{28,20},{1,9},{5... | collective-permute-start | bytes 393224 | tf_op jit(solution)/shard_map/ppermute | solution.py:393
  19.8 0.0 collective-permute-done.10.n_ref
  19.8 0.2 shard_map.96
  20.0 0.0 collective-permute-start.11
  20.0 0.3 shard_map.98
  20.3 4.2 %collective-permute-start.12 = (bf16[128,256]{1,0:T(8,128)(2,1)S(1)}, bf16[128,256]{1,0:T(8,128)(2,1)S(1)}, u32[]{:S(2)}, u32[]{:S(2)}) collective-permute-start(bf16[128,256]{1,0:T(8,128)(2,1)S(1)} %shard_map.98), channel_id=1, source_target_pairs={{0,2},{3,1},{1,0},{2,3},{4,6},{7,5},{5,4},{6,7},{8,10},{11,9},{9,8... | collective-permute-start | bytes 196616 | tf_op jit(solution)/shard_map/ppermute | solution.py:385
  24.6 0.0 collective-permute-done.3.refs_0_
  24.6 0.0 collective-permute-start.6
  24.6 1.3 %collective-permute-done.4.refs_1_ = bf16[64,1024]{1,0:T(8,128)(2,1)S(1)} collective-permute-done((bf16[64,1024]{1,0:T(8,128)(2,1)S(1)}, bf16[64,1024]{1,0:T(8,128)(2,1)S(1)}, u32[]{:S(2)}, u32[]{:S(2)}) %collective-permute-start.4) | collective-permute-done | bytes 131104 | tf_op jit(solution)/shard_map/ppermute | solution.py:393
  25.9 0.0 collective-permute-start.7
  25.9 0.1 collective-permute-done.5.refs_2_
  26.0 0.4 collective-permute-start.8
  26.4 0.2 shard_map.97
  26.6 1.5 %collective-permute-start.16 = (bf16[576,128]{1,0:T(8,128)(2,1)S(1)}, bf16[576,128]{1,0:T(8,128)(2,1)S(1)}, u32[]{:S(2)}, u32[]{:S(2)}) collective-permute-start(bf16[576,128]{1,0:T(8,128)(2,1)S(1)} %get-tuple-element.28.refs_0_), channel_id=1, source_target_pairs={{0,16},{4,20},{8,24},{12,28},{16,0},{20,4},{24,8},{28,12},{1,17},{... | collective-permute-start | bytes 442376 | tf_op jit(solution)/shard_map/ppermute | solution.py:393
  28.1 0.8 %shard_map.100 = (f32[512,256]{1,0:T(8,128)S(1)}, bf16[512,256]{1,0:T(8,128)(2,1)S(1)}, bf16[512,256]{1,0:T(8,128)(2,1)S(1)}, bf16[384,256]{1,0:T(8,128)(2,1)S(1)}) custom-call(bf16[64,1024]{1,0:T(8,128)(2,1)S(1)} %collective-permute-done.3.refs_0_, bf16[64,1024]{1,0:T(8,128)(2,1)S(1)} %collective-permute-done.4.refs_1_, ...), custom_call_target="tpu_custom_call" | custom-call | flops 536870912 | bytes 2228224 | tf_op jit(solution)/shard_map/pallas_call | solution.py:30
  28.9 4.2 %collective-permute-start.13 = (bf16[384,256]{1,0:T(8,128)(2,1)S(1)}, bf16[384,256]{1,0:T(8,128)(2,1)S(1)}, u32[]{:S(2)}, u32[]{:S(2)}) collective-permute-start(bf16[384,256]{1,0:T(8,128)(2,1)S(1)} %get-tuple-element.25), channel_id=1, source_target_pairs={{0,2},{3,1},{1,0},{2,3},{4,6},{7,5},{5,4},{6,7},{8,10},{11,9},{9,8... | collective-permute-start | bytes 589832 | tf_op jit(solution)/shard_map/ppermute | solution.py:385
  33.1 0.6 %collective-permute-start.15 = (bf16[512,256]{1,0:T(8,128)(2,1)S(1)}, bf16[512,256]{1,0:T(8,128)(2,1)S(1)}, u32[]{:S(2)}, u32[]{:S(2)}) collective-permute-start(bf16[512,256]{1,0:T(8,128)(2,1)S(1)} %get-tuple-element.27), channel_id=1, source_target_pairs={{0,1},{1,0},{2,3},{3,2},{4,5},{5,4},{6,7},{7,6},{8,9},{9,8},{10,11... | collective-permute-start | bytes 786440 | tf_op jit(solution)/shard_map/ppermute | solution.py:385
  33.8 1.4 %collective-permute-start.18 = (bf16[576,128]{1,0:T(8,128)(2,1)S(1)}, bf16[576,128]{1,0:T(8,128)(2,1)S(1)}, u32[]{:S(2)}, u32[]{:S(2)}) collective-permute-start(bf16[576,128]{1,0:T(8,128)(2,1)S(1)} %get-tuple-element.28.refs_0_), channel_id=1, source_target_pairs={{0,24},{4,28},{8,16},{12,20},{16,8},{20,12},{24,0},{28,4},{1,25},{... | collective-permute-start | bytes 442376 | tf_op jit(solution)/shard_map/ppermute | solution.py:393
  35.2 0.8 %collective-permute-start.19 = (bf16[576,128]{1,0:T(8,128)(2,1)S(1)}, bf16[576,128]{1,0:T(8,128)(2,1)S(1)}, u32[]{:S(2)}, u32[]{:S(2)}) collective-permute-start(bf16[576,128]{1,0:T(8,128)(2,1)S(1)} %get-tuple-element.28.refs_0_), channel_id=1, source_target_pairs={{0,8},{4,12},{8,0},{12,4},{16,24},{20,28},{24,16},{28,20},{1,9},{5... | collective-permute-start | bytes 442376 | tf_op jit(solution)/shard_map/ppermute | solution.py:393
  36.0 0.1 copy.10.live_ref
  36.1 5.3 %collective-permute-done.18.refs_0_ = bf16[576,128]{1,0:T(8,128)(2,1)S(1)} collective-permute-done((bf16[576,128]{1,0:T(8,128)(2,1)S(1)}, bf16[576,128]{1,0:T(8,128)(2,1)S(1)}, u32[]{:S(2)}, u32[]{:S(2)}) %collective-permute-start.18) | collective-permute-done | bytes 147488 | tf_op jit(solution)/shard_map/ppermute | solution.py:393
  41.4 1.4 %collective-permute-done.19.refs_1_ = bf16[576,128]{1,0:T(8,128)(2,1)S(1)} collective-permute-done((bf16[576,128]{1,0:T(8,128)(2,1)S(1)}, bf16[576,128]{1,0:T(8,128)(2,1)S(1)}, u32[]{:S(2)}, u32[]{:S(2)}) %collective-permute-start.19) | collective-permute-done | bytes 147488 | tf_op jit(solution)/shard_map/ppermute | solution.py:393
  42.8 0.1 collective-permute-start.20
  43.0 0.5 shard_map.102.j_ref
  43.4 1.0 %collective-permute-done.20.d_ref = bf16[1152,128]{1,0:T(8,128)(2,1)S(1)} collective-permute-done((bf16[1152,128]{1,0:T(8,128)(2,1)S(1)}, bf16[1152,128]{1,0:T(8,128)(2,1)S(1)}, u32[]{:S(2)}, u32[]{:S(2)}) %collective-permute-start.20) | collective-permute-done | bytes 294944 | tf_op jit(solution)/shard_map/ppermute | solution.py:393
  44.5 0.7 %shard_map.105.o_ref = f32[8,128]{1,0:T(8,128)S(1)} custom-call(bf16[128,512]{1,0:T(8,128)(2,1)S(1)} %shard_map.102.j_ref, bf16[1152,128]{1,0:T(8,128)(2,1)S(1)} %shard_map.103.a_ref, bf16[1152,128]{1,0:T(8,128)(2,1)S(1)} %collective-permute-done.17.b_ref, bf16[1152,128]{1,0:T(8,128)(2,1)S(1)} %shard_map.104.c_ref, ...), custom_call_target="tpu_custom_call" | custom-call | flops 4194304 | bytes 1310720 | tf_op jit(solution)/shard_map/pallas_call | solution.py:30
  45.2 0.1 collective-permute-start.21
  45.3 1.0 %collective-permute-done.21.c_ref = f32[8,128]{1,0:T(8,128)S(1)} collective-permute-done((f32[8,128]{1,0:T(8,128)S(1)}, f32[8,128]{1,0:T(8,128)S(1)}, u32[]{:S(2)}, u32[]{:S(2)}) %collective-permute-start.21) | collective-permute-done | bytes 4128 | tf_op jit(solution)/shard_map/ppermute | solution.py:390
  46.4 4.2 %collective-permute-start.22 = (f32[8,128]{1,0:T(8,128)S(1)}, f32[8,128]{1,0:T(8,128)S(1)}, u32[]{:S(2)}, u32[]{:S(2)}) collective-permute-start(f32[8,128]{1,0:T(8,128)S(1)} %shard_map.106.j_ref), channel_id=1, source_target_pairs={{0,1},{1,0},{2,3},{3,2},{4,5},{5,4},{6,7},{7,6},{8,9},{9,8},{10,11... | collective-permute-start | bytes 12296 | tf_op jit(solution)/shard_map/ppermute | solution.py:385
  50.5 1.6 %collective-permute-done.22.c_ref = f32[8,128]{1,0:T(8,128)S(1)} collective-permute-done((f32[8,128]{1,0:T(8,128)S(1)}, f32[8,128]{1,0:T(8,128)S(1)}, u32[]{:S(2)}, u32[]{:S(2)}) %collective-permute-start.22) | collective-permute-done | bytes 4128 | tf_op jit(solution)/shard_map/ppermute | solution.py:385
  52.1 0.6 %shard_map.107 = f32[2,128]{1,0:T(2,128)} custom-call(f32[8,128]{1,0:T(8,128)S(1)} %shard_map.106.j_ref, f32[8,128]{1,0:T(8,128)S(1)} %collective-permute-done.22.c_ref), custom_call_target="tpu_custom_call" | custom-call | bytes 8192 | tf_op jit(solution)/shard_map/pallas_call | solution.py:30
  (24 shorter events, 0.1 us)
Async XLA Ops:
  0.9 12.7 %collective-permute-start = (bf16[64,1024]{1,0:T(8,128)(2,1)S(1)}, bf16[64,1024]{1,0:T(8,128)(2,1)S(1)}, u32[]{:S(2)}, u32[]{:S(2)}) collective-permute-start(bf16[64,1024]{1,0:T(8,128)(2,1)S(1)} %shard_map.91.b_ref), channel_id=1, source_target_pairs={{0,2},{1,3},{2,0},{3,1},{4,6},{5,7},{6,4},{7,5},{8,10},{9,11},{10,... | collective-permute-start | bytes 393224 | tf_op jit(solution)/shard_map/ppermute | solution.py:393
  5.0 9.4 %collective-permute-start.1 = (bf16[64,1024]{1,0:T(8,128)(2,1)S(1)}, bf16[64,1024]{1,0:T(8,128)(2,1)S(1)}, u32[]{:S(2)}, u32[]{:S(2)}) collective-permute-start(bf16[64,1024]{1,0:T(8,128)(2,1)S(1)} %shard_map.91.b_ref), channel_id=1, source_target_pairs={{0,1},{1,0},{2,3},{3,2},{4,5},{5,4},{6,7},{7,6},{8,9},{9,8},{10,11... | collective-permute-start | bytes 393224 | tf_op jit(solution)/shard_map/ppermute | solution.py:393
  6.6 8.8 %collective-permute-start.2 = (bf16[64,1024]{1,0:T(8,128)(2,1)S(1)}, bf16[64,1024]{1,0:T(8,128)(2,1)S(1)}, u32[]{:S(2)}, u32[]{:S(2)}) collective-permute-start(bf16[64,1024]{1,0:T(8,128)(2,1)S(1)} %shard_map.91.b_ref), channel_id=1, source_target_pairs={{0,3},{1,2},{2,1},{3,0},{4,7},{5,6},{6,5},{7,4},{8,11},{9,10},{10,... | collective-permute-start | bytes 393224 | tf_op jit(solution)/shard_map/ppermute | solution.py:393
  6.6 0.8 %copy-start = (bf16[16,1024]{1,0:T(8,128)(2,1)S(1)}, bf16[16,1024]{1,0:T(8,128)(2,1)}, u32[]{:S(2)}) copy-start(bf16[16,1024]{1,0:T(8,128)(2,1)} %q_ref.1) | copy-start | bytes 98308
  7.4 0.7 %copy-start.1 = (bf16[3,1024]{1,0:T(4,128)(2,1)S(1)}, bf16[3,1024]{1,0:T(4,128)(2,1)}, u32[]{:S(2)}) copy-start(bf16[3,1024]{1,0:T(4,128)(2,1)} %c_ref.1) | copy-start | bytes 18436
  12.7 7.2 %collective-permute-start.10 = (bf16[448,128]{1,0:T(8,128)(2,1)S(1)}, bf16[448,128]{1,0:T(8,128)(2,1)S(1)}, u32[]{:S(2)}, u32[]{:S(2)}) collective-permute-start(bf16[448,128]{1,0:T(8,128)(2,1)S(1)} %get-tuple-element.20.o_ref), channel_id=1, source_target_pairs={{0,1},{1,0},{2,3},{3,2},{4,5},{5,4},{6,7},{7,6},{8,9},{9,8},{10,11... | collective-permute-start | bytes 344072 | tf_op jit(solution)/shard_map/ppermute | solution.py:385
  15.2 20.9 %copy-start.3 = (s32[2]{0:T(128)S(1)}, s32[2]{0:T(128)}, u32[]{:S(2)}) copy-start(s32[2]{0:T(128)} %param.11) | copy-start | bytes 28
  16.2 26.8 %copy-start.2 = (s32[2,256]{1,0:T(2,128)S(1)}, s32[2,256]{1,0:T(2,128)}, u32[]{:S(2)}) copy-start(s32[2,256]{1,0:T(2,128)} %t_ref.1) | copy-start | bytes 6148
  16.2 3.8 %collective-permute-start.9 = (bf16[64,1024]{1,0:T(8,128)(2,1)S(1)}, bf16[64,1024]{1,0:T(8,128)(2,1)S(1)}, u32[]{:S(2)}, u32[]{:S(2)}) collective-permute-start(bf16[64,1024]{1,0:T(8,128)(2,1)S(1)} %shard_map.95.a_ref.refs_3_), channel_id=1, source_target_pairs={{0,4},{4,0},{8,12},{12,8},{16,20},{20,16},{24,28},{28,24},{1,5},{5... | collective-permute-start | bytes 393224 | tf_op jit(solution)/shard_map/ppermute | solution.py:393
  16.3 8.3 %collective-permute-start.3 = (bf16[64,1024]{1,0:T(8,128)(2,1)S(1)}, bf16[64,1024]{1,0:T(8,128)(2,1)S(1)}, u32[]{:S(2)}, u32[]{:S(2)}) collective-permute-start(bf16[64,1024]{1,0:T(8,128)(2,1)S(1)} %shard_map.95.a_ref.refs_3_), channel_id=1, source_target_pairs={{0,24},{4,28},{8,16},{12,20},{16,8},{20,12},{24,0},{28,4},{1,25},{... | collective-permute-start | bytes 393224 | tf_op jit(solution)/shard_map/ppermute | solution.py:393
  18.8 7.1 %collective-permute-start.4 = (bf16[64,1024]{1,0:T(8,128)(2,1)S(1)}, bf16[64,1024]{1,0:T(8,128)(2,1)S(1)}, u32[]{:S(2)}, u32[]{:S(2)}) collective-permute-start(bf16[64,1024]{1,0:T(8,128)(2,1)S(1)} %shard_map.95.a_ref.refs_3_), channel_id=1, source_target_pairs={{0,16},{4,20},{8,24},{12,28},{16,0},{20,4},{24,8},{28,12},{1,17},{... | collective-permute-start | bytes 393224 | tf_op jit(solution)/shard_map/ppermute | solution.py:393
  19.3 6.7 %collective-permute-start.5 = (bf16[64,1024]{1,0:T(8,128)(2,1)S(1)}, bf16[64,1024]{1,0:T(8,128)(2,1)S(1)}, u32[]{:S(2)}, u32[]{:S(2)}) collective-permute-start(bf16[64,1024]{1,0:T(8,128)(2,1)S(1)} %shard_map.95.a_ref.refs_3_), channel_id=1, source_target_pairs={{0,8},{4,12},{8,0},{12,4},{16,24},{20,28},{24,16},{28,20},{1,9},{5... | collective-permute-start | bytes 393224 | tf_op jit(solution)/shard_map/ppermute | solution.py:393
  20.0 6.4 %collective-permute-start.11 = (bf16[448,128]{1,0:T(8,128)(2,1)S(1)}, bf16[448,128]{1,0:T(8,128)(2,1)S(1)}, u32[]{:S(2)}, u32[]{:S(2)}) collective-permute-start(bf16[448,128]{1,0:T(8,128)(2,1)S(1)} %get-tuple-element.21.o_ref), channel_id=1, source_target_pairs={{0,4},{1,2},{2,1},{3,7},{4,0},{5,6},{6,5},{7,3},{8,12},{9,10},{10,... | collective-permute-start | bytes 344072 | tf_op jit(solution)/shard_map/ppermute | solution.py:390
  20.3 7.8 %collective-permute-start.12 = (bf16[128,256]{1,0:T(8,128)(2,1)S(1)}, bf16[128,256]{1,0:T(8,128)(2,1)S(1)}, u32[]{:S(2)}, u32[]{:S(2)}) collective-permute-start(bf16[128,256]{1,0:T(8,128)(2,1)S(1)} %shard_map.98), channel_id=1, source_target_pairs={{0,2},{3,1},{1,0},{2,3},{4,6},{7,5},{5,4},{6,7},{8,10},{11,9},{9,8... | collective-permute-start | bytes 196616 | tf_op jit(solution)/shard_map/ppermute | solution.py:385
  24.6 3.6 %collective-permute-start.6 = (bf16[64,1024]{1,0:T(8,128)(2,1)S(1)}, bf16[64,1024]{1,0:T(8,128)(2,1)S(1)}, u32[]{:S(2)}, u32[]{:S(2)}) collective-permute-start(bf16[64,1024]{1,0:T(8,128)(2,1)S(1)} %collective-permute-done.3.refs_0_), channel_id=1, source_target_pairs={{0,4},{4,0},{8,12},{12,8},{16,20},{20,16},{24,28},{28,24},{1,5},{5... | collective-permute-start | bytes 393224 | tf_op jit(solution)/shard_map/ppermute | solution.py:393
  25.9 2.2 %collective-permute-start.7 = (bf16[64,1024]{1,0:T(8,128)(2,1)S(1)}, bf16[64,1024]{1,0:T(8,128)(2,1)S(1)}, u32[]{:S(2)}, u32[]{:S(2)}) collective-permute-start(bf16[64,1024]{1,0:T(8,128)(2,1)S(1)} %collective-permute-done.4.refs_1_), channel_id=1, source_target_pairs={{0,4},{4,0},{8,12},{12,8},{16,20},{20,16},{24,28},{28,24},{1,5},{5... | collective-permute-start | bytes 393224 | tf_op jit(solution)/shard_map/ppermute | solution.py:393
  26.0 2.1 %collective-permute-start.8 = (bf16[64,1024]{1,0:T(8,128)(2,1)S(1)}, bf16[64,1024]{1,0:T(8,128)(2,1)S(1)}, u32[]{:S(2)}, u32[]{:S(2)}) collective-permute-start(bf16[64,1024]{1,0:T(8,128)(2,1)S(1)} %collective-permute-done.5.refs_2_), channel_id=1, source_target_pairs={{0,4},{4,0},{8,12},{12,8},{16,20},{20,16},{24,28},{28,24},{1,5},{5... | collective-permute-start | bytes 393224 | tf_op jit(solution)/shard_map/ppermute | solution.py:393
  26.6 8.6 %collective-permute-start.16 = (bf16[576,128]{1,0:T(8,128)(2,1)S(1)}, bf16[576,128]{1,0:T(8,128)(2,1)S(1)}, u32[]{:S(2)}, u32[]{:S(2)}) collective-permute-start(bf16[576,128]{1,0:T(8,128)(2,1)S(1)} %get-tuple-element.28.refs_0_), channel_id=1, source_target_pairs={{0,16},{4,20},{8,24},{12,28},{16,0},{20,4},{24,8},{28,12},{1,17},{... | collective-permute-start | bytes 442376 | tf_op jit(solution)/shard_map/ppermute | solution.py:393
  28.9 14.0 %collective-permute-start.13 = (bf16[384,256]{1,0:T(8,128)(2,1)S(1)}, bf16[384,256]{1,0:T(8,128)(2,1)S(1)}, u32[]{:S(2)}, u32[]{:S(2)}) collective-permute-start(bf16[384,256]{1,0:T(8,128)(2,1)S(1)} %get-tuple-element.25), channel_id=1, source_target_pairs={{0,2},{3,1},{1,0},{2,3},{4,6},{7,5},{5,4},{6,7},{8,10},{11,9},{9,8... | collective-permute-start | bytes 589832 | tf_op jit(solution)/shard_map/ppermute | solution.py:385
  33.1 9.8 %collective-permute-start.14 = (bf16[512,256]{1,0:T(8,128)(2,1)S(1)}, bf16[512,256]{1,0:T(8,128)(2,1)S(1)}, u32[]{:S(2)}, u32[]{:S(2)}) collective-permute-start(bf16[512,256]{1,0:T(8,128)(2,1)S(1)} %get-tuple-element.26), channel_id=1, source_target_pairs={{0,4},{1,2},{2,1},{3,7},{4,0},{5,6},{6,5},{7,3},{8,12},{9,10},{10,... | collective-permute-start | bytes 786440 | tf_op jit(solution)/shard_map/ppermute | solution.py:390
  33.1 9.8 %collective-permute-start.15 = (bf16[512,256]{1,0:T(8,128)(2,1)S(1)}, bf16[512,256]{1,0:T(8,128)(2,1)S(1)}, u32[]{:S(2)}, u32[]{:S(2)}) collective-permute-start(bf16[512,256]{1,0:T(8,128)(2,1)S(1)} %get-tuple-element.27), channel_id=1, source_target_pairs={{0,1},{1,0},{2,3},{3,2},{4,5},{5,4},{6,7},{7,6},{8,9},{9,8},{10,11... | collective-permute-start | bytes 786440 | tf_op jit(solution)/shard_map/ppermute | solution.py:385
  33.8 7.6 %collective-permute-start.18 = (bf16[576,128]{1,0:T(8,128)(2,1)S(1)}, bf16[576,128]{1,0:T(8,128)(2,1)S(1)}, u32[]{:S(2)}, u32[]{:S(2)}) collective-permute-start(bf16[576,128]{1,0:T(8,128)(2,1)S(1)} %get-tuple-element.28.refs_0_), channel_id=1, source_target_pairs={{0,24},{4,28},{8,16},{12,20},{16,8},{20,12},{24,0},{28,4},{1,25},{... | collective-permute-start | bytes 442376 | tf_op jit(solution)/shard_map/ppermute | solution.py:393
  35.2 7.6 %collective-permute-start.19 = (bf16[576,128]{1,0:T(8,128)(2,1)S(1)}, bf16[576,128]{1,0:T(8,128)(2,1)S(1)}, u32[]{:S(2)}, u32[]{:S(2)}) collective-permute-start(bf16[576,128]{1,0:T(8,128)(2,1)S(1)} %get-tuple-element.28.refs_0_), channel_id=1, source_target_pairs={{0,8},{4,12},{8,0},{12,4},{16,24},{20,28},{24,16},{28,20},{1,9},{5... | collective-permute-start | bytes 442376 | tf_op jit(solution)/shard_map/ppermute | solution.py:393
  41.4 2.0 %collective-permute-start.17 = (bf16[1152,128]{1,0:T(8,128)(2,1)S(1)}, bf16[1152,128]{1,0:T(8,128)(2,1)S(1)}, u32[]{:S(2)}, u32[]{:S(2)}) collective-permute-start(bf16[1152,128]{1,0:T(8,128)(2,1)S(1)} %shard_map.103.a_ref), channel_id=1, source_target_pairs={{0,4},{4,0},{8,12},{12,8},{16,20},{20,16},{24,28},{28,24},{1,5},{5... | collective-permute-start | bytes 884744 | tf_op jit(solution)/shard_map/ppermute | solution.py:393
  42.8 1.6 %collective-permute-start.20 = (bf16[1152,128]{1,0:T(8,128)(2,1)S(1)}, bf16[1152,128]{1,0:T(8,128)(2,1)S(1)}, u32[]{:S(2)}, u32[]{:S(2)}) collective-permute-start(bf16[1152,128]{1,0:T(8,128)(2,1)S(1)} %shard_map.104.c_ref), channel_id=1, source_target_pairs={{0,4},{4,0},{8,12},{12,8},{16,20},{20,16},{24,28},{28,24},{1,5},{5... | collective-permute-start | bytes 884744 | tf_op jit(solution)/shard_map/ppermute | solution.py:393
  45.2 1.2 %collective-permute-start.21 = (f32[8,128]{1,0:T(8,128)S(1)}, f32[8,128]{1,0:T(8,128)S(1)}, u32[]{:S(2)}, u32[]{:S(2)}) collective-permute-start(f32[8,128]{1,0:T(8,128)S(1)} %shard_map.105.o_ref), channel_id=1, source_target_pairs={{0,4},{1,2},{2,1},{3,7},{4,0},{5,6},{6,5},{7,3},{8,12},{9,10},{10,... | collective-permute-start | bytes 12296 | tf_op jit(solution)/shard_map/ppermute | solution.py:390
  46.4 5.8 %collective-permute-start.22 = (f32[8,128]{1,0:T(8,128)S(1)}, f32[8,128]{1,0:T(8,128)S(1)}, u32[]{:S(2)}, u32[]{:S(2)}) collective-permute-start(f32[8,128]{1,0:T(8,128)S(1)} %shard_map.106.j_ref), channel_id=1, source_target_pairs={{0,1},{1,0},{2,3},{3,2},{4,5},{5,4},{6,7},{7,6},{8,9},{9,8},{10,11... | collective-permute-start | bytes 12296 | tf_op jit(solution)/shard_map/ppermute | solution.py:385

commit v8 on v6

--- a/solution.py
+++ b/solution.py
@@ -83,10 +83,10 @@
     side_begin = u_begin + step
 
     def body(
-        h_any, p_any, o_any, w_any, c_ref, q_ref, b_ref,
-        mixed_ref, out_ref, fold_ref, w_ref, h_ref, p_ref, o_ref, hold, sems,
+        h_any, p_any, o_any, q_any, w_any, c_ref, b_ref,
+        mixed_ref, out_ref, fold_ref, w_ref, h_ref, p_ref, o_ref, q_ref, hold, sems,
     ):
-        pairs = ((h_any, h_ref), (p_any, p_ref), (o_any, o_ref), (w_any, w_ref))
+        pairs = ((h_any, h_ref), (p_any, p_ref), (o_any, o_ref), (q_any, q_ref), (w_any, w_ref))
         copies = [pltpu.make_async_copy(a, b, sems.at[k]) for k, (a, b) in enumerate(pairs)]
         for copy in copies:
             copy.start()
@@ -108,12 +108,13 @@
             pair = [hold[k, pl.ds(odd, rank // 2, stride=2), :] for odd in (0, 1)]
             begin = side_begin + k * rank
             out_ref[begin : begin + rank, :] = jnp.concatenate(pair, axis=0).astype(bf16)
+        copies[3].wait()
         for k in range(lines):
             out_ref[k * q_rows : (k + 1) * q_rows, :] = q_ref[:, k * wide : (k + 1) * wide]
         copies[2].wait()
         u = lax.dot_general(b_ref[...], o_ref[...], NT, preferred_element_type=f32)
         out_ref[u_begin:side_begin, :] = split2(u, 1)
-        copies[3].wait()
+        copies[4].wait()
         fold_ref[...] = fold_term(b_ref[...], w_ref, lax.axis_index("tensor"))
 
     return call(
@@ -124,15 +125,16 @@
             arr((step, width), f32),
             pltpu.VMEM(proj_weight.shape, bf16),
         ),
-        (far(hidden), far(proj_in_t), far(proj_out_t), far(proj_weight), conv_filter, query_grads, start),
+        (*(far(x) for x in (hidden, proj_in_t, proj_out_t, query_grads, proj_weight)), conv_filter, start),
         2 * tokens * width * rank + 2 * step * width * width,
-        in_specs=[ANY] * 4 + [VM] * 3,
+        in_specs=[ANY] * 5 + [VM] * 2,
         scratch=[
             pltpu.VMEM(hidden.shape, bf16),
             pltpu.VMEM(proj_in_t.shape, bf16),
             pltpu.VMEM(proj_out_t.shape, bf16),
+            pltpu.VMEM(query_grads.shape, bf16),
             pltpu.VMEM((tokens // wide, rank, wide), f32),
-            pltpu.SemaphoreType.DMA((4,)),
+            pltpu.SemaphoreType.DMA((5,)),
         ],
     )
 
@@ -294,11 +296,10 @@
         joint = lax.dot_general(split2(side_ref[...], 0), grad, NT, preferred_element_type=f32)
         out_ref[...] = split2(halve(joint), 0)
 
-    spread = jnp.broadcast_to(lengths[:, None], targets.shape)
     return call(
         body,
         arr((2 * rank, vocab), bf16),
-        (*pieces, first, side_in, targets, spread),
+        (*pieces, first, side_in, targets, lengths[:, None]),
         1 << 34,
     )
 
@@ -309,7 +310,7 @@
     step = vocab // parts
     lines = rank // 2
     count = parts if queries is None else queries.shape[0]
-    high = shares[0].shape[0] // 2
+    high = shares[2].shape[0]
     rows = (high - step) // lines
     extra_args = () if queries is None else (queries,)
 
@@ -317,9 +318,8 @@
         q_ref, refs = (None, refs) if queries is None else (refs[0], refs[1:])
         out_ref, hold = refs
         own = lax.axis_index("dp") % parts
-        s_refs = []
-        for begin, pair in ((0, (a_ref, b_ref)), (1, (c_ref, d_ref)), (1, (a_ref, b_ref)), (0, (c_ref, d_ref))):
-            s_refs += [ref.at[pl.ds(begin * high, high), :] for ref in pair]
+        cut = [[ref.at[pl.ds(k * high, high), :] for ref in (a_ref, b_ref)] for k in range(3)]
+        s_refs = [*cut[0], c_ref, d_ref, *cut[1], *cut[2]]
         u = jnp.concatenate([ref[rows * lines :, :] for ref in s_refs], axis=0)
         grads = halve(jnp.dot(j_ref[...], u, preferred_element_type=f32))
         grads = grads[:, :rank] + grads[:, rank:]
@@ -402,8 +402,8 @@
     if n_dp != parts:
         queries = lax.all_gather(whole[: 4 * block], "dp", axis=0)
     others = {s: swap(whole, "dp", s) for s in range(2, parts, 2)}
-    pairs = stack((whole, others[4])), stack((others[6], others[2]))
-    shares = [y for x in pairs for y in (x, swap(x, "dp", 1))]
+    first_three = stack((whole, others[4], others[6]))
+    shares = [y for x in (first_three, others[2]) for y in (x, swap(x, "dp", 1))]
     joint = token_grads(parts, pieces, first, side_in, targets, lengths)
     scores = row_scores(parts, joint, shares, queries)
     joined = join_rows(scores, cross(scores))

time: 52.6 us -> 52.5 us (level)
  local copies, waits for them, and re-layouts: 1.53 us -> 0.8 us
    unnamed x8 -> x6, local copies, waits for them, and re-layouts: 1.46 us -> 0.71 us
    pallas_call x16 -> x15, Pallas kernels: 11 us -> 11 us  [call(): pl.pallas_call(body, out_shape=outs, in_specs=in_specs or [VM] * len(args...]
  transfers between devices with their start and end apart: 23 -> 23, of which waited for: 8 -> 9; matrix products, arithmetic and copies ran while one was open for 0% -> 0% of each run, Pallas kernels for 17% -> 17%
where the time goes in v8:
time: 52.5 us; the launch traced here: 52.3 us
  starting transfers between devices  27.8 us (53%)
  waiting for transfers between devices  12.5 us (24%)
  Pallas kernels  11 us (21%)
  local copies, waits for them, and re-layouts  0.8 us (2%)
    ppermute x5, starting transfers between devices, send(): return lax.ppermute(x, 'tensor', pairs)  13.9 us
    ppermute x15, starting transfers between devices, swap(): lax.ppermute(x, axis, [(i, i ^ slot) for i in range(lax.axis_size(axis))])  13.7 us
    pallas_call x15, Pallas kernels, call(): pl.pallas_call(body, out_shape=outs, in_specs=in_specs or [VM] * len(args...  11 us
    ppermute x15, waiting for transfers between devices, swap(): lax.ppermute(x, axis, [(i, i ^ slot) for i in range(lax.axis_size(axis))])  9.92 us
    ppermute x5, waiting for transfers between devices, send(): return lax.ppermute(x, 'tensor', pairs)  1.59 us
  transfers between devices with their start and end apart: 23, of which 9 were waited for; matrix products, arithmetic and copies ran while one was open for 0% of the time, Pallas kernels for 17%

profile of v8, /device:TPU:0, one launch (start us, length us, event | category | flops | bytes accessed | tf_op | source)
XLA Modules:
  0.0 52.3 jit_solution(12136870637920698245)
XLA Ops:
  0.0 0.9 %shard_map.91.b_ref = bf16[64,1024]{1,0:T(8,128)(2,1)S(1)} custom-call(bf16[512,1024]{1,0:T(8,128)(2,1)} %e_ref.1), custom_call_target="tpu_custom_call" | custom-call | bytes 1048576 | tf_op jit(solution)/shard_map/pallas_call | solution.py:30
  0.9 4.1 %collective-permute-start = (bf16[64,1024]{1,0:T(8,128)(2,1)S(1)}, bf16[64,1024]{1,0:T(8,128)(2,1)S(1)}, u32[]{:S(2)}, u32[]{:S(2)}) collective-permute-start(bf16[64,1024]{1,0:T(8,128)(2,1)S(1)} %shard_map.91.b_ref), channel_id=1, source_target_pairs={{0,2},{1,3},{2,0},{3,1},{4,6},{5,7},{6,4},{7,5},{8,10},{9,11},{10,... | collective-permute-start | bytes 393224 | tf_op jit(solution)/shard_map/ppermute | solution.py:382
  5.0 1.6 %collective-permute-start.1 = (bf16[64,1024]{1,0:T(8,128)(2,1)S(1)}, bf16[64,1024]{1,0:T(8,128)(2,1)S(1)}, u32[]{:S(2)}, u32[]{:S(2)}) collective-permute-start(bf16[64,1024]{1,0:T(8,128)(2,1)S(1)} %shard_map.91.b_ref), channel_id=1, source_target_pairs={{0,1},{1,0},{2,3},{3,2},{4,5},{5,4},{6,7},{7,6},{8,9},{9,8},{10,11... | collective-permute-start | bytes 393224 | tf_op jit(solution)/shard_map/ppermute | solution.py:382
  6.6 0.0 collective-permute-start.2
  6.6 0.7 %copy-done = bf16[3,1024]{1,0:T(4,128)(2,1)S(1)} copy-done((bf16[3,1024]{1,0:T(4,128)(2,1)S(1)}, bf16[3,1024]{1,0:T(4,128)(2,1)}, u32[]{:S(2)}) %copy-start) | copy-done | bytes 6168
  7.3 4.6 %shard_map.92 = (bf16[512,1024]{1,0:T(8,128)(2,1)S(1)}, bf16[448,128]{1,0:T(8,128)(2,1)S(1)}, f32[64,1024]{1,0:T(8,128)S(1)}, bf16[1024,4096]{1,0:T(8,128)(2,1)S(1)}) custom-call(bf16[2,256,1024]{2,1,0:T(8,128)(2,1)} %h_any.1, bf16[64,1024]{1,0:T(8,128)(2,1)} %bitcast.3, bf16[64,1024]{1,0:T(8,128)(2,1)} %bitcast.4, bf16[16,1024]{1,0:T(8,128)(2,1)} %q_any.1, ...), custom_call_target="tpu_custom_call" | custom-call | flops 201326592 | bytes 9869312 | tf_op jit(solution)/shard_map/pallas_call | solution.py:30
  11.9 1.0 %collective-permute-start.10 = (bf16[448,128]{1,0:T(8,128)(2,1)S(1)}, bf16[448,128]{1,0:T(8,128)(2,1)S(1)}, u32[]{:S(2)}, u32[]{:S(2)}) collective-permute-start(bf16[448,128]{1,0:T(8,128)(2,1)S(1)} %get-tuple-element.20.o_ref), channel_id=1, source_target_pairs={{0,1},{1,0},{2,3},{3,2},{4,5},{5,4},{6,7},{7,6},{8,9},{9,8},{10,11... | collective-permute-start | bytes 344072 | tf_op jit(solution)/shard_map/ppermute | solution.py:374
  12.9 0.1 collective-permute-done.b_ref
  13.0 0.8 %shard_map.93.f_ref = f32[64,1024]{1,0:T(8,128)S(1)} custom-call(f32[64,1024]{1,0:T(8,128)S(1)} %get-tuple-element.17.f_ref, bf16[64,1024]{1,0:T(8,128)(2,1)S(1)} %collective-permute-done.b_ref, bf16[1024,4096]{1,0:T(8,128)(2,1)S(1)} %get-tuple-element.18.w_ref), custom_call_target="tpu_custom_call" | custom-call | flops 134217728 | bytes 8781824 | tf_op jit(solution)/shard_map/pallas_call | solution.py:30
  13.7 0.0 collective-permute-done.1.b_ref
  13.7 0.8 %shard_map.94.f_ref = f32[64,1024]{1,0:T(8,128)S(1)} custom-call(f32[64,1024]{1,0:T(8,128)S(1)} %shard_map.93.f_ref, bf16[64,1024]{1,0:T(8,128)(2,1)S(1)} %collective-permute-done.1.b_ref, bf16[1024,4096]{1,0:T(8,128)(2,1)S(1)} %get-tuple-element.18.w_ref), custom_call_target="tpu_custom_call" | custom-call | flops 134217728 | bytes 8781824 | tf_op jit(solution)/shard_map/pallas_call | solution.py:30
  14.5 0.0 copy-start.1
  14.5 0.9 %collective-permute-done.2.b_ref = bf16[64,1024]{1,0:T(8,128)(2,1)S(1)} collective-permute-done((bf16[64,1024]{1,0:T(8,128)(2,1)S(1)}, bf16[64,1024]{1,0:T(8,128)(2,1)S(1)}, u32[]{:S(2)}, u32[]{:S(2)}) %collective-permute-start.2) | collective-permute-done | bytes 131104 | tf_op jit(solution)/shard_map/ppermute | solution.py:382
  15.4 0.8 %shard_map.95.a_ref.refs_3_ = bf16[64,1024]{1,0:T(8,128)(2,1)S(1)} custom-call(f32[64,1024]{1,0:T(8,128)S(1)} %shard_map.94.f_ref, bf16[64,1024]{1,0:T(8,128)(2,1)S(1)} %collective-permute-done.2.b_ref, bf16[1024,4096]{1,0:T(8,128)(2,1)S(1)} %get-tuple-element.18.w_ref), custom_call_target="tpu_custom_call" | custom-call | flops 134217728 | bytes 8781824 | tf_op jit(solution)/shard_map/pallas_call | solution.py:30
  16.2 0.1 collective-permute-start.9
  16.3 2.5 %collective-permute-start.3 = (bf16[64,1024]{1,0:T(8,128)(2,1)S(1)}, bf16[64,1024]{1,0:T(8,128)(2,1)S(1)}, u32[]{:S(2)}, u32[]{:S(2)}) collective-permute-start(bf16[64,1024]{1,0:T(8,128)(2,1)S(1)} %shard_map.95.a_ref.refs_3_), channel_id=1, source_target_pairs={{0,24},{4,28},{8,16},{12,20},{16,8},{20,12},{24,0},{28,4},{1,25},{... | collective-permute-start | bytes 393224 | tf_op jit(solution)/shard_map/ppermute | solution.py:382
  18.8 0.5 collective-permute-start.4
  19.3 0.5 %collective-permute-start.5 = (bf16[64,1024]{1,0:T(8,128)(2,1)S(1)}, bf16[64,1024]{1,0:T(8,128)(2,1)S(1)}, u32[]{:S(2)}, u32[]{:S(2)}) collective-permute-start(bf16[64,1024]{1,0:T(8,128)(2,1)S(1)} %shard_map.95.a_ref.refs_3_), channel_id=1, source_target_pairs={{0,8},{4,12},{8,0},{12,4},{16,24},{20,28},{24,16},{28,20},{1,9},{5... | collective-permute-start | bytes 393224 | tf_op jit(solution)/shard_map/ppermute | solution.py:382
  19.8 0.2 shard_map.96
  20.0 0.0 collective-permute-start.11
  20.0 0.3 shard_map.98
  20.4 4.2 %collective-permute-start.12 = (bf16[128,256]{1,0:T(8,128)(2,1)S(1)}, bf16[128,256]{1,0:T(8,128)(2,1)S(1)}, u32[]{:S(2)}, u32[]{:S(2)}) collective-permute-start(bf16[128,256]{1,0:T(8,128)(2,1)S(1)} %shard_map.98), channel_id=1, source_target_pairs={{0,2},{3,1},{1,0},{2,3},{4,6},{7,5},{5,4},{6,7},{8,10},{11,9},{9,8... | collective-permute-start | bytes 196616 | tf_op jit(solution)/shard_map/ppermute | solution.py:374
  24.5 0.0 collective-permute-done.3.refs_0_
  24.5 1.4 %collective-permute-done.4.refs_1_ = bf16[64,1024]{1,0:T(8,128)(2,1)S(1)} collective-permute-done((bf16[64,1024]{1,0:T(8,128)(2,1)S(1)}, bf16[64,1024]{1,0:T(8,128)(2,1)S(1)}, u32[]{:S(2)}, u32[]{:S(2)}) %collective-permute-start.4) | collective-permute-done | bytes 131104 | tf_op jit(solution)/shard_map/ppermute | solution.py:382
  25.9 0.0 collective-permute-start.7
  25.9 0.1 collective-permute-done.5.refs_2_
  26.0 0.4 collective-permute-start.8
  26.4 0.0 collective-permute-done.11.c_ref
  26.4 0.2 shard_map.97
  26.6 1.5 %collective-permute-start.16 = (bf16[576,128]{1,0:T(8,128)(2,1)S(1)}, bf16[576,128]{1,0:T(8,128)(2,1)S(1)}, u32[]{:S(2)}, u32[]{:S(2)}) collective-permute-start(bf16[576,128]{1,0:T(8,128)(2,1)S(1)} %get-tuple-element.28.refs_0_), channel_id=1, source_target_pairs={{0,16},{4,20},{8,24},{12,28},{16,0},{20,4},{24,8},{28,12},{1,17},{... | collective-permute-start | bytes 442376 | tf_op jit(solution)/shard_map/ppermute | solution.py:382
  28.1 0.0 collective-permute-done.12.x_ref
  28.2 0.8 %shard_map.100 = (f32[512,256]{1,0:T(8,128)S(1)}, bf16[512,256]{1,0:T(8,128)(2,1)S(1)}, bf16[512,256]{1,0:T(8,128)(2,1)S(1)}, bf16[384,256]{1,0:T(8,128)(2,1)S(1)}) custom-call(bf16[64,1024]{1,0:T(8,128)(2,1)S(1)} %collective-permute-done.3.refs_0_, bf16[64,1024]{1,0:T(8,128)(2,1)S(1)} %collective-permute-done.4.refs_1_, ...), custom_call_target="tpu_custom_call" | custom-call | flops 536870912 | bytes 2228224 | tf_op jit(solution)/shard_map/pallas_call | solution.py:30
  28.9 2.3 %collective-permute-start.13 = (bf16[512,256]{1,0:T(8,128)(2,1)S(1)}, bf16[512,256]{1,0:T(8,128)(2,1)S(1)}, u32[]{:S(2)}, u32[]{:S(2)}) collective-permute-start(bf16[512,256]{1,0:T(8,128)(2,1)S(1)} %get-tuple-element.25), channel_id=1, source_target_pairs={{0,1},{1,0},{2,3},{3,2},{4,5},{5,4},{6,7},{7,6},{8,9},{9,8},{10,11... | collective-permute-start | bytes 786440 | tf_op jit(solution)/shard_map/ppermute | solution.py:374
  31.2 2.1 %collective-permute-start.15 = (bf16[384,256]{1,0:T(8,128)(2,1)S(1)}, bf16[384,256]{1,0:T(8,128)(2,1)S(1)}, u32[]{:S(2)}, u32[]{:S(2)}) collective-permute-start(bf16[384,256]{1,0:T(8,128)(2,1)S(1)} %get-tuple-element.27), channel_id=1, source_target_pairs={{0,2},{3,1},{1,0},{2,3},{4,6},{7,5},{5,4},{6,7},{8,10},{11,9},{9,8... | collective-permute-start | bytes 589832 | tf_op jit(solution)/shard_map/ppermute | solution.py:374
  33.3 1.8 %collective-permute-start.17 = (bf16[576,128]{1,0:T(8,128)(2,1)S(1)}, bf16[576,128]{1,0:T(8,128)(2,1)S(1)}, u32[]{:S(2)}, u32[]{:S(2)}) collective-permute-start(bf16[576,128]{1,0:T(8,128)(2,1)S(1)} %get-tuple-element.28.refs_0_), channel_id=1, source_target_pairs={{0,24},{4,28},{8,16},{12,20},{16,8},{20,12},{24,0},{28,4},{1,25},{... | collective-permute-start | bytes 442376 | tf_op jit(solution)/shard_map/ppermute | solution.py:382
  35.1 0.5 %collective-permute-start.19 = (bf16[576,128]{1,0:T(8,128)(2,1)S(1)}, bf16[576,128]{1,0:T(8,128)(2,1)S(1)}, u32[]{:S(2)}, u32[]{:S(2)}) collective-permute-start(bf16[576,128]{1,0:T(8,128)(2,1)S(1)} %get-tuple-element.28.refs_0_), channel_id=1, source_target_pairs={{0,8},{4,12},{8,0},{12,4},{16,24},{20,28},{24,16},{28,20},{1,9},{5... | collective-permute-start | bytes 442376 | tf_op jit(solution)/shard_map/ppermute | solution.py:382
  35.6 0.1 copy.10.live_ref
  35.7 5.2 %collective-permute-done.17.refs_2_ = bf16[576,128]{1,0:T(8,128)(2,1)S(1)} collective-permute-done((bf16[576,128]{1,0:T(8,128)(2,1)S(1)}, bf16[576,128]{1,0:T(8,128)(2,1)S(1)}, u32[]{:S(2)}, u32[]{:S(2)}) %collective-permute-start.17) | collective-permute-done | bytes 147488 | tf_op jit(solution)/shard_map/ppermute | solution.py:382
  41.0 0.1 collective-permute-start.18
  41.1 1.4 %collective-permute-done.19.c_ref = bf16[576,128]{1,0:T(8,128)(2,1)S(1)} collective-permute-done((bf16[576,128]{1,0:T(8,128)(2,1)S(1)}, bf16[576,128]{1,0:T(8,128)(2,1)S(1)}, u32[]{:S(2)}, u32[]{:S(2)}) %collective-permute-start.19) | collective-permute-done | bytes 147488 | tf_op jit(solution)/shard_map/ppermute | solution.py:382
  42.5 0.5 shard_map.101.j_ref
  43.0 0.9 %collective-permute-done.20.d_ref = bf16[576,128]{1,0:T(8,128)(2,1)S(1)} collective-permute-done((bf16[576,128]{1,0:T(8,128)(2,1)S(1)}, bf16[576,128]{1,0:T(8,128)(2,1)S(1)}, u32[]{:S(2)}, u32[]{:S(2)}) %collective-permute-start.20) | collective-permute-done | bytes 147488 | tf_op jit(solution)/shard_map/ppermute | solution.py:382
  43.8 0.7 %shard_map.103.o_ref = f32[8,128]{1,0:T(8,128)S(1)} custom-call(bf16[128,512]{1,0:T(8,128)(2,1)S(1)} %shard_map.101.j_ref, bf16[1728,128]{1,0:T(8,128)(2,1)S(1)} %shard_map.102.a_ref, bf16[1728,128]{1,0:T(8,128)(2,1)S(1)} %collective-permute-done.18.b_ref, bf16[576,128]{1,0:T(8,128)(2,1)S(1)} %collective-permute-done.19.c_ref, ...), custom_call_target="tpu_custom_call" | custom-call | flops 4194304 | bytes 1310720 | tf_op jit(solution)/shard_map/pallas_call | solution.py:30
  44.5 0.2 collective-permute-start.21
  44.7 1.0 %collective-permute-done.21.c_ref = f32[8,128]{1,0:T(8,128)S(1)} collective-permute-done((f32[8,128]{1,0:T(8,128)S(1)}, f32[8,128]{1,0:T(8,128)S(1)}, u32[]{:S(2)}, u32[]{:S(2)}) %collective-permute-start.21) | collective-permute-done | bytes 4128 | tf_op jit(solution)/shard_map/ppermute | solution.py:379
  45.7 4.4 %collective-permute-start.22 = (f32[8,128]{1,0:T(8,128)S(1)}, f32[8,128]{1,0:T(8,128)S(1)}, u32[]{:S(2)}, u32[]{:S(2)}) collective-permute-start(f32[8,128]{1,0:T(8,128)S(1)} %shard_map.104.j_ref), channel_id=1, source_target_pairs={{0,1},{1,0},{2,3},{3,2},{4,5},{5,4},{6,7},{7,6},{8,9},{9,8},{10,11... | collective-permute-start | bytes 12296 | tf_op jit(solution)/shard_map/ppermute | solution.py:374
  50.2 1.6 %collective-permute-done.22.c_ref = f32[8,128]{1,0:T(8,128)S(1)} collective-permute-done((f32[8,128]{1,0:T(8,128)S(1)}, f32[8,128]{1,0:T(8,128)S(1)}, u32[]{:S(2)}, u32[]{:S(2)}) %collective-permute-start.22) | collective-permute-done | bytes 4128 | tf_op jit(solution)/shard_map/ppermute | solution.py:374
  51.7 0.6 %shard_map.105 = f32[2,128]{1,0:T(2,128)} custom-call(f32[8,128]{1,0:T(8,128)S(1)} %shard_map.104.j_ref, f32[8,128]{1,0:T(8,128)S(1)} %collective-permute-done.22.c_ref), custom_call_target="tpu_custom_call" | custom-call | bytes 8192 | tf_op jit(solution)/shard_map/pallas_call | solution.py:30
  (20 shorter events, 0.1 us)
Async XLA Ops:
  0.9 12.1 %collective-permute-start = (bf16[64,1024]{1,0:T(8,128)(2,1)S(1)}, bf16[64,1024]{1,0:T(8,128)(2,1)S(1)}, u32[]{:S(2)}, u32[]{:S(2)}) collective-permute-start(bf16[64,1024]{1,0:T(8,128)(2,1)S(1)} %shard_map.91.b_ref), channel_id=1, source_target_pairs={{0,2},{1,3},{2,0},{3,1},{4,6},{5,7},{6,4},{7,5},{8,10},{9,11},{10,... | collective-permute-start | bytes 393224 | tf_op jit(solution)/shard_map/ppermute | solution.py:382
  5.0 8.7 %collective-permute-start.1 = (bf16[64,1024]{1,0:T(8,128)(2,1)S(1)}, bf16[64,1024]{1,0:T(8,128)(2,1)S(1)}, u32[]{:S(2)}, u32[]{:S(2)}) collective-permute-start(bf16[64,1024]{1,0:T(8,128)(2,1)S(1)} %shard_map.91.b_ref), channel_id=1, source_target_pairs={{0,1},{1,0},{2,3},{3,2},{4,5},{5,4},{6,7},{7,6},{8,9},{9,8},{10,11... | collective-permute-start | bytes 393224 | tf_op jit(solution)/shard_map/ppermute | solution.py:382
  6.6 8.8 %collective-permute-start.2 = (bf16[64,1024]{1,0:T(8,128)(2,1)S(1)}, bf16[64,1024]{1,0:T(8,128)(2,1)S(1)}, u32[]{:S(2)}, u32[]{:S(2)}) collective-permute-start(bf16[64,1024]{1,0:T(8,128)(2,1)S(1)} %shard_map.91.b_ref), channel_id=1, source_target_pairs={{0,3},{1,2},{2,1},{3,0},{4,7},{5,6},{6,5},{7,4},{8,11},{9,10},{10,... | collective-permute-start | bytes 393224 | tf_op jit(solution)/shard_map/ppermute | solution.py:382
  6.6 0.7 %copy-start = (bf16[3,1024]{1,0:T(4,128)(2,1)S(1)}, bf16[3,1024]{1,0:T(4,128)(2,1)}, u32[]{:S(2)}) copy-start(bf16[3,1024]{1,0:T(4,128)(2,1)} %c_ref.1) | copy-start | bytes 18436
  11.9 7.9 %collective-permute-start.10 = (bf16[448,128]{1,0:T(8,128)(2,1)S(1)}, bf16[448,128]{1,0:T(8,128)(2,1)S(1)}, u32[]{:S(2)}, u32[]{:S(2)}) collective-permute-start(bf16[448,128]{1,0:T(8,128)(2,1)S(1)} %get-tuple-element.20.o_ref), channel_id=1, source_target_pairs={{0,1},{1,0},{2,3},{3,2},{4,5},{5,4},{6,7},{7,6},{8,9},{9,8},{10,11... | collective-permute-start | bytes 344072 | tf_op jit(solution)/shard_map/ppermute | solution.py:374
  14.5 21.1 %copy-start.2 = (s32[2]{0:T(128)S(1)}, s32[2]{0:T(128)}, u32[]{:S(2)}) copy-start(s32[2]{0:T(128)} %param.11) | copy-start | bytes 28
  14.5 28.0 %copy-start.1 = (s32[2,256]{1,0:T(2,128)S(1)}, s32[2,256]{1,0:T(2,128)}, u32[]{:S(2)}) copy-start(s32[2,256]{1,0:T(2,128)} %t_ref.1) | copy-start | bytes 6148
  16.2 3.8 %collective-permute-start.9 = (bf16[64,1024]{1,0:T(8,128)(2,1)S(1)}, bf16[64,1024]{1,0:T(8,128)(2,1)S(1)}, u32[]{:S(2)}, u32[]{:S(2)}) collective-permute-start(bf16[64,1024]{1,0:T(8,128)(2,1)S(1)} %shard_map.95.a_ref.refs_3_), channel_id=1, source_target_pairs={{0,4},{4,0},{8,12},{12,8},{16,20},{20,16},{24,28},{28,24},{1,5},{5... | collective-permute-start | bytes 393224 | tf_op jit(solution)/shard_map/ppermute | solution.py:382
  16.3 8.3 %collective-permute-start.3 = (bf16[64,1024]{1,0:T(8,128)(2,1)S(1)}, bf16[64,1024]{1,0:T(8,128)(2,1)S(1)}, u32[]{:S(2)}, u32[]{:S(2)}) collective-permute-start(bf16[64,1024]{1,0:T(8,128)(2,1)S(1)} %shard_map.95.a_ref.refs_3_), channel_id=1, source_target_pairs={{0,24},{4,28},{8,16},{12,20},{16,8},{20,12},{24,0},{28,4},{1,25},{... | collective-permute-start | bytes 393224 | tf_op jit(solution)/shard_map/ppermute | solution.py:382
  18.8 7.1 %collective-permute-start.4 = (bf16[64,1024]{1,0:T(8,128)(2,1)S(1)}, bf16[64,1024]{1,0:T(8,128)(2,1)S(1)}, u32[]{:S(2)}, u32[]{:S(2)}) collective-permute-start(bf16[64,1024]{1,0:T(8,128)(2,1)S(1)} %shard_map.95.a_ref.refs_3_), channel_id=1, source_target_pairs={{0,16},{4,20},{8,24},{12,28},{16,0},{20,4},{24,8},{28,12},{1,17},{... | collective-permute-start | bytes 393224 | tf_op jit(solution)/shard_map/ppermute | solution.py:382
  19.3 6.7 %collective-permute-start.5 = (bf16[64,1024]{1,0:T(8,128)(2,1)S(1)}, bf16[64,1024]{1,0:T(8,128)(2,1)S(1)}, u32[]{:S(2)}, u32[]{:S(2)}) collective-permute-start(bf16[64,1024]{1,0:T(8,128)(2,1)S(1)} %shard_map.95.a_ref.refs_3_), channel_id=1, source_target_pairs={{0,8},{4,12},{8,0},{12,4},{16,24},{20,28},{24,16},{28,20},{1,9},{5... | collective-permute-start | bytes 393224 | tf_op jit(solution)/shard_map/ppermute | solution.py:382
  20.0 6.4 %collective-permute-start.11 = (bf16[448,128]{1,0:T(8,128)(2,1)S(1)}, bf16[448,128]{1,0:T(8,128)(2,1)S(1)}, u32[]{:S(2)}, u32[]{:S(2)}) collective-permute-start(bf16[448,128]{1,0:T(8,128)(2,1)S(1)} %get-tuple-element.21.o_ref), channel_id=1, source_target_pairs={{0,4},{1,2},{2,1},{3,7},{4,0},{5,6},{6,5},{7,3},{8,12},{9,10},{10,... | collective-permute-start | bytes 344072 | tf_op jit(solution)/shard_map/ppermute | solution.py:379
  20.4 7.8 %collective-permute-start.12 = (bf16[128,256]{1,0:T(8,128)(2,1)S(1)}, bf16[128,256]{1,0:T(8,128)(2,1)S(1)}, u32[]{:S(2)}, u32[]{:S(2)}) collective-permute-start(bf16[128,256]{1,0:T(8,128)(2,1)S(1)} %shard_map.98), channel_id=1, source_target_pairs={{0,2},{3,1},{1,0},{2,3},{4,6},{7,5},{5,4},{6,7},{8,10},{11,9},{9,8... | collective-permute-start | bytes 196616 | tf_op jit(solution)/shard_map/ppermute | solution.py:374
  24.5 3.6 %collective-permute-start.6 = (bf16[64,1024]{1,0:T(8,128)(2,1)S(1)}, bf16[64,1024]{1,0:T(8,128)(2,1)S(1)}, u32[]{:S(2)}, u32[]{:S(2)}) collective-permute-start(bf16[64,1024]{1,0:T(8,128)(2,1)S(1)} %collective-permute-done.3.refs_0_), channel_id=1, source_target_pairs={{0,4},{4,0},{8,12},{12,8},{16,20},{20,16},{24,28},{28,24},{1,5},{5... | collective-permute-start | bytes 393224 | tf_op jit(solution)/shard_map/ppermute | solution.py:382
  25.9 2.2 %collective-permute-start.7 = (bf16[64,1024]{1,0:T(8,128)(2,1)S(1)}, bf16[64,1024]{1,0:T(8,128)(2,1)S(1)}, u32[]{:S(2)}, u32[]{:S(2)}) collective-permute-start(bf16[64,1024]{1,0:T(8,128)(2,1)S(1)} %collective-permute-done.4.refs_1_), channel_id=1, source_target_pairs={{0,4},{4,0},{8,12},{12,8},{16,20},{20,16},{24,28},{28,24},{1,5},{5... | collective-permute-start | bytes 393224 | tf_op jit(solution)/shard_map/ppermute | solution.py:382
  26.0 2.1 %collective-permute-start.8 = (bf16[64,1024]{1,0:T(8,128)(2,1)S(1)}, bf16[64,1024]{1,0:T(8,128)(2,1)S(1)}, u32[]{:S(2)}, u32[]{:S(2)}) collective-permute-start(bf16[64,1024]{1,0:T(8,128)(2,1)S(1)} %collective-permute-done.5.refs_2_), channel_id=1, source_target_pairs={{0,4},{4,0},{8,12},{12,8},{16,20},{20,16},{24,28},{28,24},{1,5},{5... | collective-permute-start | bytes 393224 | tf_op jit(solution)/shard_map/ppermute | solution.py:382
  26.6 8.5 %collective-permute-start.16 = (bf16[576,128]{1,0:T(8,128)(2,1)S(1)}, bf16[576,128]{1,0:T(8,128)(2,1)S(1)}, u32[]{:S(2)}, u32[]{:S(2)}) collective-permute-start(bf16[576,128]{1,0:T(8,128)(2,1)S(1)} %get-tuple-element.28.refs_0_), channel_id=1, source_target_pairs={{0,16},{4,20},{8,24},{12,28},{16,0},{20,4},{24,8},{28,12},{1,17},{... | collective-permute-start | bytes 442376 | tf_op jit(solution)/shard_map/ppermute | solution.py:382
  28.9 13.5 %collective-permute-start.13 = (bf16[512,256]{1,0:T(8,128)(2,1)S(1)}, bf16[512,256]{1,0:T(8,128)(2,1)S(1)}, u32[]{:S(2)}, u32[]{:S(2)}) collective-permute-start(bf16[512,256]{1,0:T(8,128)(2,1)S(1)} %get-tuple-element.25), channel_id=1, source_target_pairs={{0,1},{1,0},{2,3},{3,2},{4,5},{5,4},{6,7},{7,6},{8,9},{9,8},{10,11... | collective-permute-start | bytes 786440 | tf_op jit(solution)/shard_map/ppermute | solution.py:374
  31.2 11.3 %collective-permute-start.14 = (bf16[512,256]{1,0:T(8,128)(2,1)S(1)}, bf16[512,256]{1,0:T(8,128)(2,1)S(1)}, u32[]{:S(2)}, u32[]{:S(2)}) collective-permute-start(bf16[512,256]{1,0:T(8,128)(2,1)S(1)} %get-tuple-element.26), channel_id=1, source_target_pairs={{0,4},{1,2},{2,1},{3,7},{4,0},{5,6},{6,5},{7,3},{8,12},{9,10},{10,... | collective-permute-start | bytes 786440 | tf_op jit(solution)/shard_map/ppermute | solution.py:379
  31.2 11.3 %collective-permute-start.15 = (bf16[384,256]{1,0:T(8,128)(2,1)S(1)}, bf16[384,256]{1,0:T(8,128)(2,1)S(1)}, u32[]{:S(2)}, u32[]{:S(2)}) collective-permute-start(bf16[384,256]{1,0:T(8,128)(2,1)S(1)} %get-tuple-element.27), channel_id=1, source_target_pairs={{0,2},{3,1},{1,0},{2,3},{4,6},{7,5},{5,4},{6,7},{8,10},{11,9},{9,8... | collective-permute-start | bytes 589832 | tf_op jit(solution)/shard_map/ppermute | solution.py:374
  33.3 7.7 %collective-permute-start.17 = (bf16[576,128]{1,0:T(8,128)(2,1)S(1)}, bf16[576,128]{1,0:T(8,128)(2,1)S(1)}, u32[]{:S(2)}, u32[]{:S(2)}) collective-permute-start(bf16[576,128]{1,0:T(8,128)(2,1)S(1)} %get-tuple-element.28.refs_0_), channel_id=1, source_target_pairs={{0,24},{4,28},{8,16},{12,20},{16,8},{20,12},{24,0},{28,4},{1,25},{... | collective-permute-start | bytes 442376 | tf_op jit(solution)/shard_map/ppermute | solution.py:382
  35.1 7.4 %collective-permute-start.19 = (bf16[576,128]{1,0:T(8,128)(2,1)S(1)}, bf16[576,128]{1,0:T(8,128)(2,1)S(1)}, u32[]{:S(2)}, u32[]{:S(2)}) collective-permute-start(bf16[576,128]{1,0:T(8,128)(2,1)S(1)} %get-tuple-element.28.refs_0_), channel_id=1, source_target_pairs={{0,8},{4,12},{8,0},{12,4},{16,24},{20,28},{24,16},{28,20},{1,9},{5... | collective-permute-start | bytes 442376 | tf_op jit(solution)/shard_map/ppermute | solution.py:382
  41.0 2.8 %collective-permute-start.18 = (bf16[1728,128]{1,0:T(8,128)(2,1)S(1)}, bf16[1728,128]{1,0:T(8,128)(2,1)S(1)}, u32[]{:S(2)}, u32[]{:S(2)}) collective-permute-start(bf16[1728,128]{1,0:T(8,128)(2,1)S(1)} %shard_map.102.a_ref), channel_id=1, source_target_pairs={{0,4},{4,0},{8,12},{12,8},{16,20},{20,16},{24,28},{28,24},{1,5},{5... | collective-permute-start | bytes 1327112 | tf_op jit(solution)/shard_map/ppermute | solution.py:382
  42.5 1.4 %collective-permute-start.20 = (bf16[576,128]{1,0:T(8,128)(2,1)S(1)}, bf16[576,128]{1,0:T(8,128)(2,1)S(1)}, u32[]{:S(2)}, u32[]{:S(2)}) collective-permute-start(bf16[576,128]{1,0:T(8,128)(2,1)S(1)} %collective-permute-done.19.c_ref), channel_id=1, source_target_pairs={{0,4},{4,0},{8,12},{12,8},{16,20},{20,16},{24,28},{28,24},{1,5},{5... | collective-permute-start | bytes 442376 | tf_op jit(solution)/shard_map/ppermute | solution.py:382
  44.5 1.2 %collective-permute-start.21 = (f32[8,128]{1,0:T(8,128)S(1)}, f32[8,128]{1,0:T(8,128)S(1)}, u32[]{:S(2)}, u32[]{:S(2)}) collective-permute-start(f32[8,128]{1,0:T(8,128)S(1)} %shard_map.103.o_ref), channel_id=1, source_target_pairs={{0,4},{1,2},{2,1},{3,7},{4,0},{5,6},{6,5},{7,3},{8,12},{9,10},{10,... | collective-permute-start | bytes 12296 | tf_op jit(solution)/shard_map/ppermute | solution.py:379
  45.7 6.0 %collective-permute-start.22 = (f32[8,128]{1,0:T(8,128)S(1)}, f32[8,128]{1,0:T(8,128)S(1)}, u32[]{:S(2)}, u32[]{:S(2)}) collective-permute-start(f32[8,128]{1,0:T(8,128)S(1)} %shard_map.104.j_ref), channel_id=1, source_target_pairs={{0,1},{1,0},{2,3},{3,2},{4,5},{5,4},{6,7},{7,6},{8,9},{9,8},{10,11... | collective-permute-start | bytes 12296 | tf_op jit(solution)/shard_map/ppermute | solution.py:374
